TPU v7x, 32 devices: a whole 2x2x4 slice. The times are simulated.
32 devices in a mesh: seq: 8 (over y, x, core), fsdp: 4 (over z).
Axes of the slice: x: 2, y: 2, z: 4, core: 2. Of those that a mesh axis runs over, the one named last changes fastest.
Arguments:
- inputs: bfloat16 [4, 1024, 768], P('fsdp', 'seq'), may hold values from -6 to 6
- positions: int32 [4, 1024], P('fsdp', 'seq'), may hold values from 0 to 1023, as said below
- cotangent: bfloat16 [4, 1024, 768], P('fsdp', 'seq'), may hold values from -6 to 6
- w_qkv: bfloat16 [768, 2304], P('fsdp'), may hold values from -0.21875 to 0.21875
- w_out: bfloat16 [768, 768], P('fsdp'), may hold values from -0.875 to 0.875
- w_in: bfloat16 [768, 2304], P('fsdp'), may hold values from -0.21875 to 0.21875
- w_down: bfloat16 [1152, 768], P('fsdp'), may hold values from -0.1875 to 0.1875
- gain_attn: bfloat16 [768], P('fsdp'), may hold values from 0.5 to 1.5
- gain_mlp: bfloat16 [768], P('fsdp'), may hold values from 0.5 to 1.5
Outputs:
- output: bfloat16 [4, 1024, 768], P('fsdp', 'seq')
- grad_inputs: float32 [4, 1024, 768], P('fsdp', 'seq')
- grad_qkv: float32 [768, 2304], P('fsdp')
- grad_out: float32 [768, 768], P('fsdp')
- grad_in: float32 [768, 2304], P('fsdp')
- grad_down: float32 [1152, 768], P('fsdp')
- grad_gain_attn: float32 [768], P('fsdp')
- grad_gain_mlp: float32 [768], P('fsdp')
Inputs may be any that keep to these rules, and one draw needn't show every extreme that they name: `positions`: positions restart at 0 at each sequence start and otherwise rise by one from token to token; the stream's first sequence may begin at a position above 0. No sequence is longer than 8192 tokens. One sequence of each stream begins within its first 128 tokens and ends within its last 128. The first stream reaches the largest position.
All inputs are finite; a program needn't handle non-finite values.
Results may differ from a plain program's by a relative error of at most 0.018.
Values may be sent and summed in bfloat16 or wider, within the bound.
A program may use at most 128 MiB of HBM per device.

v0:
```python
import math

import jax
import jax.numpy as jnp
from jax import lax
from jax.sharding import PartitionSpec as P

D = 768
HEADS = 12
HEAD_DIM = 64
FF = 1152
HALF_WINDOW = 64


eps = 1e-05
rope_base = 10000.0
masked_score = -1e30


def with_halo(cells, sides, width):
    for axis, dim in sides:
        count = lax.axis_size(axis)
        ends = count - 1
        head = lax.slice_in_dim(cells, 0, width, axis=dim)
        tail = lax.slice_in_dim(cells, cells.shape[dim] - width, cells.shape[dim], axis=dim)
        cells = jnp.concatenate(
            [
                lax.ppermute(tail, axis, [(i, (i + 1) % count) for i in range(ends)]),
                cells,
                lax.ppermute(head, axis, [((i + 1) % count, i) for i in range(ends)]),
            ],
            axis=dim,
        )
    return cells


def layer_norm(values, gain):
    center = values - jnp.mean(values, axis=-1, keepdims=True)
    spread = jnp.mean(center * center, axis=-1, keepdims=True)
    return center * lax.rsqrt(spread + eps) * gain


def rotary(values, token_pos):
    half = values.shape[-1] // 2
    ladder = jnp.arange(half).astype(jnp.float32) * (2.0 / values.shape[-1])
    freqs = rope_base ** (-ladder)
    angles = token_pos.astype(jnp.float32)[:, None] * freqs[None, :]
    cosine = jnp.concatenate([jnp.cos(angles), jnp.cos(angles)], axis=-1)[:, None, :]
    sine = jnp.concatenate([jnp.sin(angles), jnp.sin(angles)], axis=-1)[:, None, :]
    turned = jnp.concatenate([-values[..., half:], values[..., :half]], axis=-1)
    return values * cosine + turned * sine


def window_mask(token_pos, wide_flags, count):
    offsets = jnp.arange(count + 2 * HALF_WINDOW, dtype=jnp.int32) - HALF_WINDOW
    offset = offsets[None, :] - jnp.arange(count, dtype=jnp.int32)[:, None]
    flag_float = wide_flags.astype(jnp.float32)[None, :]
    earlier = token_pos[:, None] >= -offset
    later = flag_float - 1.0 >= offset.astype(jnp.float32)
    return (
        (jnp.abs(offset) <= HALF_WINDOW)
        & (flag_float > 0.5)
        & jnp.where(offset < 0, earlier, later)
    )


def matmul_left(left, right):
    return lax.dot_general(
        left, right, (((0,), (0,)), ((), ())), preferred_element_type=jnp.float32
    )


def matmul_right(left, right):
    return lax.dot_general(
        left, right, (((1,), (1,)), ((), ())), preferred_element_type=jnp.float32
    )


def pack_rows(pieces, groups):
    joined = jnp.concatenate([piece.reshape(groups, -1) for piece in pieces], axis=1)
    return joined


def unpack_row(flat_row, pieces, groups):
    results = []
    offset = 0
    for piece in pieces:
        shape = (piece.shape[0] // groups,) + piece.shape[1:]
        size = math.prod(shape)
        results.append(flat_row[offset : offset + size].reshape(shape))
        offset = offset + size
    return results


def on_device(inputs, positions, cotangent, w_qkv, w_out, w_in, w_down, gain_attn, gain_mlp):
    gathered = (
        lax.all_gather(w_qkv, "fsdp", axis=0, tiled=True),
        lax.all_gather(w_out, "fsdp", axis=0, tiled=True),
        lax.all_gather(w_in, "fsdp", axis=0, tiled=True),
        lax.all_gather(w_down, "fsdp", axis=0, tiled=True),
        lax.all_gather(gain_attn, "fsdp", axis=0, tiled=True),
        lax.all_gather(gain_mlp, "fsdp", axis=0, tiled=True),
    )
    full_qkv, full_out, full_in, full_down, gain_first, gain_second = gathered
    gain_first = gain_first.astype(jnp.float32)
    gain_second = gain_second.astype(jnp.float32)
    scale = HEAD_DIM ** (-0.5)
    tokens = inputs[0].astype(jnp.float32)
    token_pos = positions[0]
    count = tokens.shape[0]
    extent = count + 2 * HALF_WINDOW
    normed, norm_back = jax.vjp(layer_norm, tokens, gain_first)
    normed_low = normed.astype(jnp.bfloat16)
    mixed = jnp.dot(normed_low, full_qkv, preferred_element_type=jnp.float32)
    query_raw = mixed[:, :D].reshape(count, HEADS, HEAD_DIM)
    key_raw = mixed[:, D : 2 * D].reshape(count, HEADS, HEAD_DIM)
    value_low = mixed[:, 2 * D :].astype(jnp.bfloat16)
    query_rot, query_back = jax.vjp(lambda piece: rotary(piece, token_pos), query_raw)
    key_rot, key_back = jax.vjp(lambda piece: rotary(piece, token_pos), key_raw)
    query_low = query_rot.astype(jnp.bfloat16)
    key_value = jnp.concatenate([key_rot.reshape(count, D).astype(jnp.bfloat16), value_low], axis=1)
    flags = (jnp.minimum(token_pos, 127) + 1).astype(jnp.bfloat16)
    wide_kv, wide_flags = (
        with_halo(key_value, (("seq", 0),), HALF_WINDOW),
        with_halo(flags, (("seq", 0),), HALF_WINDOW),
    )
    keys_wide = wide_kv[:, :D].reshape(extent, HEADS, HEAD_DIM)
    values_wide = wide_kv[:, D:].reshape(extent, HEADS, HEAD_DIM)
    allowed = window_mask(token_pos, wide_flags, count)

    def score_table():
        raw = (
            jnp.einsum("qhd,khd->hqk", query_low, keys_wide, preferred_element_type=jnp.float32)
            * scale
        )
        return jnp.where(allowed[None], raw, masked_score)

    scores = score_table()
    top = jnp.max(scores, axis=-1, keepdims=True)
    expo = jnp.exp(scores - top)
    totals = jnp.sum(expo, axis=-1, keepdims=True)
    logsum = top + jnp.log(totals)
    probs_low = (expo / totals).astype(jnp.bfloat16)
    attended = jnp.einsum(
        "hqk,khd->qhd", probs_low, values_wide, preferred_element_type=jnp.float32
    )
    attended_low = attended.reshape(count, D).astype(jnp.bfloat16)
    middle = tokens + jnp.dot(attended_low, full_out, preferred_element_type=jnp.float32)
    normed_mlp, mlp_norm_back = jax.vjp(layer_norm, middle, gain_second)
    normed_mlp_low = normed_mlp.astype(jnp.bfloat16)
    gate_up = jnp.dot(normed_mlp_low, full_in, preferred_element_type=jnp.float32)

    def geglu(paired):
        return jax.nn.gelu(paired[:, :FF], approximate=False) * paired[:, FF:]

    hidden, geglu_back = jax.vjp(geglu, gate_up)
    hidden_low = hidden.astype(jnp.bfloat16)
    result = middle + jnp.dot(hidden_low, full_down, preferred_element_type=jnp.float32)
    grad_result = cotangent[0]
    grad_down_local = matmul_left(hidden_low, grad_result)
    grad_hidden = matmul_right(grad_result, full_down)
    grad_gate_up = geglu_back(grad_hidden)[0].astype(jnp.bfloat16)
    grad_in_local = matmul_left(normed_mlp_low, grad_gate_up)
    grad_normed_mlp = matmul_right(grad_gate_up, full_in)
    grad_middle_norm, grad_gain_second = mlp_norm_back(grad_normed_mlp)
    grad_middle = grad_result.astype(jnp.float32) + grad_middle_norm
    grad_branch = grad_middle.astype(jnp.bfloat16)
    grad_out_local = matmul_left(attended_low, grad_branch)
    grad_attended = (
        matmul_right(grad_branch, full_out).reshape(count, HEADS, HEAD_DIM).astype(jnp.bfloat16)
    )
    probs = jnp.exp(score_table() - logsum)
    probs_low = probs.astype(jnp.bfloat16)
    grad_probs = jnp.einsum(
        "qhd,khd->hqk", grad_attended, values_wide, preferred_element_type=jnp.float32
    )
    row_dot = jnp.sum(probs * grad_probs, axis=-1, keepdims=True)
    grad_scores = (probs * (grad_probs - row_dot)).astype(jnp.bfloat16)
    grad_query = (
        jnp.einsum("hqk,khd->qhd", grad_scores, keys_wide, preferred_element_type=jnp.float32)
        * scale
    )
    grad_keys_wide = (
        jnp.einsum("hqk,qhd->khd", grad_scores, query_low, preferred_element_type=jnp.float32)
        * scale
    )
    grad_values_wide = jnp.einsum(
        "hqk,qhd->khd", probs_low, grad_attended, preferred_element_type=jnp.float32
    )
    grad_wide = jnp.concatenate(
        [grad_keys_wide.reshape(extent, D), grad_values_wide.reshape(extent, D)], axis=1
    )
    rims = jnp.concatenate([grad_wide[:HALF_WINDOW], grad_wide[extent - HALF_WINDOW :]], axis=0)
    returned = with_halo(rims.astype(jnp.bfloat16), (("seq", 0),), HALF_WINDOW).astype(rims.dtype)
    grad_own = grad_wide[HALF_WINDOW : HALF_WINDOW + count]
    grad_own = grad_own.at[:HALF_WINDOW].add(returned[:HALF_WINDOW])
    grad_own = grad_own.at[count - HALF_WINDOW :].add(returned[returned.shape[0] - HALF_WINDOW :])
    grad_key = key_back(grad_own[:, :D].reshape(count, HEADS, HEAD_DIM))[0]
    grad_q = query_back(grad_query)[0]
    grad_mixed = jnp.concatenate(
        [grad_q.reshape(count, D), grad_key.reshape(count, D), grad_own[:, D:]], axis=1
    ).astype(jnp.bfloat16)
    grad_qkv_local = matmul_left(normed_low, grad_mixed)
    grad_normed = matmul_right(grad_mixed, full_qkv)
    grad_tokens_norm, grad_gain_first = norm_back(grad_normed)
    grad_tokens = grad_middle + grad_tokens_norm
    lanes = lax.axis_size("seq")
    owned = (
        lax.psum_scatter(
            grad_qkv_local.astype(jnp.bfloat16), "fsdp", scatter_dimension=0, tiled=True
        ).astype(jnp.float32),
        lax.psum_scatter(
            grad_out_local.astype(jnp.bfloat16), "fsdp", scatter_dimension=0, tiled=True
        ).astype(jnp.float32),
        lax.psum_scatter(
            grad_in_local.astype(jnp.bfloat16), "fsdp", scatter_dimension=0, tiled=True
        ).astype(jnp.float32),
        lax.psum_scatter(
            grad_down_local.astype(jnp.bfloat16), "fsdp", scatter_dimension=0, tiled=True
        ).astype(jnp.float32),
        lax.psum_scatter(
            grad_gain_first.astype(jnp.bfloat16), "fsdp", scatter_dimension=0, tiled=True
        ).astype(jnp.float32),
        lax.psum_scatter(
            grad_gain_second.astype(jnp.bfloat16), "fsdp", scatter_dimension=0, tiled=True
        ).astype(jnp.float32),
    )
    owned_flat = pack_rows(owned, 1)
    owned_share = owned_flat.shape[1] // lanes
    lane_part = lax.psum_scatter(
        owned_flat.reshape(lanes, owned_share), "seq", scatter_dimension=0, tiled=True
    )
    summed_row = (
        lax.all_gather(lane_part.astype(jnp.bfloat16), "seq", axis=0, tiled=True)
        .astype(lane_part.dtype)
        .reshape(-1)
    )
    grad_qkv, grad_out, grad_in, grad_down, grad_gain_attn, grad_gain_mlp = unpack_row(
        summed_row, owned, 1
    )
    return (
        result[None].astype(jnp.bfloat16),
        grad_tokens[None],
        grad_qkv,
        grad_out,
        grad_in,
        grad_down,
        grad_gain_attn,
        grad_gain_mlp,
    )


def solution(mesh):
    in_specs = (
        P("fsdp", "seq", None),
        P("fsdp", "seq"),
        P("fsdp", "seq", None),
        P("fsdp", None),
        P("fsdp", None),
        P("fsdp", None),
        P("fsdp", None),
        P("fsdp"),
        P("fsdp"),
    )
    out_specs = (
        P("fsdp", "seq", None),
        P("fsdp", "seq", None),
        P("fsdp", None),
        P("fsdp", None),
        P("fsdp", None),
        P("fsdp", None),
        P("fsdp"),
        P("fsdp"),
    )
    return jax.shard_map(
        on_device, mesh=mesh, in_specs=in_specs, out_specs=out_specs, check_vma=False
    )
```

profile of v0, /device:TPU:1, one launch (start us, length us, event | category | flops | bytes accessed | tf_op | source)
XLA Modules:
  0.0 703.3 jit_solution(1595886783287851060)
XLA Ops:
  9.6 4.5 collective-permute-start.2
  14.1 1.9 collective-permute-start.3
  18.3 10.3 %all-reduce.12 = (bf16[768]{0:T(1024)(128)(2,1)S(1)}, bf16[768]{0:T(1024)(128)(2,1)S(1)}) all-reduce(bf16[768]{0:T(1024)(128)(2,1)S(1)} %dynamic-update-slice.6, bf16[768]{0:T(1024)(128)(2,1)S(1)} %dynamic-update-slice.7), channel_id=1, replica_groups=mesh['seq'=8,'fsdp'=4] {'fsdp'}, use_global_device_ids=true, to_apply=%add.6 | all-reduce | flops 1536 | bytes 6144
  29.9 52.1 %all-gather.7.cloned.1.call-done = bf16[768,2304]{1,0:T(8,128)(2,1)} async-done(((bf16[192,2304]{1,0:T(8,128)(2,1)}), bf16[768,2304]{1,0:T(8,128)(2,1)}) %all-gather.7.cloned.1.call-update) | async-done | bytes 3538960 | tf_op jit(solution)/shard_map/all_gather | solution.py:97
  82.0 2.7 fusion.51
  85.5 3.7 collective-permute-start
  89.2 1.9 collective-permute-start.1
  91.8 4.8 collective-permute-done.1
  98.8 13.1 %all-gather.9.cloned.1.call-done = bf16[768,768]{1,0:T(8,128)(2,1)} async-done(((bf16[192,768]{1,0:T(8,128)(2,1)}), bf16[768,768]{1,0:T(8,128)(2,1)}) %all-gather.9.cloned.1.call-update) | async-done | bytes 1179664 | tf_op jit(solution)/shard_map/all_gather | solution.py:98
  111.9 1.7 fusion.67
  114.4 68.8 %all-gather.11.cloned.1.call-done = bf16[768,2304]{1,0:T(8,128)(2,1)} async-done(((bf16[192,2304]{1,0:T(8,128)(2,1)}), bf16[768,2304]{1,0:T(8,128)(2,1)}) %all-gather.11.cloned.1.call-update) | async-done | bytes 3538960 | tf_op jit(solution)/shard_map/all_gather | solution.py:99
  183.2 2.7 fusion.54
  185.9 37.7 %all-gather.13.cloned.1.call-done = bf16[1152,768]{1,0:T(8,128)(2,1)} async-done(((bf16[288,768]{1,0:T(8,128)(2,1)}), bf16[1152,768]{1,0:T(8,128)(2,1)}) %all-gather.13.cloned.1.call-update) | async-done | bytes 1769488 | tf_op jit(solution)/shard_map/all_gather | solution.py:100
  223.6 3.3 fusion.38
  226.9 1.8 multiply_add_fusion
  228.7 1.9 multiply_reduce_fusion.1
  233.4 2.8 convolution_convert_fusion.2
  237.2 3.6 convolution_convert_fusion
  242.2 2.1 convolution_convert_fusion.4
  246.1 1.7 multiply_reduce_fusion
  249.4 3.7 collective-permute-start.4
  253.1 1.9 collective-permute-start.5
  256.3 1.5 collective-permute-done.4
  257.8 5.8 collective-permute-done.5
  265.3 5.7 scatter-add.6
  272.4 6.5 scatter-add.9
  279.8 3.1 convolution_convert_fusion.1
  284.8 3.4 fusion.29
  288.5 8.5 %all-reduce.11 = (bf16[768]{0:T(1024)(128)(2,1)S(1)}, bf16[768]{0:T(1024)(128)(2,1)S(1)}) all-reduce(bf16[768]{0:T(1024)(128)(2,1)S(1)} %get-tuple-element.34, bf16[768]{0:T(1024)(128)(2,1)S(1)} %copy-done.32), channel_id=6, replica_groups=mesh['seq'=8,'fsdp'=4] {'fsdp'}, use_global_device_ids=true, to_apply=%region_16.17.clone | all-reduce | flops 1536 | bytes 6144
  298.6 2.9 reduce-scatter.11.cloned.1.call-done
  301.5 1.7 copy.47
  303.2 66.2 %reduce-scatter.9.cloned.1.call-done = bf16[192,2304]{1,0:T(8,128)(2,1)} async-done(((bf16[768,2304]{1,0:T(8,128)(2,1)}), bf16[192,2304]{1,0:T(8,128)(2,1)}) %reduce-scatter.9.cloned.1.call-update) | async-done | bytes 884752 | tf_op jit(solution)/shard_map/reduce_scatter | solution.py:215
  369.4 3.7 copy.46
  373.2 65.4 %reduce-scatter.5.cloned.1.call-done = bf16[192,2304]{1,0:T(8,128)(2,1)} async-done(((bf16[768,2304]{1,0:T(8,128)(2,1)}), bf16[192,2304]{1,0:T(8,128)(2,1)}) %reduce-scatter.5.cloned.1.call-update) | async-done | bytes 884752 | tf_op jit(solution)/shard_map/reduce_scatter | solution.py:209
  438.5 2.5 copy.44
  441.1 3.0 constant_dynamic-update-slice_fusion.3
  445.3 3.0 constant_dynamic-update-slice_fusion.1
  448.3 1.7 constant_dynamic-update-slice_fusion
  452.5 52.0 %convert_reduce_fusion.1 = f32[1253760]{0:T(1024)} fusion(bf16[1,1253760]{1,0:T(2,128)(2,1)} %dynamic-update-slice.13), kind=kLoop, calls=%fused_computation.3 | loop fusion | flops 1253760 | bytes 7522560 | tf_op jit(solution)/shard_map/reshape | solution.py:231
  504.5 7.4 %reshape.371 = f32[8,156720]{1,0:T(8,128)} reshape(f32[1253760]{0:T(1024)} %convert_reduce_fusion.1) | data formatting | bytes 10030080 | tf_op jit(solution)/shard_map/reshape | solution.py:231
  511.9 104.8 %all-reduce.14 = bf16[8,156720]{1,0:T(8,128)(2,1)} all-reduce(f32[8,156720]{1,0:T(8,128)} %reshape.371), channel_id=8, replica_groups=mesh['seq'=8,'fsdp'=4] {'seq'}, use_global_device_ids=true, to_apply=%region_19.20.clone | all-reduce | flops 1253760 | bytes 7522560
  616.7 3.4 fusion.11
  620.2 2.6 fusion.4
  623.8 36.2 %all-gather.15.cloned.1.call-done = bf16[8,1,156720]{2,1,0:T(2,128)(2,1)} async-done(((bf16[1,1,156720]{2,1,0:T(2,128)(2,1)}), bf16[8,1,156720]{2,1,0:T(2,128)(2,1)}) %all-gather.15.cloned.1.call-update) | async-done | bytes 2507536 | tf_op jit(solution)/shard_map/all_gather | solution.py:234
  660.0 17.6 %convert_reduce_fusion = f32[8,156720]{1,0:T(8,128)} fusion(bf16[8,1,156720]{2,1,0:T(2,128)(2,1)} %all-gather.15.cloned.1.call-done), kind=kLoop, calls=%fused_computation.2 | loop fusion | flops 1253760 | bytes 7522560 | tf_op jit(solution)/shard_map/reshape | solution.py:236
  677.6 7.5 %reshape.373 = f32[1253760]{0:T(1024)} reshape(f32[8,156720]{1,0:T(8,128)} %convert_reduce_fusion) | data formatting | bytes 10030080 | tf_op jit(solution)/shard_map/reshape | solution.py:236
  686.6 3.5 fusion.58
  691.0 2.7 reshape.368
  (201 shorter events, 35.3 us)
Async XLA Ops:
  7.2 9.4 %copy-start.34 = (u32[32]{0:T(128)S(1)}, u32[32]{0:T(128)}, u32[]{:S(2)}) copy-start(u32[32]{0:T(128)} %constant.175) | copy-start | bytes 388
  7.2 2.3 copy-start.37
  7.2 9.0 %copy-start.1 = (bf16[1,128,768]{2,1,0:T(8,128)(2,1)S(1)}, bf16[1,128,768]{2,1,0:T(8,128)(2,1)}, u32[]{:S(2)}) copy-start(bf16[1,128,768]{2,1,0:T(8,128)(2,1)} %param.13) | copy-start | bytes 589828
  7.2 10.6 %copy-start.42 = (bf16[192]{0:T(256)(128)(2,1)S(1)}, bf16[192]{0:T(256)(128)(2,1)}, u32[]{:S(2)}) copy-start(bf16[192]{0:T(256)(128)(2,1)} %param.20) | copy-start | bytes 1156
  7.2 10.8 %copy-start.43 = (bf16[192]{0:T(256)(128)(2,1)S(1)}, bf16[192]{0:T(256)(128)(2,1)}, u32[]{:S(2)}) copy-start(bf16[192]{0:T(256)(128)(2,1)} %param.21) | copy-start | bytes 1156
  7.2 74.7 %all-gather.7.cloned.1.call-start = ((), (), s32[]{:S(2)}) async-start(), calls=%async_computation.4 | async-start | bytes 4423680 | tf_op jit(solution)/shard_map/all_gather | solution.py:97
  8.0 104.0 %all-gather.9.cloned.1.call-start = ((), (), s32[]{:S(2)}) async-start(), calls=%async_computation.5 | async-start | bytes 1474560 | tf_op jit(solution)/shard_map/all_gather | solution.py:98
  8.7 174.5 %all-gather.11.cloned.1.call-start = ((), (), s32[]{:S(2)}) async-start(), calls=%async_computation.6 | async-start | bytes 4423680 | tf_op jit(solution)/shard_map/all_gather | solution.py:99
  9.4 214.1 %all-gather.13.cloned.1.call-start = ((), (), s32[]{:S(2)}) async-start(), calls=%async_computation.7 | async-start | bytes 2211840 | tf_op jit(solution)/shard_map/all_gather | solution.py:100
  9.6 20.1 %collective-permute-start.2 = (bf16[64]{0:T(256)(128)(2,1)S(1)}, bf16[64]{0:T(256)(128)(2,1)S(1)}, u32[]{:S(2)}, u32[]{:S(2)}) collective-permute-start(bf16[64]{0:T(256)(128)(2,1)S(1)} %get-tuple-element.76), channel_id=1, source_target_pairs={{0,4},{4,8},{8,12},{12,16},{16,20},{20,24},{24,28},{1,5},{5,9},{9,... | collective-permute-start | bytes 392 | tf_op jit(solution)/shard_map/ppermute | solution.py:28
  14.1 15.6 %collective-permute-start.3 = (bf16[64]{0:T(256)(128)(2,1)S(1)}, bf16[64]{0:T(256)(128)(2,1)S(1)}, u32[]{:S(2)}, u32[]{:S(2)}) collective-permute-start(bf16[64]{0:T(256)(128)(2,1)S(1)} %get-tuple-element.77), channel_id=1, source_target_pairs={{4,0},{8,4},{12,8},{16,12},{20,16},{24,20},{28,24},{5,1},{9,5},{13... | collective-permute-start | bytes 392 | tf_op jit(solution)/shard_map/ppermute | solution.py:30
  16.0 281.1 %reduce-scatter.7.cloned.1.call-start = ((), (), s32[]{:S(2)}) async-start(), calls=%async_computation.9 | async-start | bytes 1474560 | tf_op jit(solution)/shard_map/reduce_scatter | solution.py:212
  16.3 68.4 %copy-start.26 = (f32[128]{0:T(128)}, f32[128]{0:T(128)S(1)}, u32[]{:S(2)}) copy-start(f32[128]{0:T(128)S(1)} %broadcast_multiply_fusion.5) | copy-start | bytes 1540
  16.5 1.6 copy-start.38
  16.5 68.2 %copy-start.28 = (f32[128]{0:T(128)}, f32[128]{0:T(128)S(1)}, u32[]{:S(2)}) copy-start(f32[128]{0:T(128)S(1)} %fusion.44) | copy-start | bytes 1540
  29.4 61.7 %copy-start.19 = (f32[128,64]{0,1:T(8,128)}, f32[128,64]{0,1:T(8,128)S(1)}, u32[]{:S(2)}) copy-start(f32[128,64]{0,1:T(8,128)S(1)} %get-tuple-element.71) | copy-start | bytes 98308
  29.4 61.7 %copy-start.21 = (f32[128,64]{0,1:T(8,128)}, f32[128,64]{0,1:T(8,128)S(1)}, u32[]{:S(2)}) copy-start(f32[128,64]{0,1:T(8,128)S(1)} %get-tuple-element.92) | copy-start | bytes 98308
  85.5 6.3 collective-permute-start
  89.2 7.4 %collective-permute-start.1 = (bf16[64,1536]{1,0:T(8,128)(2,1)S(1)}, bf16[64,1536]{1,0:T(8,128)(2,1)S(1)}, u32[]{:S(2)}, u32[]{:S(2)}) collective-permute-start(bf16[64,1536]{1,0:T(8,128)(2,1)S(1)} %get-tuple-element.65), channel_id=1, source_target_pairs={{4,0},{8,4},{12,8},{16,12},{20,16},{24,20},{28,24},{5,1},{9,5},{13... | collective-permute-start | bytes 589832 | tf_op jit(solution)/shard_map/ppermute | solution.py:30
  98.8 15.6 %copy-start.17 = (bf16[12,64,128]{2,1,0:T(8,128)(2,1)}, bf16[12,64,128]{2,1,0:T(8,128)(2,1)S(1)}, u32[]{:S(2)}) copy-start(bf16[12,64,128]{2,1,0:T(8,128)(2,1)S(1)} %convolution_convert_fusion.5) | copy-start | bytes 589828
  185.9 41.0 %copy-start.4 = (f32[128,2304]{1,0:T(8,128)}, f32[128,2304]{1,0:T(8,128)S(1)}, u32[]{:S(2)}) copy-start(f32[128,2304]{1,0:T(8,128)S(1)} %fusion.54) | copy-start | bytes 3538948
  223.6 5.1 copy-start
  226.9 1.8 copy-start.11
  226.9 1.8 copy-start.31
  226.9 1.8 copy-start.33
  228.7 4.7 copy-start.9
  228.7 2.0 copy-start.41
  228.7 2.9 copy-start.14
  230.9 2.4 copy-start.35
  231.8 1.6 copy-start.13
  233.3 68.2 %reduce-scatter.11.cloned.1.call-start = ((), (), s32[]{:S(2)}) async-start(), calls=%async_computation.11 | async-start | bytes 2211840 | tf_op jit(solution)/shard_map/reduce_scatter | solution.py:218
  236.2 133.2 %reduce-scatter.9.cloned.1.call-start = ((), (), s32[]{:S(2)}) async-start(), calls=%async_computation.10 | async-start | bytes 4423680 | tf_op jit(solution)/shard_map/reduce_scatter | solution.py:215
  240.9 197.6 %reduce-scatter.5.cloned.1.call-start = ((), (), s32[]{:S(2)}) async-start(), calls=%async_computation.8 | async-start | bytes 4423680 | tf_op jit(solution)/shard_map/reduce_scatter | solution.py:209
  249.1 5.9 copy-start.8
  249.1 5.9 copy-start.23
  249.4 8.4 %collective-permute-start.4 = (bf16[64,1536]{0,1:T(8,128)(2,1)S(1)}, bf16[64,1536]{0,1:T(8,128)(2,1)S(1)}, u32[]{:S(2)}, u32[]{:S(2)}) collective-permute-start(bf16[64,1536]{0,1:T(8,128)(2,1)S(1)} %get-tuple-element.54), channel_id=1, source_target_pairs={{0,4},{4,8},{8,12},{12,16},{16,20},{20,24},{24,28},{1,5},{5,9},{9,... | collective-permute-start | bytes 589832 | tf_op jit(solution)/shard_map/ppermute | solution.py:28
  253.1 10.5 %collective-permute-start.5 = (bf16[64,1536]{0,1:T(8,128)(2,1)S(1)}, bf16[64,1536]{0,1:T(8,128)(2,1)S(1)}, u32[]{:S(2)}, u32[]{:S(2)}) collective-permute-start(bf16[64,1536]{0,1:T(8,128)(2,1)S(1)} %get-tuple-element.55), channel_id=1, source_target_pairs={{4,0},{8,4},{12,8},{16,12},{20,16},{24,20},{28,24},{5,1},{9,5},{13... | collective-permute-start | bytes 589832 | tf_op jit(solution)/shard_map/ppermute | solution.py:30
  272.4 6.7 copy-start.20
  282.9 377.1 %all-gather.15.cloned.1.call-start = ((), (), s32[]{:S(2)}) async-start(), calls=%async_computation.12 | async-start | bytes 5644800 | tf_op jit(solution)/shard_map/all_gather | solution.py:234
  284.8 3.4 copy-start.39
  284.8 3.7 copy-start.32
  441.0 4.3 copy-start.2
  616.7 3.5 copy-start.10
  620.1 2.7 copy-start.6
  620.1 2.7 copy-start.15
  620.1 2.7 copy-start.36
  686.5 3.5 slice-start
  691.0 2.7 slice-start.1
  (14 other events, 12.2 us)
Sparse Core Ops, SparseCore 0:
  9.6 72.2 all-gather.6
  83.5 28.3 all-gather.8
  113.5 69.6 all-gather.10
  184.6 38.9 all-gather.12
  233.4 27.8 reduce-scatter.6
  264.1 37.3 reduce-scatter.10
  303.9 65.4 reduce-scatter.8
  371.8 66.6 reduce-scatter.4
  620.3 39.7 all-gather.14
where the time goes:
time: 713 us; the launch traced here: 703 us
  waiting for transfers between devices  357 us (50%)
  blocking collectives  124 us (17%)
  other arithmetic  80.7 us (11%)
  local copies, waits for them, and re-layouts  71.4 us (10%)
  matrix products  35.5 us (5%)
  starting transfers between devices  18.1 us (3%)
  between operations  16.6 us (2%)
    unnamed x3, blocking collectives  124 us
    all_gather x1, waiting for transfers between devices, on_device(): lax.all_gather(w_in, 'fsdp', axis=0, tiled=True)  68.8 us
    reduce_scatter x1, waiting for transfers between devices, on_device(): lax.psum_scatter(grad_in_local.astype(jnp.bfloat16), 'fsdp', scatter_dime...  66.2 us
    reduce_scatter x1, waiting for transfers between devices, on_device(): lax.psum_scatter(grad_qkv_local.astype(jnp.bfloat16), 'fsdp', scatter_dim...  65.4 us
    all_gather x1, waiting for transfers between devices, on_device(): lax.all_gather(w_qkv, 'fsdp', axis=0, tiled=True)  52.1 us
    reshape x1, other arithmetic, on_device(): owned_flat.reshape(lanes, owned_share)  52 us
    all_gather x1, waiting for transfers between devices, on_device(): lax.all_gather(w_down, 'fsdp', axis=0, tiled=True)  37.7 us
    all_gather x1, waiting for transfers between devices, on_device(): lax.all_gather(lane_part.astype(jnp.bfloat16), 'seq', axis=0, tiled=True)  36.2 us
  transfers between devices with their start and end apart: 15, of which 12 were waited for; matrix products, arithmetic and copies ran while one was open for 9% of the time, Pallas kernels for 0%

commit v1 on v0

--- a/solution.py
+++ b/solution.py
@@ -1,8 +1,11 @@
+import functools
 import math
 
 import jax
 import jax.numpy as jnp
 from jax import lax
+from jax.experimental import pallas as pl
+from jax.experimental.pallas import tpu as pltpu
 from jax.sharding import PartitionSpec as P
 
 D = 768
@@ -92,18 +95,320 @@
     return results
 
 
+MESH = pl.DeviceIdType.MESH
+PAD = 32
+SHARES = ((48, 1152), (48, 384), (48, 1152), (80, 384))
+BIT1_FIRST = (True, True, False, False)
+
+
+def partner(me, step):
+    return me + step * (1 - 2 * ((me // step) % 2))
+
+
+def place():
+    me, z = lax.axis_index("seq"), lax.axis_index("fsdp")
+    core, b1, b2 = me % 2, (me // 2) % 2, (me // 4) % 2
+    return me, z, core, b1, b2
+
+
+def greet(me, z):
+    barrier = pltpu.get_barrier_semaphore()
+    for step in (1, 2, 4):
+        pl.semaphore_signal(
+            barrier, inc=1, device_id={"seq": partner(me, step)}, device_id_type=MESH
+        )
+    for step in (1, 2, 3):
+        pl.semaphore_signal(
+            barrier, inc=1, device_id={"fsdp": (z + step) % 4}, device_id_type=MESH
+        )
+    pl.semaphore_wait(barrier, 6)
+
+
+def rows(block, size, count=1):
+    return pl.ds(pl.multiple_of(block * size, 16), size * count)
+
+
+def cols(half, size):
+    return pl.ds(pl.multiple_of(half * size, 128), size)
+
+
+def push(src, dst, send, recv, target):
+    return pltpu.make_async_remote_copy(
+        src_ref=src, dst_ref=dst, send_sem=send, recv_sem=recv,
+        device_id=target, device_id_type=MESH,
+    )
+
+
+def gather_kernel(*refs):
+    ins, outs = refs[:4], refs[4:8]
+    local, zs, zr, fs, s1, r1, s2, r2, s3, r3 = refs[8:]
+    me, z, core, b1, b2 = place()
+    quarter = b1 + 2 * b2
+    greet(me, z)
+    inner = (z == 1) | (z == 2)
+    sent = []
+    own = []
+    for w, (r, c) in enumerate(SHARES):
+        src = ins[w].at[rows(quarter, r), cols(core, c)]
+        dst = outs[w].at[z, rows(quarter, r), cols(core, c)]
+        up = push(src, dst, zs.at[w, 0], zr.at[w, z], {"fsdp": lax.rem(z + 1, 4)})
+        down = push(src, dst, zs.at[w, 1], zr.at[w, z], {"fsdp": lax.rem(z + 3, 4)})
+        own.append((up, down))
+        pl.when(z < 3)(up.start)
+        pl.when(z > 0)(down.start)
+    copies = []
+    for w in range(4):
+        copy = pltpu.make_async_copy(ins[w], outs[w].at[z], local.at[w])
+        copy.start()
+        copies.append(copy)
+    first = (z + 3) % 4 - 2 * ((3 - z) // 3)
+    last = 3 * (1 - z // 2)
+    second = 6 - z - first - last
+    origins = (first, second, last)
+    onward = ((z + 1) % 4, (z + 3) % 4, (3 * z + 1) % 4)
+    events = [(k, w) for k in range(3) for w in range(4)]
+    forwards, stage1, stage2, stage3 = {}, {}, {}, {}
+
+    def arrive(k, w):
+        r, c = SHARES[w]
+        o = origins[k]
+        mine = outs[w].at[o, rows(quarter, r), cols(core, c)]
+        forward = push(mine, mine, fs.at[w, k], zr.at[w, o], {"fsdp": onward[k]})
+        forwards[k, w] = forward
+        forward.wait_recv()
+        pl.when(inner)(forward.start)
+        step = 2 if BIT1_FIRST[w] else 4
+        copy = push(mine, mine, s1.at[w, k], r1.at[w, k], {"seq": partner(me, step)})
+        copy.start()
+        stage1[k, w] = copy
+
+    def pair(k, w):
+        r, c = SHARES[w]
+        o = origins[k]
+        stage1[k, w].wait_recv()
+        half = cols(core, c)
+        if BIT1_FIRST[w]:
+            blocks = [outs[w].at[o, rows(2 * b2, r, 2), half]]
+            step = 4
+        else:
+            blocks = [outs[w].at[o, rows(b1 + 2 * j, r), half] for j in range(2)]
+            step = 2
+        stage2[k, w] = []
+        for j, block in enumerate(blocks):
+            copy = push(block, block, s2.at[w, k, j], r2.at[w, k, j], {"seq": partner(me, step)})
+            copy.start()
+            stage2[k, w].append(copy)
+
+    def across(k, w):
+        r, c = SHARES[w]
+        for copy in stage2[k, w]:
+            copy.wait_recv()
+        block = outs[w].at[origins[k], :, cols(core, c)]
+        copy = push(block, block, s3.at[w, k], r3.at[w, k], {"seq": partner(me, 1)})
+        copy.start()
+        stage3[k, w] = copy
+
+    for t in range(len(events) + 4):
+        if t < len(events):
+            arrive(*events[t])
+        if 0 <= t - 2 < len(events):
+            pair(*events[t - 2])
+        if 0 <= t - 4 < len(events):
+            across(*events[t - 4])
+    for event in events:
+        stage3[event].wait_recv()
+    for copy in copies:
+        copy.wait()
+    for up, down in own:
+        pl.when(z < 3)(up.wait_send)
+        pl.when(z > 0)(down.wait_send)
+    for event in events:
+        pl.when(inner)(forwards[event].wait_send)
+        stage1[event].wait_send()
+        for copy in stage2[event]:
+            copy.wait_send()
+        stage3[event].wait_send()
+
+
+def gather_weights(shards):
+    sem = pltpu.SemaphoreType.DMA
+    return pl.pallas_call(
+        gather_kernel,
+        out_shape=[jax.ShapeDtypeStruct((4, 4 * r, 2 * c), jnp.bfloat16) for r, c in SHARES],
+        in_specs=[pl.BlockSpec(memory_space=pl.ANY)] * 4,
+        out_specs=[pl.BlockSpec(memory_space=pl.ANY)] * 4,
+        scratch_shapes=[
+            sem((4,)), sem((4, 2)), sem((4, 4)), sem((4, 3)), sem((4, 3)), sem((4, 3)),
+            sem((4, 3, 2)), sem((4, 3, 2)), sem((4, 3)), sem((4, 3)),
+        ],
+        compiler_params=pltpu.CompilerParams(collective_id=0, has_side_effects=True),
+    )(*shards)
+
+
+def reduce_kernel(*refs):
+    ins, outs = refs[:4], refs[4:8]
+    cb, cs, b1s, s1s, b2s, s2s, bz, ag = (refs[8 + 4 * i : 12 + 4 * i] for i in range(8))
+    csem, sem1, sem2, zsem, asem = refs[40:]
+    me, z, core, b1, b2 = place()
+    quarter = b1 + 2 * b2
+    greet(me, z)
+    f32, low = jnp.float32, jnp.bfloat16
+    sent = []
+    table = {}
+
+    def go(key, src, dst, sems, target):
+        copy = push(src, dst, sems.at[0], sems.at[1], target)
+        copy.start()
+        sent.append(copy)
+        table.setdefault(key, []).append(copy)
+
+    def take(key):
+        for copy in table[key]:
+            copy.wait_recv()
+
+    def begin(w):
+        r, c = SHARES[w]
+        src = ins[w].at[:, :, cols(1 - core, c)]
+        go((0, w), src, cb[w], csem.at[w], {"seq": partner(me, 1)})
+
+    def core_sum(w):
+        r, c = SHARES[w]
+        take((0, w))
+
+        def body(i, carry):
+            part = (i // 4, pl.ds(pl.multiple_of((i % 4) * r, 16), r))
+            mine = ins[w][part[0], part[1], cols(core, c)].astype(f32)
+            cs[w][part[0], part[1], :] = (mine + cb[w][part[0], part[1], :].astype(f32)).astype(low)
+            return carry
+
+        lax.fori_loop(0, 16, body, 0)
+        if BIT1_FIRST[w]:
+            src = cs[w].at[:, rows(2 * (1 - b2), r, 2), :]
+            go((1, w), src, b1s[w], sem1.at[w, 0], {"seq": partner(me, 4)})
+        else:
+            for j in range(2):
+                src = cs[w].at[:, rows(1 - b1 + 2 * j, r), :]
+                dst = b1s[w].at[:, pl.ds(j * r, r), :]
+                go((1, w), src, dst, sem1.at[w, j], {"seq": partner(me, 2)})
+
+    def pair_sum(w):
+        r, c = SHARES[w]
+        take((1, w))
+
+        def body(i, carry):
+            o, j = i // 2, i % 2
+            block = 2 * b2 + j if BIT1_FIRST[w] else b1 + 2 * j
+            there = pl.ds(pl.multiple_of(j * r, 16), r)
+            mine = cs[w][o, rows(block, r), :].astype(f32)
+            s1s[w][o, there, :] = (mine + b1s[w][o, there, :].astype(f32)).astype(low)
+            return carry
+
+        lax.fori_loop(0, 8, body, 0)
+        bit, step = (b1, 2) if BIT1_FIRST[w] else (b2, 4)
+        src = s1s[w].at[:, rows(1 - bit, r), :]
+        go((2, w), src, b2s[w], sem2.at[w], {"seq": partner(me, step)})
+
+    def share_sum(w):
+        r, c = SHARES[w]
+        take((2, w))
+        bit = b1 if BIT1_FIRST[w] else b2
+
+        def body(o, carry):
+            mine = s1s[w][o, rows(bit, r), :].astype(f32)
+            s2s[w][o] = (mine + b2s[w][o].astype(f32)).astype(low)
+            return carry
+
+        lax.fori_loop(0, 4, body, 0)
+        for d in (2, 1, 3):
+            to = (z + d) % 4
+            go((3, w), s2s[w].at[to], bz[w].at[d - 1], zsem.at[w, d - 1], {"fsdp": to})
+
+    def owner_sum(w):
+        r, c = SHARES[w]
+        take((3, w))
+        total = s2s[w][z].astype(f32)
+        for d in range(3):
+            total = total + bz[w][d].astype(f32)
+        ag[w][rows(quarter, r), cols(core, c)] = total.astype(low)
+        block = ag[w].at[rows(quarter, r), cols(core, c)]
+        step = 2 if BIT1_FIRST[w] else 4
+        go((4, w), block, block, asem.at[w, 0], {"seq": partner(me, step)})
+
+    def spread(w):
+        r, c = SHARES[w]
+        take((4, w))
+        half = cols(core, c)
+        if BIT1_FIRST[w]:
+            block = ag[w].at[rows(2 * b2, r, 2), half]
+            go((5, w), block, block, asem.at[w, 1], {"seq": partner(me, 4)})
+        else:
+            for j in range(2):
+                block = ag[w].at[rows(b1 + 2 * j, r), half]
+                go((5, w), block, block, asem.at[w, 1 + j], {"seq": partner(me, 2)})
+
+    def across(w):
+        r, c = SHARES[w]
+        take((5, w))
+        block = ag[w].at[:, cols(core, c)]
+        go((6, w), block, block, asem.at[w, 3], {"seq": partner(me, 1)})
+
+    def finish(w):
+        r, c = SHARES[w]
+        take((6, w))
+
+        def body(i, carry):
+            part = pl.ds(pl.multiple_of(i * r, 16), r)
+            outs[w][part, :] = ag[w][part, :].astype(f32)
+            return carry
+
+        lax.fori_loop(0, 4, body, 0)
+
+    order = (2, 0, 3, 1)
+    steps = (core_sum, pair_sum, share_sum, owner_sum, spread, across, finish)
+    for w in order:
+        begin(w)
+    for t in range(len(steps) + 3):
+        for i, w in enumerate(order):
+            if 0 <= t - i < len(steps):
+                steps[t - i](w)
+    for copy in sent:
+        copy.wait_send()
+
+
+def reduce_grads(parts):
+    sem = pltpu.SemaphoreType.DMA
+    vmem = lambda shape: pltpu.VMEM(shape, jnp.bfloat16)
+    half = [vmem((4, 4 * r, c)) for r, c in SHARES]
+    two = [vmem((4, 2 * r, c)) for r, c in SHARES]
+    one = [vmem((4, r, c)) for r, c in SHARES]
+    slots = [vmem((3, r, c)) for r, c in SHARES]
+    whole = [vmem((4 * r, 2 * c)) for r, c in SHARES]
+    return pl.pallas_call(
+        reduce_kernel,
+        out_shape=[jax.ShapeDtypeStruct((4 * r, 2 * c), jnp.float32) for r, c in SHARES],
+        in_specs=[pl.BlockSpec(memory_space=pltpu.VMEM)] * 4,
+        out_specs=[pl.BlockSpec(memory_space=pltpu.VMEM)] * 4,
+        scratch_shapes=half + half + two + two + one + one + slots + whole
+        + [sem((4, 2)), sem((4, 2, 2)), sem((4, 2)), sem((4, 3, 2)), sem((4, 4, 2))],
+        compiler_params=pltpu.CompilerParams(
+            collective_id=1, has_side_effects=True, vmem_limit_bytes=56 * 1024 * 1024
+        ),
+    )(*parts)
+
+
 def on_device(inputs, positions, cotangent, w_qkv, w_out, w_in, w_down, gain_attn, gain_mlp):
-    gathered = (
-        lax.all_gather(w_qkv, "fsdp", axis=0, tiled=True),
-        lax.all_gather(w_out, "fsdp", axis=0, tiled=True),
-        lax.all_gather(w_in, "fsdp", axis=0, tiled=True),
-        lax.all_gather(w_down, "fsdp", axis=0, tiled=True),
-        lax.all_gather(gain_attn, "fsdp", axis=0, tiled=True),
-        lax.all_gather(gain_mlp, "fsdp", axis=0, tiled=True),
-    )
-    full_qkv, full_out, full_in, full_down, gain_first, gain_second = gathered
-    gain_first = gain_first.astype(jnp.float32)
-    gain_second = gain_second.astype(jnp.float32)
+    gains = jnp.concatenate([gain_attn, gain_mlp])
+    gains = jnp.pad(gains[None], ((0, PAD - 1), (0, D - gains.shape[0])))
+    packed = jnp.concatenate([w_down, gains], axis=0)
+    full_qkv, full_out, full_in, full_packed = gather_weights([w_qkv, w_out, w_in, packed])
+    full_qkv = full_qkv.reshape(D, 3 * D)
+    full_out = full_out.reshape(D, D)
+    full_in = full_in.reshape(D, 2 * FF)
+    owned_rows = w_down.shape[0]
+    full_down = full_packed[:, :owned_rows].reshape(FF, D)
+    held = gain_attn.shape[0]
+    gain_first = full_packed[:, owned_rows, :held].reshape(D).astype(jnp.float32)
+    gain_second = full_packed[:, owned_rows, held : 2 * held].reshape(D).astype(jnp.float32)
     scale = HEAD_DIM ** (-0.5)
     tokens = inputs[0].astype(jnp.float32)
     token_pos = positions[0]
@@ -118,14 +423,14 @@
     query_rot, query_back = jax.vjp(lambda piece: rotary(piece, token_pos), query_raw)
     key_rot, key_back = jax.vjp(lambda piece: rotary(piece, token_pos), key_raw)
     query_low = query_rot.astype(jnp.bfloat16)
-    key_value = jnp.concatenate([key_rot.reshape(count, D).astype(jnp.bfloat16), value_low], axis=1)
     flags = (jnp.minimum(token_pos, 127) + 1).astype(jnp.bfloat16)
-    wide_kv, wide_flags = (
-        with_halo(key_value, (("seq", 0),), HALF_WINDOW),
-        with_halo(flags, (("seq", 0),), HALF_WINDOW),
-    )
+    key_value = jnp.concatenate(
+        [key_rot.reshape(count, D).astype(jnp.bfloat16), value_low, flags[:, None]], axis=1
+    )
+    wide_kv = with_halo(key_value, (("seq", 0),), HALF_WINDOW)
+    wide_flags = wide_kv[:, 2 * D]
     keys_wide = wide_kv[:, :D].reshape(extent, HEADS, HEAD_DIM)
-    values_wide = wide_kv[:, D:].reshape(extent, HEADS, HEAD_DIM)
+    values_wide = wide_kv[:, D : 2 * D].reshape(extent, HEADS, HEAD_DIM)
     allowed = window_mask(token_pos, wide_flags, count)
 
     def score_table():
@@ -190,11 +495,19 @@
     grad_wide = jnp.concatenate(
         [grad_keys_wide.reshape(extent, D), grad_values_wide.reshape(extent, D)], axis=1
     )
-    rims = jnp.concatenate([grad_wide[:HALF_WINDOW], grad_wide[extent - HALF_WINDOW :]], axis=0)
-    returned = with_halo(rims.astype(jnp.bfloat16), (("seq", 0),), HALF_WINDOW).astype(rims.dtype)
-    grad_own = grad_wide[HALF_WINDOW : HALF_WINDOW + count]
-    grad_own = grad_own.at[:HALF_WINDOW].add(returned[:HALF_WINDOW])
-    grad_own = grad_own.at[count - HALF_WINDOW :].add(returned[returned.shape[0] - HALF_WINDOW :])
+    lanes = lax.axis_size("seq")
+    above = lax.ppermute(
+        grad_wide[extent - HALF_WINDOW :].astype(jnp.bfloat16),
+        "seq",
+        [(i, i + 1) for i in range(lanes - 1)],
+    )
+    below = lax.ppermute(
+        grad_wide[:HALF_WINDOW].astype(jnp.bfloat16),
+        "seq",
+        [(i + 1, i) for i in range(lanes - 1)],
+    )
+    returned = jnp.concatenate([above, below], axis=0).astype(jnp.float32)
+    grad_own = grad_wide[HALF_WINDOW : HALF_WINDOW + count] + returned
     grad_key = key_back(grad_own[:, :D].reshape(count, HEADS, HEAD_DIM))[0]
     grad_q = query_back(grad_query)[0]
     grad_mixed = jnp.concatenate(
@@ -204,7 +517,33 @@
     grad_normed = matmul_right(grad_mixed, full_qkv)
     grad_tokens_norm, grad_gain_first = norm_back(grad_normed)
     grad_tokens = grad_middle + grad_tokens_norm
-    lanes = lax.axis_size("seq")
+    if lanes == 8:
+        gain_rows = jnp.concatenate(
+            [grad_gain_first.reshape(4, 1, held), grad_gain_second.reshape(4, 1, held)], axis=2
+        )
+        gain_rows = jnp.pad(gain_rows, ((0, 0), (0, PAD - 1), (0, D - 2 * held)))
+        grad_packed = jnp.concatenate(
+            [grad_down_local.reshape(4, owned_rows, D), gain_rows], axis=1
+        )
+        parts = (
+            grad_qkv_local.reshape(4, held, 3 * D),
+            grad_out_local.reshape(4, held, D),
+            grad_in_local.reshape(4, held, 2 * FF),
+            grad_packed,
+        )
+        grad_qkv, grad_out, grad_in, packed = reduce_grads(
+            [part.astype(jnp.bfloat16) for part in parts]
+        )
+        return (
+            result[None].astype(jnp.bfloat16),
+            grad_tokens[None],
+            grad_qkv,
+            grad_out,
+            grad_in,
+            packed[:owned_rows],
+            packed[owned_rows, :held],
+            packed[owned_rows, held : 2 * held],
+        )
     owned = (
         lax.psum_scatter(
             grad_qkv_local.astype(jnp.bfloat16), "fsdp", scatter_dimension=0, tiled=True

time: 713 us -> 281 us (0.39); the launches traced: 703 us -> 280 us
  waiting for transfers between devices: 357 us -> 5.49 us
  Pallas kernels: 0 us -> 202 us
  blocking collectives: 124 us -> 0 us
  other arithmetic: 80.7 us -> 15.7 us
  local copies, waits for them, and re-layouts: 71.4 us -> 17.8 us
  between operations: 16.6 us -> 1.36 us
  matrix products: 35.5 us -> 27.4 us
  starting transfers between devices: 18.1 us -> 10.9 us
    all_gather x5 -> x0, waiting for transfers between devices: 208 us -> none  [the longest x1 68.8 us: on_device(): lax.all_gather(w_in, 'fsdp', axis=0, tiled=True)]
    pallas_call x0 -> x2, Pallas kernels: none -> 202 us  [the longest x1 118 us: reduce_grads(): pl.pallas_call(reduce_kernel, out_shape=[jax.ShapeDtypeStruct((4 * r, 2 *...]
    reduce_scatter x4 -> x0, waiting for transfers between devices: 135 us -> none  [the longest x1 66.2 us: on_device(): lax.psum_scatter(grad_in_local.astype(jnp.bfloat16), 'fsdp', scatter_dime...]
    unnamed x3 -> x0, blocking collectives: 124 us -> none
    reshape x2 -> x0, other arithmetic: 69.6 us -> none  [the longest x1 52 us: on_device(): owned_flat.reshape(lanes, owned_share)]
    unnamed x108 -> x71, local copies, waits for them, and re-layouts: 29.3 us -> 7.29 us
    reshape x8 -> x6, local copies, waits for them, and re-layouts: 21.2 us -> 2.8 us  [the longest x1 1.39 us: on_device(): grad_values_wide.reshape(extent, D)]
    scatter-add x2 -> x0, local copies, waits for them, and re-layouts: 12.3 us -> none  [the longest x1 6.54 us: on_device(): grad_own.at[count - HALF_WINDOW:]]
  transfers between devices with their start and end apart: 15 -> 4, of which waited for: 12 -> 2; matrix products, arithmetic and copies ran while one was open for 9% -> 2% of each run, Pallas kernels for 0% -> 0%
where the time goes in v1:
time: 281 us; the launch traced here: 280 us
  Pallas kernels  202 us (72%)
  matrix products  27.4 us (10%)
  local copies, waits for them, and re-layouts  17.8 us (6%)
  other arithmetic  15.7 us (6%)
  starting transfers between devices  10.9 us (4%)
  waiting for transfers between devices  5.49 us (2%)
    pallas_call x1, Pallas kernels, reduce_grads(): pl.pallas_call(reduce_kernel, out_shape=[jax.ShapeDtypeStruct((4 * r, 2 *...  118 us
    pallas_call x1, Pallas kernels, gather_weights(): pl.pallas_call(gather_kernel, out_shape=[jax.ShapeDtypeStruct((4, 4 * r,...  84 us
    dot_general x4, matrix products, matmul_left(): lax.dot_general(left, right, (((0,), (0,)), ((), ())), preferred_element_...  9.14 us
    unnamed x71, local copies, waits for them, and re-layouts  7.29 us
    dot_general x4, matrix products, matmul_right(): lax.dot_general(left, right, (((1,), (1,)), ((), ())), preferred_element_...  6.83 us
  transfers between devices with their start and end apart: 4, of which 2 were waited for; matrix products, arithmetic and copies ran while one was open for 2% of the time, Pallas kernels for 0%

profile of v1, /device:TPU:1, one launch (start us, length us, event | category | flops | bytes accessed | tf_op | source)
XLA Modules:
  0.0 280.4 jit_solution(1544354579836302284)
XLA Ops:
  0.6 1.0 convert_reduce_fusion
  1.7 1.1 fusion.29
  2.8 0.5 copy-done.32
  3.4 0.8 pad_maximum_fusion.11
  4.2 1.9 fusion.24.refs_3_
  6.0 84.0 %shard_map.152 = (bf16[4,192,2304]{2,1,0:T(8,128)(2,1)}, bf16[4,192,768]{2,1,0:T(8,128)(2,1)}, bf16[4,192,2304]{2,1,0:T(8,128)(2,1)}, bf16[4,320,768]{2,1,0:T(8,128)(2,1)}) custom-call(bf16[192,2304]{1,0:T(8,128)(2,1)} %refs_0_.1, bf16[192,768]{1,0:T(8,128)(2,1)} %refs_1_.1, bf16[192,2304]{1,0:T(8,128)(2,1)} %refs_2_.1, bf16[320,768]{1,0:T(8,128)(2,1)} %fusion.24.refs_3_), custom_call_target="tpu_custom_call" | custom-call | tf_op jit(solution)/shard_map/pallas_call | solution.py:235
  90.0 0.9 convert_reduce_fusion.1
  91.0 2.7 fusion.46
  94.0 0.6 broadcast_multiply_fusion.2
  95.5 4.1 %collective-permute-start = (bf16[64,1537]{1,0:T(8,128)(2,1)S(1)}, bf16[64,1537]{1,0:T(8,128)(2,1)S(1)}, u32[]{:S(2)}, u32[]{:S(2)}) collective-permute-start(bf16[64,1537]{1,0:T(8,128)(2,1)S(1)} %get-tuple-element.44), channel_id=1, source_target_pairs={{0,4},{4,8},{8,12},{12,16},{16,20},{20,24},{24,28},{1,5},{5,9},{9,... | collective-permute-start | bytes 590216 | tf_op jit(solution)/shard_map/ppermute | solution.py:31
  99.6 2.1 collective-permute-start.1
  101.7 1.3 slice.95
  103.4 3.3 %collective-permute-done.1 = bf16[64,1537]{1,0:T(8,128)(2,1)S(1)} collective-permute-done((bf16[64,1537]{1,0:T(8,128)(2,1)S(1)}, bf16[64,1537]{1,0:T(8,128)(2,1)S(1)}, u32[]{:S(2)}, u32[]{:S(2)}) %collective-permute-start.1) | collective-permute-done | bytes 196768 | tf_op jit(solution)/shard_map/ppermute | solution.py:33
  107.6 0.5 fusion.78
  108.1 0.5 fusion.1
  108.7 0.7 convolution_convert_fusion.5
  109.4 0.6 copy-done.5
  111.0 0.7 fusion.69
  111.7 0.8 copy-done.2
  112.5 1.6 fusion.54
  114.4 1.4 multiply_reduce_fusion.1
  116.7 1.4 fusion.6
  118.0 2.4 multiply_reduce_fusion
  120.5 3.0 %convolution_convert_fusion = bf16[768,2304]{1,0:T(8,128)(2,1)} fusion(f32[128,1152]{1,0:T(8,128)S(1)} %get-tuple-element.36, f32[128,1152]{1,0:T(8,128)S(1)} %get-tuple-element.32, f32[128,768]{1,0:T(8,128)S(1)} %get-tuple-element.66, f32[768]{0:T(1024)S(1)} %reshape.331, f32[128]{0:T(128)S(1)} %fusion.63, f32[128]{0:T(128)S(1)} %broadcast_multiply_fusion.4), kind=kOutput, calls=%fused_computation | convolution fusion | flops 455737344 | bytes 5115904 | tf_op jit(solution)/shard_map/dot_general | solution.py:71
  123.4 0.9 copy.52
  124.4 1.5 convolution_convert_fusion.3.refs_1_
  125.9 1.4 copy.47
  127.3 1.9 multiply_convert_fusion
  129.5 0.7 copy-done.7
  130.2 1.3 broadcast_multiply_fusion
  131.8 1.1 fusion.76
  132.8 1.1 add_convert_fusion.2
  133.9 0.8 copy.49
  134.9 2.1 collective-permute-start.2
  136.9 2.6 collective-permute-start.3
  139.6 1.8 convolution_convert_fusion.2
  141.4 1.1 fusion.4
  142.5 2.2 collective-permute-done.3
  146.0 3.4 %fusion.30 = (f32[128]{0:T(128)S(1)}, f32[128,768]{1,0:T(8,128)S(1)}) fusion(bf16[1,128,768]{2,1,0:T(8,128)(2,1)S(1)} %copy-done.1, f32[768]{0:T(1024)S(1)} %reshape.330, f32[128]{0:T(128)S(1)} %copy-done.26, bf16[768,2304]{1,0:T(8,128)(2,1)} %bitcast.132, bf16[128,768]{1,0:T(8,128)(2,1)S(1)} %slice.153, bf16[128,768]{1,0:T(8,128)(2,1)S(1)} %copy.50, ...), kind=kOutput, calls=%fused_computation.72 | convolution fusion | flops 455245696 | bytes 4722688 | tf_op jit(solution)/shard_map/dot_general | solution.py:77
  150.0 2.8 %convolution_convert_fusion.1.refs_0_ = bf16[4,192,2304]{2,1,0:T(8,128)(2,1)} fusion(bf16[4,192,128]{2,1,0:T(8,128)(2,1)S(1)} %bitcast.148, bf16[128,768]{1,0:T(8,128)(2,1)S(1)} %slice.153, bf16[128,768]{1,0:T(8,128)(2,1)S(1)} %copy.50, bf16[128,768]{1,0:T(8,128)(2,1)S(1)} %copy-done.18), kind=kOutput, calls=%fused_computation.1 | convolution fusion | flops 456523776 | bytes 4325376 | tf_op jit(solution)/shard_map/dot_general | solution.py:71
  152.9 1.5 pad_maximum_fusion.refs_3_
  154.4 117.8 %shard_map.153 = (f32[192,2304]{1,0:T(8,128)}, f32[192,768]{1,0:T(8,128)}, f32[192,2304]{1,0:T(8,128)}, f32[320,768]{1,0:T(8,128)}) custom-call(bf16[4,192,2304]{2,1,0:T(8,128)(2,1)} %convolution_convert_fusion.1.refs_0_, bf16[4,192,768]{2,1,0:T(8,128)(2,1)} %convolution_convert_fusion.3.refs_1_, bf16[4,192,2304]{2,1,0:T(8,128)(2,1)} %bitcast.126, ...), custom_call_target="tpu_custom_call" | custom-call | tf_op jit(solution)/shard_map/pallas_call | solution.py:386
  272.2 1.4 fusion.73
  273.6 2.3 slice.101
  275.9 1.0 add_bitcast_fusion
  276.9 1.2 copy.59
  278.3 0.8 copy.60
  279.2 1.2 copy.61
  (128 shorter events, 7.5 us)
Async XLA Ops:
  1.7 89.3 %copy-start.25 = (f32[128]{0:T(128)}, f32[128]{0:T(128)S(1)}, u32[]{:S(2)}) copy-start(f32[128]{0:T(128)S(1)} %broadcast_multiply_fusion.5) | copy-start | bytes 1540
  2.8 0.6 copy-start.32
  3.4 87.6 %copy-start.27 = (f32[128]{0:T(128)}, f32[128]{0:T(128)S(1)}, u32[]{:S(2)}) copy-start(f32[128]{0:T(128)S(1)} %fusion.62) | copy-start | bytes 1540
  4.1 86.8 %copy-start.1 = (bf16[1,128,768]{2,1,0:T(8,128)(2,1)S(1)}, bf16[1,128,768]{2,1,0:T(8,128)(2,1)}, u32[]{:S(2)}) copy-start(bf16[1,128,768]{2,1,0:T(8,128)(2,1)} %param.9) | copy-start | bytes 589828
  91.0 2.8 copy-start.31
  94.7 8.6 %copy-start.20 = (f32[128,64]{0,1:T(8,128)}, f32[128,64]{0,1:T(8,128)S(1)}, u32[]{:S(2)}) copy-start(f32[128,64]{0,1:T(8,128)S(1)} %get-tuple-element.58) | copy-start | bytes 98308
  94.7 8.6 %copy-start.22 = (f32[128,64]{0,1:T(8,128)}, f32[128,64]{0,1:T(8,128)S(1)}, u32[]{:S(2)}) copy-start(f32[128,64]{0,1:T(8,128)S(1)} %get-tuple-element.75) | copy-start | bytes 98308
  95.3 6.4 %copy-start.14 = (bf16[4,320,768]{2,1,0:T(8,128)(2,1)S(1)}, bf16[4,320,768]{2,1,0:T(8,128)(2,1)}, u32[]{:S(2)}) copy-start(bf16[4,320,768]{2,1,0:T(8,128)(2,1)} %get-tuple-element.16) | copy-start | bytes 5898244
  95.5 7.9 %collective-permute-start = (bf16[64,1537]{1,0:T(8,128)(2,1)S(1)}, bf16[64,1537]{1,0:T(8,128)(2,1)S(1)}, u32[]{:S(2)}, u32[]{:S(2)}) collective-permute-start(bf16[64,1537]{1,0:T(8,128)(2,1)S(1)} %get-tuple-element.44), channel_id=1, source_target_pairs={{0,4},{4,8},{8,12},{12,16},{16,20},{20,24},{24,28},{1,5},{5,9},{9,... | collective-permute-start | bytes 590216 | tf_op jit(solution)/shard_map/ppermute | solution.py:31
  99.6 7.2 %collective-permute-start.1 = (bf16[64,1537]{1,0:T(8,128)(2,1)S(1)}, bf16[64,1537]{1,0:T(8,128)(2,1)S(1)}, u32[]{:S(2)}, u32[]{:S(2)}) collective-permute-start(bf16[64,1537]{1,0:T(8,128)(2,1)S(1)} %get-tuple-element.45), channel_id=1, source_target_pairs={{4,0},{8,4},{12,8},{16,12},{20,16},{24,20},{28,24},{5,1},{9,5},{13... | collective-permute-start | bytes 590216 | tf_op jit(solution)/shard_map/ppermute | solution.py:33
  107.3 1.4 copy-start.15
  107.5 1.2 copy-start.6
  108.7 1.3 copy-start.5
  108.7 2.4 copy-start
  111.0 1.5 copy-start.2
  111.0 1.5 copy-start.12
  114.4 9.1 %copy-start.8 = (bf16[128,1152]{1,0:T(8,128)(2,1)}, bf16[128,1152]{1,0:T(8,128)(2,1)S(1)}, u32[]{:S(2)}) copy-start(bf16[128,1152]{1,0:T(8,128)(2,1)S(1)} %get-tuple-element.37) | copy-start | bytes 884740
  116.1 2.0 copy-start.29
  116.7 1.4 copy-start.16
  129.2 1.0 copy-start.7
  129.2 1.0 copy-start.24
  134.7 4.8 %copy-start.13 = (bf16[1,128,768]{2,1,0:T(8,128)(2,1)S(1)}, bf16[1,128,768]{2,1,0:T(8,128)(2,1)}, u32[]{:S(2)}) copy-start(bf16[1,128,768]{2,1,0:T(8,128)(2,1)} %param.11) | copy-start | bytes 589828
  134.7 4.9 %copy-start.17 = (bf16[1152,128]{1,0:T(8,128)(2,1)S(1)}, bf16[1152,128]{1,0:T(8,128)(2,1)}, u32[]{:S(2)}) copy-start(bf16[1152,128]{1,0:T(8,128)(2,1)} %copy.52) | copy-start | bytes 884740
  134.8 6.6 %copy-start.3 = (bf16[4,288,768]{2,1,0:T(8,128)(2,1)S(1)}, bf16[4,288,768]{2,1,0:T(8,128)(2,1)}, u32[]{:S(2)}) copy-start(bf16[4,288,768]{2,1,0:T(8,128)(2,1)} %slice.95) | copy-start | bytes 5308420
  134.8 6.6 %copy-start.9 = (bf16[128,1152]{1,0:T(8,128)(2,1)S(1)}, bf16[128,1152]{1,0:T(8,128)(2,1)}, u32[]{:S(2)}) copy-start(bf16[128,1152]{1,0:T(8,128)(2,1)} %copy-done.8) | copy-start | bytes 884740
  134.9 7.7 %collective-permute-start.2 = (bf16[64,1536]{1,0:T(8,128)(2,1)S(1)}, bf16[64,1536]{1,0:T(8,128)(2,1)S(1)}, u32[]{:S(2)}, u32[]{:S(2)}) collective-permute-start(bf16[64,1536]{1,0:T(8,128)(2,1)S(1)} %get-tuple-element.42), channel_id=1, source_target_pairs={{0,4},{4,8},{8,12},{12,16},{16,20},{20,24},{24,28},{1,5},{5,9},{9,... | collective-permute-start | bytes 589832 | tf_op jit(solution)/shard_map/ppermute | solution.py:499
  136.9 7.7 %collective-permute-start.3 = (bf16[64,1536]{1,0:T(8,128)(2,1)S(1)}, bf16[64,1536]{1,0:T(8,128)(2,1)S(1)}, u32[]{:S(2)}, u32[]{:S(2)}) collective-permute-start(bf16[64,1536]{1,0:T(8,128)(2,1)S(1)} %get-tuple-element.43), channel_id=1, source_target_pairs={{4,0},{8,4},{12,8},{16,12},{20,16},{24,20},{28,24},{5,1},{9,5},{13... | collective-permute-start | bytes 589832 | tf_op jit(solution)/shard_map/ppermute | solution.py:504
  144.8 0.8 copy-start.21
  144.8 0.8 copy-start.23
  145.0 0.9 copy-start.18
  145.0 0.9 copy-start.26
  146.0 3.4 %copy-start.33 = (f32[128]{0:T(128)S(1)}, f32[128]{0:T(128)}, u32[]{:S(2)}) copy-start(f32[128]{0:T(128)} %copy-done.32) | copy-start | bytes 1540
  146.0 3.4 %copy-start.28 = (f32[128]{0:T(128)S(1)}, f32[128]{0:T(128)}, u32[]{:S(2)}) copy-start(f32[128]{0:T(128)} %copy-done.27) | copy-start | bytes 1540
  150.0 2.9 %copy-start.4 = (bf16[4,288,768]{2,1,0:T(8,128)(2,1)S(1)}, bf16[4,288,768]{2,1,0:T(8,128)(2,1)}, u32[]{:S(2)}) copy-start(bf16[4,288,768]{2,1,0:T(8,128)(2,1)} %convolution_convert_fusion.2) | copy-start | bytes 5308420
  272.2 3.7 %copy-start.30 = (f32[128]{0:T(128)S(1)}, f32[128]{0:T(128)}, u32[]{:S(2)}) copy-start(f32[128]{0:T(128)} %copy-done.29) | copy-start | bytes 1540
  273.6 3.2 %copy-start.11 = (f32[192,2304]{1,0:T(8,128)S(1)}, f32[192,2304]{1,0:T(8,128)}, u32[]{:S(2)}) copy-start(f32[192,2304]{1,0:T(8,128)} %get-tuple-element.87) | copy-start | bytes 5308420
  276.9 1.4 copy-start.19
  276.9 2.3 copy-start.10

commit v2 on v1

--- a/solution.py
+++ b/solution.py
@@ -137,6 +137,18 @@
         src_ref=src, dst_ref=dst, send_sem=send, recv_sem=recv,
         device_id=target, device_id_type=MESH,
     )
+
+
+def gather_order():
+    order = []
+    for k in range(4):
+        if k < 3:
+            order += [(0, k, w) for w in range(4)]
+        if k > 0:
+            order += [(2, k - 1, w) for w in range(4)]
+        if k < 3:
+            order += [(1, k, w) for w in range(4)]
+    return order
 
 
 def gather_kernel(*refs):
@@ -208,13 +220,9 @@
         copy.start()
         stage3[k, w] = copy
 
-    for t in range(len(events) + 4):
-        if t < len(events):
-            arrive(*events[t])
-        if 0 <= t - 2 < len(events):
-            pair(*events[t - 2])
-        if 0 <= t - 4 < len(events):
-            across(*events[t - 4])
+    acts = (arrive, pair, across)
+    for act, k, w in gather_order():
+        acts[act](k, w)
     for event in events:
         stage3[event].wait_recv()
     for copy in copies:
@@ -235,20 +243,41 @@
     return pl.pallas_call(
         gather_kernel,
         out_shape=[jax.ShapeDtypeStruct((4, 4 * r, 2 * c), jnp.bfloat16) for r, c in SHARES],
-        in_specs=[pl.BlockSpec(memory_space=pl.ANY)] * 4,
+        in_specs=[pl.BlockSpec(memory_space=pltpu.VMEM)] * 4,
         out_specs=[pl.BlockSpec(memory_space=pl.ANY)] * 4,
         scratch_shapes=[
             sem((4,)), sem((4, 2)), sem((4, 4)), sem((4, 3)), sem((4, 3)), sem((4, 3)),
             sem((4, 3, 2)), sem((4, 3, 2)), sem((4, 3)), sem((4, 3)),
         ],
-        compiler_params=pltpu.CompilerParams(collective_id=0, has_side_effects=True),
+        compiler_params=pltpu.CompilerParams(
+            collective_id=0, has_side_effects=True, vmem_limit_bytes=32 * 1024 * 1024
+        ),
     )(*shards)
 
 
+WIDE = 384
+CHUNKS = ((2, 0), (0, 0), (2, 384), (0, 384), (2, 768), (0, 768), (3, 0), (1, 0))
+
+
+def reduce_order():
+    ahead = 4
+    order = [("first", p) for p in range(ahead)]
+    for t in range(4 + 6):
+        for act, lag in (
+            ("finish", 6), ("across", 5), ("spread", 4), ("owner", 3), ("share", 2), ("pair", 0)
+        ):
+            if 0 <= t - lag < 4:
+                order.append((act, t - lag))
+        if t + ahead < 4:
+            order.append(("first", t + ahead))
+    return order
+
+
 def reduce_kernel(*refs):
-    ins, outs = refs[:4], refs[4:8]
-    cb, cs, b1s, s1s, b2s, s2s, bz, ag = (refs[8 + 4 * i : 12 + 4 * i] for i in range(8))
-    csem, sem1, sem2, zsem, asem = refs[40:]
+    xin, yin, gin, outs = refs[:4], refs[4:8], refs[8], refs[9:13]
+    xb, yb, gb = refs[13:17], refs[17:21], refs[21]
+    cs, b1s, s1s, b2s, s2s, bz, ag = (refs[22 + 8 * i : 30 + 8 * i] for i in range(7))
+    csem, sem1, sem2, zsem, asem = refs[78:]
     me, z, core, b1, b2 = place()
     quarter = b1 + 2 * b2
     greet(me, z)
@@ -266,134 +295,162 @@
         for copy in table[key]:
             copy.wait_recv()
 
-    def begin(w):
-        r, c = SHARES[w]
-        src = ins[w].at[:, :, cols(1 - core, c)]
-        go((0, w), src, cb[w], csem.at[w], {"seq": partner(me, 1)})
-
-    def core_sum(w):
-        r, c = SHARES[w]
-        take((0, w))
-
-        def body(i, carry):
-            part = (i // 4, pl.ds(pl.multiple_of((i % 4) * r, 16), r))
-            mine = ins[w][part[0], part[1], cols(core, c)].astype(f32)
-            cs[w][part[0], part[1], :] = (mine + cb[w][part[0], part[1], :].astype(f32)).astype(low)
+    twin = {"seq": partner(me, 1)}
+    lanes = cols(core, 128)
+    for w in (2, 0, 3, 1):
+        c = SHARES[w][1]
+        go(("x", w), xin[w], xb[w].at[:, lanes], csem.at[0, w], twin)
+        go(("x", w), yin[w].at[:, cols(1 - core, c)], yb[w].at[rows(core, 128)], csem.at[1, w], twin)
+    go("g", gin.at[:, :, cols(1 - core, WIDE)], gb, csem.at[2, 0], twin)
+    for w in (2, 0, 3, 1):
+        xb[w][:, lanes] = xin[w][...]
+        yb[w][rows(core, 128), :] = yin[w][:, cols(core, SHARES[w][1])]
+
+    def product(i):
+        w, start = CHUNKS[i]
+        height = 4 * SHARES[w][0]
+        if start == 0:
+            take(("x", w))
+
+        def body(o, carry):
+            left = xb[w][pl.ds(pl.multiple_of(o * height, 16), height), :]
+            right = yb[w][:, start : start + WIDE]
+            cs[i][o] = jnp.dot(left, right, preferred_element_type=f32).astype(low)
             return carry
 
-        lax.fori_loop(0, 16, body, 0)
+        lax.fori_loop(0, 4, body, 0)
+        if w == 3:
+            take("g")
+            mine = gin[:, :, cols(core, WIDE)].astype(f32)
+            cs[i][:, height - PAD :, :] = (mine + gb[...].astype(f32)).astype(low)
+
+    def first(i):
+        product(i)
+        w = CHUNKS[i][0]
+        r = SHARES[w][0]
         if BIT1_FIRST[w]:
-            src = cs[w].at[:, rows(2 * (1 - b2), r, 2), :]
-            go((1, w), src, b1s[w], sem1.at[w, 0], {"seq": partner(me, 4)})
+            src = cs[i].at[:, rows(2 * (1 - b2), r, 2), :]
+            go((1, i), src, b1s[i], sem1.at[i, 0], {"seq": partner(me, 4)})
         else:
             for j in range(2):
-                src = cs[w].at[:, rows(1 - b1 + 2 * j, r), :]
-                dst = b1s[w].at[:, pl.ds(j * r, r), :]
-                go((1, w), src, dst, sem1.at[w, j], {"seq": partner(me, 2)})
-
-    def pair_sum(w):
-        r, c = SHARES[w]
-        take((1, w))
-
-        def body(i, carry):
-            o, j = i // 2, i % 2
+                src = cs[i].at[:, rows(1 - b1 + 2 * j, r), :]
+                dst = b1s[i].at[:, pl.ds(j * r, r), :]
+                go((1, i), src, dst, sem1.at[i, j], {"seq": partner(me, 2)})
+
+    def pair(i):
+        w = CHUNKS[i][0]
+        r = SHARES[w][0]
+        take((1, i))
+
+        def body(t, carry):
+            o, j = t // 2, t % 2
             block = 2 * b2 + j if BIT1_FIRST[w] else b1 + 2 * j
             there = pl.ds(pl.multiple_of(j * r, 16), r)
-            mine = cs[w][o, rows(block, r), :].astype(f32)
-            s1s[w][o, there, :] = (mine + b1s[w][o, there, :].astype(f32)).astype(low)
+            mine = cs[i][o, rows(block, r), :].astype(f32)
+            s1s[i][o, there, :] = (mine + b1s[i][o, there, :].astype(f32)).astype(low)
             return carry
 
         lax.fori_loop(0, 8, body, 0)
         bit, step = (b1, 2) if BIT1_FIRST[w] else (b2, 4)
-        src = s1s[w].at[:, rows(1 - bit, r), :]
-        go((2, w), src, b2s[w], sem2.at[w], {"seq": partner(me, step)})
-
-    def share_sum(w):
-        r, c = SHARES[w]
-        take((2, w))
+        src = s1s[i].at[:, rows(1 - bit, r), :]
+        go((2, i), src, b2s[i], sem2.at[i], {"seq": partner(me, step)})
+
+    def share(i):
+        w = CHUNKS[i][0]
+        r = SHARES[w][0]
+        take((2, i))
         bit = b1 if BIT1_FIRST[w] else b2
 
         def body(o, carry):
-            mine = s1s[w][o, rows(bit, r), :].astype(f32)
-            s2s[w][o] = (mine + b2s[w][o].astype(f32)).astype(low)
+            mine = s1s[i][o, rows(bit, r), :].astype(f32)
+            s2s[i][o] = (mine + b2s[i][o].astype(f32)).astype(low)
             return carry
 
         lax.fori_loop(0, 4, body, 0)
         for d in (2, 1, 3):
             to = (z + d) % 4
-            go((3, w), s2s[w].at[to], bz[w].at[d - 1], zsem.at[w, d - 1], {"fsdp": to})
-
-    def owner_sum(w):
-        r, c = SHARES[w]
-        take((3, w))
-        total = s2s[w][z].astype(f32)
+            go((3, i), s2s[i].at[to], bz[i].at[d - 1], zsem.at[i, d - 1], {"fsdp": to})
+
+    def owner(i):
+        w = CHUNKS[i][0]
+        r = SHARES[w][0]
+        take((3, i))
+        total = s2s[i][z].astype(f32)
         for d in range(3):
-            total = total + bz[w][d].astype(f32)
-        ag[w][rows(quarter, r), cols(core, c)] = total.astype(low)
-        block = ag[w].at[rows(quarter, r), cols(core, c)]
+            total = total + bz[i][d].astype(f32)
+        ag[i][core, rows(quarter, r), :] = total.astype(low)
+        block = ag[i].at[core, rows(quarter, r), :]
         step = 2 if BIT1_FIRST[w] else 4
-        go((4, w), block, block, asem.at[w, 0], {"seq": partner(me, step)})
-
-    def spread(w):
-        r, c = SHARES[w]
-        take((4, w))
-        half = cols(core, c)
+        go((4, i), block, block, asem.at[i, 0], {"seq": partner(me, step)})
+
+    def spread(i):
+        w = CHUNKS[i][0]
+        r = SHARES[w][0]
+        take((4, i))
         if BIT1_FIRST[w]:
-            block = ag[w].at[rows(2 * b2, r, 2), half]
-            go((5, w), block, block, asem.at[w, 1], {"seq": partner(me, 4)})
+            block = ag[i].at[core, rows(2 * b2, r, 2), :]
+            go((5, i), block, block, asem.at[i, 1], {"seq": partner(me, 4)})
         else:
             for j in range(2):
-                block = ag[w].at[rows(b1 + 2 * j, r), half]
-                go((5, w), block, block, asem.at[w, 1 + j], {"seq": partner(me, 2)})
-
-    def across(w):
+                block = ag[i].at[core, rows(b1 + 2 * j, r), :]
+                go((5, i), block, block, asem.at[i, 1 + j], {"seq": partner(me, 2)})
+
+    def across(i):
+        take((5, i))
+        block = ag[i].at[core]
+        go((6, i), block, block, asem.at[i, 3], twin)
+
+    def finish(i):
+        w, start = CHUNKS[i]
         r, c = SHARES[w]
-        take((5, w))
-        block = ag[w].at[:, cols(core, c)]
-        go((6, w), block, block, asem.at[w, 3], {"seq": partner(me, 1)})
-
-    def finish(w):
-        r, c = SHARES[w]
-        take((6, w))
-
-        def body(i, carry):
-            part = pl.ds(pl.multiple_of(i * r, 16), r)
-            outs[w][part, :] = ag[w][part, :].astype(f32)
+        take((6, i))
+
+        def body(t, carry):
+            part = pl.ds(pl.multiple_of(t * r, 16), r)
+            for half in range(2):
+                at = half * c + start
+                outs[w][part, at : at + WIDE] = ag[i][half, part, :].astype(f32)
             return carry
 
         lax.fori_loop(0, 4, body, 0)
 
-    order = (2, 0, 3, 1)
-    steps = (core_sum, pair_sum, share_sum, owner_sum, spread, across, finish)
-    for w in order:
-        begin(w)
-    for t in range(len(steps) + 3):
-        for i, w in enumerate(order):
-            if 0 <= t - i < len(steps):
-                steps[t - i](w)
+    acts = {
+        "first": first, "pair": pair, "share": share, "owner": owner,
+        "spread": spread, "across": across, "finish": finish,
+    }
+    for act, p in reduce_order():
+        for i in (2 * p, 2 * p + 1):
+            acts[act](i)
     for copy in sent:
         copy.wait_send()
 
 
-def reduce_grads(parts):
+def reduce_grads(lefts, rights, gain_rows):
     sem = pltpu.SemaphoreType.DMA
-    vmem = lambda shape: pltpu.VMEM(shape, jnp.bfloat16)
-    half = [vmem((4, 4 * r, c)) for r, c in SHARES]
-    two = [vmem((4, 2 * r, c)) for r, c in SHARES]
-    one = [vmem((4, r, c)) for r, c in SHARES]
-    slots = [vmem((3, r, c)) for r, c in SHARES]
-    whole = [vmem((4 * r, 2 * c)) for r, c in SHARES]
+    vmem = lambda *shape: pltpu.VMEM(shape, jnp.bfloat16)
+    heights = [SHARES[w][0] for w, start in CHUNKS]
+    count = len(CHUNKS)
     return pl.pallas_call(
         reduce_kernel,
         out_shape=[jax.ShapeDtypeStruct((4 * r, 2 * c), jnp.float32) for r, c in SHARES],
-        in_specs=[pl.BlockSpec(memory_space=pltpu.VMEM)] * 4,
+        in_specs=[pl.BlockSpec(memory_space=pltpu.VMEM)] * 9,
         out_specs=[pl.BlockSpec(memory_space=pltpu.VMEM)] * 4,
-        scratch_shapes=half + half + two + two + one + one + slots + whole
-        + [sem((4, 2)), sem((4, 2, 2)), sem((4, 2)), sem((4, 3, 2)), sem((4, 4, 2))],
+        scratch_shapes=[vmem(16 * r, 256) for r, c in SHARES]
+        + [vmem(256, c) for r, c in SHARES]
+        + [vmem(4, PAD, WIDE)]
+        + [vmem(4, 4 * r, WIDE) for r in heights]
+        + [vmem(4, 2 * r, WIDE) for r in heights] * 2
+        + [vmem(4, r, WIDE) for r in heights] * 2
+        + [vmem(3, r, WIDE) for r in heights]
+        + [vmem(2, 4 * r, WIDE) for r in heights]
+        + [
+            sem((3, 4, 2)), sem((count, 2, 2)), sem((count, 2)), sem((count, 3, 2)),
+            sem((count, 4, 2)),
+        ],
         compiler_params=pltpu.CompilerParams(
             collective_id=1, has_side_effects=True, vmem_limit_bytes=56 * 1024 * 1024
         ),
-    )(*parts)
+    )(*lefts, *rights, gain_rows)
 
 
 def on_device(inputs, positions, cotangent, w_qkv, w_out, w_in, w_down, gain_attn, gain_mlp):
@@ -522,17 +579,13 @@
             [grad_gain_first.reshape(4, 1, held), grad_gain_second.reshape(4, 1, held)], axis=2
         )
         gain_rows = jnp.pad(gain_rows, ((0, 0), (0, PAD - 1), (0, D - 2 * held)))
-        grad_packed = jnp.concatenate(
-            [grad_down_local.reshape(4, owned_rows, D), gain_rows], axis=1
-        )
-        parts = (
-            grad_qkv_local.reshape(4, held, 3 * D),
-            grad_out_local.reshape(4, held, D),
-            grad_in_local.reshape(4, held, 2 * FF),
-            grad_packed,
+        hidden_rows = jnp.pad(
+            hidden_low.T.reshape(4, owned_rows, count), ((0, 0), (0, PAD), (0, 0))
         )
         grad_qkv, grad_out, grad_in, packed = reduce_grads(
-            [part.astype(jnp.bfloat16) for part in parts]
+            [normed_low.T, attended_low.T, normed_mlp_low.T, hidden_rows.reshape(-1, count)],
+            [grad_mixed, grad_branch, grad_gate_up, grad_result],
+            gain_rows.astype(jnp.bfloat16),
         )
         return (
             result[None].astype(jnp.bfloat16),

time: 281 us -> 244 us (0.87)
  Pallas kernels: 202 us -> 132 us
  local copies, waits for them, and re-layouts: 17.8 us -> 47.9 us
  other arithmetic: 15.7 us -> 31 us
  matrix products: 27.4 us -> 16.9 us
    pallas_call x1, Pallas kernels: 84 us -> 48.5 us  [gather_weights(): pl.pallas_call(gather_kernel, out_shape=[jax.ShapeDtypeStruct((4, 4 * r,...]
    pallas_call x1, Pallas kernels: 118 us -> 83.2 us  [reduce_grads(): pl.pallas_call(reduce_kernel, out_shape=[jax.ShapeDtypeStruct((4 * r, 2 *...]
    dot_general x4 -> x0, matrix products: 9.14 us -> none  [matmul_left(): lax.dot_general(left, right, (((0,), (0,)), ((), ())), preferred_element_...]
    unnamed x71 -> x117, local copies, waits for them, and re-layouts: 7.29 us -> 16 us
    mul x3, local copies, waits for them, and re-layouts: 0.35 us -> 4.6 us  [rotary(): return values * cosine + turned * sine]
    ppermute x1, waiting for transfers between devices: 3.34 us -> 0.01 us  [with_halo(): lax.ppermute(head, axis, [((i + 1) % count, i) for i in range(ends)])]
  transfers between devices with their start and end apart: 4 -> 4, of which waited for: 2 -> 1; matrix products, arithmetic and copies ran while one was open for 2% -> 4% of each run, Pallas kernels for 0% -> 0%
where the time goes in v2:
time: 244 us; the launch traced here: 243 us
  Pallas kernels  132 us (54%)
  local copies, waits for them, and re-layouts  47.9 us (20%)
  other arithmetic  31 us (13%)
  matrix products  16.9 us (7%)
  starting transfers between devices  11 us (5%)
  waiting for transfers between devices  2.96 us (1%)
    pallas_call x1, Pallas kernels, reduce_grads(): pl.pallas_call(reduce_kernel, out_shape=[jax.ShapeDtypeStruct((4 * r, 2 *...  83.2 us
    pallas_call x1, Pallas kernels, gather_weights(): pl.pallas_call(gather_kernel, out_shape=[jax.ShapeDtypeStruct((4, 4 * r,...  48.5 us
    unnamed x117, local copies, waits for them, and re-layouts  16 us
    dot_general x4, matrix products, matmul_right(): lax.dot_general(left, right, (((1,), (1,)), ((), ())), preferred_element_...  6.58 us
  transfers between devices with their start and end apart: 4, of which 1 were waited for; matrix products, arithmetic and copies ran while one was open for 4% of the time, Pallas kernels for 0%

profile of v2, /device:TPU:1, one launch (start us, length us, event | category | flops | bytes accessed | tf_op | source)
XLA Modules:
  0.0 242.9 jit_solution(5511137395850741813)
XLA Ops:
  1.2 1.0 convert_reduce_fusion
  2.2 1.1 fusion.28
  5.2 1.0 fusion.23.refs_3_
  6.3 1.2 copy-done.7
  7.5 1.0 copy-done.8
  8.4 48.5 %shard_map.152 = (bf16[4,192,2304]{2,1,0:T(8,128)(2,1)S(1)}, bf16[4,192,768]{2,1,0:T(8,128)(2,1)S(1)}, bf16[4,192,2304]{2,1,0:T(8,128)(2,1)S(1)}, bf16[4,320,768]{2,1,0:T(8,128)(2,1)S(1)}) custom-call(bf16[192,2304]{1,0:T(8,128)(2,1)S(1)} %copy-done.6, bf16[192,768]{1,0:T(8,128)(2,1)S(1)} %copy-done.8, bf16[192,2304]{1,0:T(8,128)(2,1)S(1)} %copy-done.7, ...), custom_call_target="tpu_custom_call" | custom-call | tf_op jit(solution)/shard_map/pallas_call | solution.py:243
  57.0 1.0 copy-done
  58.0 1.7 copy-done.2
  59.7 1.3 copy-done.4
  61.2 2.8 %fusion.43 = f32[128,2304]{1,0:T(8,128)S(1)} fusion(bf16[768,2304]{1,0:T(8,128)(2,1)} %bitcast.118, bf16[1,128,768]{2,1,0:T(8,128)(2,1)} %param.9, f32[768]{0:T(1024)S(1)} %reshape.330, f32[128]{0:T(128)} %fusion.57, f32[128]{0:T(128)S(1)} %broadcast_multiply_fusion.5), kind=kOutput, calls=%fused_computation.96 | convolution fusion | flops 453476352 | bytes 4919296 | tf_op jit(solution)/shard_map/dot_general | solution.py:476
  66.4 1.4 copy.42
  70.6 1.9 copy.39
  72.5 1.9 copy.40
  74.4 1.1 slice_negate_fusion.3
  75.5 1.5 maximum_multiply_fusion
  77.0 1.9 copy.41
  78.9 2.3 fusion.66
  83.5 3.0 %collective-permute-start = (bf16[64,1537]{1,0:T(8,128)(2,1)}, bf16[64,1537]{1,0:T(8,128)(2,1)}, u32[]{:S(2)}, u32[]{:S(2)}) collective-permute-start(bf16[64,1537]{1,0:T(8,128)(2,1)} %get-tuple-element.44), channel_id=1, source_target_pairs={{0,4},{4,8},{8,12},{12,16},{16,20},{20,24},{24,28},{1,5},{5,9},{9,... | collective-permute-start | bytes 590216 | tf_op jit(solution)/shard_map/ppermute | solution.py:31
  86.6 2.1 collective-permute-start.1
  89.3 1.3 slice.95
  90.7 1.9 copy.44
  92.6 1.1 slice_negate_fusion.2
  93.7 1.8 fusion.37
  96.5 1.1 pad_maximum_fusion.1
  98.4 1.9 copy.43
  100.3 1.8 pad_maximum_fusion.4
  102.1 1.9 copy.45
  104.8 1.6 fusion.72
  110.4 1.5 fusion.50
  112.0 1.0 multiply_add_fusion
  113.1 1.9 multiply_reduce_fusion.1
  117.8 1.8 multiply_reduce_fusion
  121.7 1.9 multiply_convert_fusion
  126.9 3.7 %collective-permute-start.2 = (bf16[64,1536]{1,0:T(8,128)(2,1)S(1)}, bf16[64,1536]{1,0:T(8,128)(2,1)S(1)}, u32[]{:S(2)}, u32[]{:S(2)}) collective-permute-start(bf16[64,1536]{1,0:T(8,128)(2,1)S(1)} %get-tuple-element.42), channel_id=1, source_target_pairs={{0,4},{4,8},{8,12},{12,16},{16,20},{20,24},{24,28},{1,5},{5,9},{9,... | collective-permute-start | bytes 589832 | tf_op jit(solution)/shard_map/ppermute | solution.py:556
  130.6 2.1 collective-permute-start.3
  133.5 1.1 fusion.4
  134.6 3.0 %collective-permute-done.3 = bf16[64,1536]{1,0:T(8,128)(2,1)S(1)} collective-permute-done((bf16[64,1536]{1,0:T(8,128)(2,1)S(1)}, bf16[64,1536]{1,0:T(8,128)(2,1)S(1)}, u32[]{:S(2)}, u32[]{:S(2)}) %collective-permute-start.3) | collective-permute-done | bytes 196640 | tf_op jit(solution)/shard_map/ppermute | solution.py:561
  139.2 2.1 copy.49
  141.2 1.0 broadcast_multiply_fusion.1
  142.3 1.7 add_convert_fusion.1
  144.0 1.7 copy.51
  145.8 2.7 %fusion.29 = (f32[128]{0:T(128)S(1)}, f32[128,768]{1,0:T(8,128)S(1)}) fusion(bf16[1,128,768]{2,1,0:T(8,128)(2,1)} %param.9, f32[768]{0:T(1024)S(1)} %reshape.330, f32[128]{0:T(128)S(1)} %copy-done.48, bf16[768,2304]{1,0:T(8,128)(2,1)S(1)} %bitcast.119, bf16[128,768]{1,0:T(8,128)(2,1)} %slice.153, bf16[128,768]{1,0:T(8,128)(2,1)} %copy.51, ...), kind=kOutput, calls=%fused_computation.66 | convolution fusion | flops 455245696 | bytes 4722688 | tf_op jit(solution)/shard_map/dot_general | solution.py:77
  151.5 83.2 %shard_map.153 = (f32[192,2304]{1,0:T(8,128)}, f32[192,768]{1,0:T(8,128)}, f32[192,2304]{1,0:T(8,128)}, f32[320,768]{1,0:T(8,128)}) custom-call(bf16[768,128]{1,0:T(8,128)(2,1)} %copy.55.refs_0_, bf16[768,128]{1,0:T(8,128)(2,1)} %bitcast.142, bf16[768,128]{1,0:T(8,128)(2,1)} %copy.56.refs_2_, bf16[1280,128]{1,0:T(8,128)(2,1)} %bitcast.137, ...), custom_call_target="tpu_custom_call" | custom-call | tf_op jit(solution)/shard_map/pallas_call | solution.py:433
  234.7 1.4 fusion.67
  236.1 2.3 slice.101
  238.5 1.0 add_bitcast_fusion
  239.4 1.2 copy.61
  241.7 1.2 copy.63
  (173 shorter events, 31.5 us)
Async XLA Ops:
  0.6 5.6 %copy-start.6 = (bf16[192,2304]{1,0:T(8,128)(2,1)S(1)}, bf16[192,2304]{1,0:T(8,128)(2,1)}, u32[]{:S(2)}) copy-start(bf16[192,2304]{1,0:T(8,128)(2,1)} %refs_0_.1) | copy-start | bytes 2654212
  2.2 59.0 %copy-start.47 = (f32[128]{0:T(128)}, f32[128]{0:T(128)S(1)}, u32[]{:S(2)}) copy-start(f32[128]{0:T(128)S(1)} %broadcast_multiply_fusion.5) | copy-start | bytes 1540
  58.0 1.7 copy-start.2
  59.7 1.3 copy-start.4
  61.2 4.7 %copy-start.54 = (s32[1,128]{1,0:T(1,128)S(1)}, s32[1,128]{1,0:T(1,128)}, u32[]{:S(2)}) copy-start(s32[1,128]{1,0:T(1,128)} %param.10) | copy-start | bytes 1540
  78.9 3.0 %copy-start.22 = (bf16[128,768]{1,0:T(8,128)(2,1)S(1)}, bf16[128,768]{1,0:T(8,128)(2,1)}, u32[]{:S(2)}) copy-start(bf16[128,768]{1,0:T(8,128)(2,1)} %slice.154) | copy-start | bytes 589828
  78.9 10.3 %copy-start.5 = (bf16[4,320,768]{2,1,0:T(8,128)(2,1)S(1)}, bf16[4,320,768]{2,1,0:T(8,128)(2,1)}, u32[]{:S(2)}) copy-start(bf16[4,320,768]{2,1,0:T(8,128)(2,1)} %copy-done.4) | copy-start | bytes 5898244
  83.5 11.9 %collective-permute-start = (bf16[64,1537]{1,0:T(8,128)(2,1)}, bf16[64,1537]{1,0:T(8,128)(2,1)}, u32[]{:S(2)}, u32[]{:S(2)}) collective-permute-start(bf16[64,1537]{1,0:T(8,128)(2,1)} %get-tuple-element.44), channel_id=1, source_target_pairs={{0,4},{4,8},{8,12},{12,16},{16,20},{20,24},{24,28},{1,5},{5,9},{9,... | collective-permute-start | bytes 590216 | tf_op jit(solution)/shard_map/ppermute | solution.py:31
  86.6 8.9 %collective-permute-start.1 = (bf16[64,1537]{1,0:T(8,128)(2,1)}, bf16[64,1537]{1,0:T(8,128)(2,1)}, u32[]{:S(2)}, u32[]{:S(2)}) collective-permute-start(bf16[64,1537]{1,0:T(8,128)(2,1)} %get-tuple-element.45), channel_id=1, source_target_pairs={{4,0},{8,4},{12,8},{16,12},{20,16},{24,20},{28,24},{5,1},{9,5},{13... | collective-permute-start | bytes 590216 | tf_op jit(solution)/shard_map/ppermute | solution.py:33
  92.6 2.9 %copy-start.21 = (bf16[128,768]{1,0:T(8,128)(2,1)S(1)}, bf16[128,768]{1,0:T(8,128)(2,1)}, u32[]{:S(2)}) copy-start(bf16[128,768]{1,0:T(8,128)(2,1)} %copy-done.20) | copy-start | bytes 589828
  92.6 2.9 %copy-start.23 = (bf16[128,768]{1,0:T(8,128)(2,1)S(1)}, bf16[128,768]{1,0:T(8,128)(2,1)}, u32[]{:S(2)}) copy-start(bf16[128,768]{1,0:T(8,128)(2,1)} %slice.154) | copy-start | bytes 589828
  92.6 2.9 %copy-start.38 = (bf16[128,1]{1,0:T(8,128)(2,1)S(1)}, bf16[128,1]{1,0:T(8,128)(2,1)}, u32[]{:S(2)}) copy-start(bf16[128,1]{1,0:T(8,128)(2,1)} %copy.42) | copy-start | bytes 772
  104.8 2.2 copy-start.34
  106.4 11.4 %copy-start.9 = (f32[12,128,256]{2,1,0:T(8,128)}, f32[12,128,256]{2,1,0:T(8,128)S(1)}, u32[]{:S(2)}) copy-start(f32[12,128,256]{2,1,0:T(8,128)S(1)} %get-tuple-element.65) | copy-start | bytes 4718596
  107.0 1.3 copy-start.1
  107.0 1.3 copy-start.13
  107.7 2.0 copy-start.42
  108.7 6.3 %copy-start.11 = (f32[128,768]{1,0:T(8,128)}, f32[128,768]{1,0:T(8,128)S(1)}, u32[]{:S(2)}) copy-start(f32[128,768]{1,0:T(8,128)S(1)} %get-tuple-element.67) | copy-start | bytes 1179652
  108.9 1.5 copy-start.16
  108.9 1.5 copy-start.32
  113.1 1.9 copy-start.19
  115.3 2.5 %copy-start.52 = (f32[128]{0:T(128)}, f32[128]{0:T(128)S(1)}, u32[]{:S(2)}) copy-start(f32[128]{0:T(128)S(1)} %negate_multiply_fusion.2) | copy-start | bytes 1540
  117.8 1.9 copy-start.27
  117.8 2.7 %copy-start.49 = (bf16[768]{0:T(1024)(128)(2,1)S(1)}, bf16[768]{0:T(1024)(128)(2,1)}, u32[]{:S(2)}) copy-start(bf16[768]{0:T(1024)(128)(2,1)} %get-tuple-element.26) | copy-start | bytes 4612
  119.7 2.1 copy-start.10
  121.7 1.9 copy-start.28
  126.7 6.0 %copy-start.37 = (bf16[1152,128]{1,0:T(8,128)(2,1)S(1)}, bf16[1152,128]{1,0:T(8,128)(2,1)}, u32[]{:S(2)}) copy-start(bf16[1152,128]{1,0:T(8,128)(2,1)} %copy.52) | copy-start | bytes 884740
  126.7 6.8 %copy-start.12 = (f32[128,768]{1,0:T(8,128)S(1)}, f32[128,768]{1,0:T(8,128)}, u32[]{:S(2)}) copy-start(f32[128,768]{1,0:T(8,128)} %copy-done.11) | copy-start | bytes 1179652
  126.7 6.8 %copy-start.17 = (bf16[4,288,768]{2,1,0:T(8,128)(2,1)S(1)}, bf16[4,288,768]{2,1,0:T(8,128)(2,1)}, u32[]{:S(2)}) copy-start(bf16[4,288,768]{2,1,0:T(8,128)(2,1)} %slice.95) | copy-start | bytes 5308420
  126.9 7.8 %collective-permute-start.2 = (bf16[64,1536]{1,0:T(8,128)(2,1)S(1)}, bf16[64,1536]{1,0:T(8,128)(2,1)S(1)}, u32[]{:S(2)}, u32[]{:S(2)}) collective-permute-start(bf16[64,1536]{1,0:T(8,128)(2,1)S(1)} %get-tuple-element.42), channel_id=1, source_target_pairs={{0,4},{4,8},{8,12},{12,16},{16,20},{20,24},{24,28},{1,5},{5,9},{9,... | collective-permute-start | bytes 589832 | tf_op jit(solution)/shard_map/ppermute | solution.py:556
  130.6 7.0 %collective-permute-start.3 = (bf16[64,1536]{1,0:T(8,128)(2,1)S(1)}, bf16[64,1536]{1,0:T(8,128)(2,1)S(1)}, u32[]{:S(2)}, u32[]{:S(2)}) collective-permute-start(bf16[64,1536]{1,0:T(8,128)(2,1)S(1)} %get-tuple-element.43), channel_id=1, source_target_pairs={{4,0},{8,4},{12,8},{16,12},{20,16},{24,20},{28,24},{5,1},{9,5},{13... | collective-permute-start | bytes 589832 | tf_op jit(solution)/shard_map/ppermute | solution.py:561
  139.2 6.6 %copy-start.3 = (bf16[4,192,2304]{2,1,0:T(8,128)(2,1)S(1)}, bf16[4,192,2304]{2,1,0:T(8,128)(2,1)}, u32[]{:S(2)}) copy-start(bf16[4,192,2304]{2,1,0:T(8,128)(2,1)} %copy-done.2) | copy-start | bytes 10616836
  141.2 4.6 %copy-start.48 = (f32[128]{0:T(128)S(1)}, f32[128]{0:T(128)}, u32[]{:S(2)}) copy-start(f32[128]{0:T(128)} %copy-done.47) | copy-start | bytes 1540
  145.8 2.7 %copy-start.39 = (bf16[128,768]{1,0:T(8,128)(2,1)S(1)}, bf16[128,768]{1,0:T(8,128)(2,1)}, u32[]{:S(2)}) copy-start(bf16[128,768]{1,0:T(8,128)(2,1)} %copy.50) | copy-start | bytes 589828
  145.8 2.7 %copy-start.40 = (bf16[128,768]{1,0:T(8,128)(2,1)S(1)}, bf16[128,768]{1,0:T(8,128)(2,1)}, u32[]{:S(2)}) copy-start(bf16[128,768]{1,0:T(8,128)(2,1)} %slice.153) | copy-start | bytes 589828
  145.8 2.7 %copy-start.41 = (bf16[128,768]{1,0:T(8,128)(2,1)S(1)}, bf16[128,768]{1,0:T(8,128)(2,1)}, u32[]{:S(2)}) copy-start(bf16[128,768]{1,0:T(8,128)(2,1)} %copy.51) | copy-start | bytes 589828
  145.8 3.7 %copy-start.56 = (f32[128]{0:T(128)S(1)}, f32[128]{0:T(128)}, u32[]{:S(2)}) copy-start(f32[128]{0:T(128)} %copy-done.55) | copy-start | bytes 1540
  145.8 3.7 %copy-start.14 = (bf16[1,128,768]{2,1,0:T(8,128)(2,1)S(1)}, bf16[1,128,768]{2,1,0:T(8,128)(2,1)}, u32[]{:S(2)}) copy-start(bf16[1,128,768]{2,1,0:T(8,128)(2,1)} %param.9) | copy-start | bytes 589828
  145.8 3.7 %copy-start.50 = (f32[128]{0:T(128)S(1)}, f32[128]{0:T(128)}, u32[]{:S(2)}) copy-start(f32[128]{0:T(128)} %fusion.57) | copy-start | bytes 1540
  151.5 86.9 %copy-start.15 = (bf16[1,128,768]{2,1,0:T(8,128)(2,1)S(1)}, bf16[1,128,768]{2,1,0:T(8,128)(2,1)}, u32[]{:S(2)}) copy-start(bf16[1,128,768]{2,1,0:T(8,128)(2,1)} %param.9) | copy-start | bytes 589828
  151.5 86.9 %copy-start.25 = (f32[128,768]{1,0:T(8,128)S(1)}, f32[128,768]{1,0:T(8,128)}, u32[]{:S(2)}) copy-start(f32[128,768]{1,0:T(8,128)} %copy-done.24) | copy-start | bytes 1179652
  151.5 86.9 %copy-start.33 = (bf16[1,128,768]{2,1,0:T(8,128)(2,1)S(1)}, bf16[1,128,768]{2,1,0:T(8,128)(2,1)}, u32[]{:S(2)}) copy-start(bf16[1,128,768]{2,1,0:T(8,128)(2,1)} %param.11) | copy-start | bytes 589828
  151.5 86.9 %copy-start.36 = (f32[128,768]{1,0:T(8,128)S(1)}, f32[128,768]{1,0:T(8,128)}, u32[]{:S(2)}) copy-start(f32[128,768]{1,0:T(8,128)} %copy-done.35) | copy-start | bytes 1179652
  151.5 86.9 %copy-start.51 = (f32[128]{0:T(128)S(1)}, f32[128]{0:T(128)}, u32[]{:S(2)}) copy-start(f32[128]{0:T(128)} %fusion.57) | copy-start | bytes 1540
  151.5 86.9 %copy-start.53 = (f32[128]{0:T(128)S(1)}, f32[128]{0:T(128)}, u32[]{:S(2)}) copy-start(f32[128]{0:T(128)} %copy-done.52) | copy-start | bytes 1540
  236.1 3.3 %copy-start.30 = (f32[192,2304]{1,0:T(8,128)S(1)}, f32[192,2304]{1,0:T(8,128)}, u32[]{:S(2)}) copy-start(f32[192,2304]{1,0:T(8,128)} %get-tuple-element.88) | copy-start | bytes 5308420
  239.4 1.4 copy-start.43
  239.4 2.3 copy-start.29
  (13 other events, 11.5 us)

commit v3 on v2

--- a/solution.py
+++ b/solution.py
@@ -20,51 +20,10 @@
 masked_score = -1e30
 
 
-def with_halo(cells, sides, width):
-    for axis, dim in sides:
-        count = lax.axis_size(axis)
-        ends = count - 1
-        head = lax.slice_in_dim(cells, 0, width, axis=dim)
-        tail = lax.slice_in_dim(cells, cells.shape[dim] - width, cells.shape[dim], axis=dim)
-        cells = jnp.concatenate(
-            [
-                lax.ppermute(tail, axis, [(i, (i + 1) % count) for i in range(ends)]),
-                cells,
-                lax.ppermute(head, axis, [((i + 1) % count, i) for i in range(ends)]),
-            ],
-            axis=dim,
-        )
-    return cells
-
-
 def layer_norm(values, gain):
     center = values - jnp.mean(values, axis=-1, keepdims=True)
     spread = jnp.mean(center * center, axis=-1, keepdims=True)
     return center * lax.rsqrt(spread + eps) * gain
-
-
-def rotary(values, token_pos):
-    half = values.shape[-1] // 2
-    ladder = jnp.arange(half).astype(jnp.float32) * (2.0 / values.shape[-1])
-    freqs = rope_base ** (-ladder)
-    angles = token_pos.astype(jnp.float32)[:, None] * freqs[None, :]
-    cosine = jnp.concatenate([jnp.cos(angles), jnp.cos(angles)], axis=-1)[:, None, :]
-    sine = jnp.concatenate([jnp.sin(angles), jnp.sin(angles)], axis=-1)[:, None, :]
-    turned = jnp.concatenate([-values[..., half:], values[..., :half]], axis=-1)
-    return values * cosine + turned * sine
-
-
-def window_mask(token_pos, wide_flags, count):
-    offsets = jnp.arange(count + 2 * HALF_WINDOW, dtype=jnp.int32) - HALF_WINDOW
-    offset = offsets[None, :] - jnp.arange(count, dtype=jnp.int32)[:, None]
-    flag_float = wide_flags.astype(jnp.float32)[None, :]
-    earlier = token_pos[:, None] >= -offset
-    later = flag_float - 1.0 >= offset.astype(jnp.float32)
-    return (
-        (jnp.abs(offset) <= HALF_WINDOW)
-        & (flag_float > 0.5)
-        & jnp.where(offset < 0, earlier, later)
-    )
 
 
 def matmul_left(left, right):
@@ -274,10 +233,10 @@
 
 
 def reduce_kernel(*refs):
-    xin, yin, gin, outs = refs[:4], refs[4:8], refs[8], refs[9:13]
-    xb, yb, gb = refs[13:17], refs[17:21], refs[21]
-    cs, b1s, s1s, b2s, s2s, bz, ag = (refs[22 + 8 * i : 30 + 8 * i] for i in range(7))
-    csem, sem1, sem2, zsem, asem = refs[78:]
+    xin, yin, gin, outs = refs[:4], refs[4:8], refs[8], refs[9:14]
+    xb, yb, gb = refs[14:18], refs[18:22], refs[22]
+    cs, b1s, s1s, b2s, s2s, bz, ag = (refs[23 + 8 * i : 31 + 8 * i] for i in range(7))
+    csem, sem1, sem2, zsem, asem = refs[79:]
     me, z, core, b1, b2 = place()
     quarter = b1 + 2 * b2
     greet(me, z)
@@ -412,7 +371,16 @@
                 outs[w][part, at : at + WIDE] = ag[i][half, part, :].astype(f32)
             return carry
 
-        lax.fori_loop(0, 4, body, 0)
+        if w < 3:
+            lax.fori_loop(0, 4, body, 0)
+            return
+        lax.fori_loop(0, 3, body, 0)
+        for half in range(2):
+            at = half * c
+            for to, begin, end in ((3, 3 * r, 4 * r - PAD), (4, 4 * r - PAD, 4 * r)):
+                low_row = begin if to == 3 else 0
+                part = ag[i][half, begin:end, :].astype(f32)
+                outs[to][low_row : low_row + end - begin, at : at + WIDE] = part
 
     acts = {
         "first": first, "pair": pair, "share": share, "owner": owner,
@@ -430,11 +398,13 @@
     vmem = lambda *shape: pltpu.VMEM(shape, jnp.bfloat16)
     heights = [SHARES[w][0] for w, start in CHUNKS]
     count = len(CHUNKS)
+    shapes = [(4 * r, 2 * c) for r, c in SHARES]
+    shapes = shapes[:3] + [(shapes[3][0] - PAD, shapes[3][1]), (PAD, shapes[3][1])]
     return pl.pallas_call(
         reduce_kernel,
-        out_shape=[jax.ShapeDtypeStruct((4 * r, 2 * c), jnp.float32) for r, c in SHARES],
+        out_shape=[jax.ShapeDtypeStruct(shape, jnp.float32) for shape in shapes],
         in_specs=[pl.BlockSpec(memory_space=pltpu.VMEM)] * 9,
-        out_specs=[pl.BlockSpec(memory_space=pltpu.VMEM)] * 4,
+        out_specs=[pl.BlockSpec(memory_space=pltpu.VMEM)] * 5,
         scratch_shapes=[vmem(16 * r, 256) for r, c in SHARES]
         + [vmem(256, c) for r, c in SHARES]
         + [vmem(4, PAD, WIDE)]
@@ -453,6 +423,141 @@
     )(*lefts, *rights, gain_rows)
 
 
+def swap_halves(values):
+    lane = lax.broadcasted_iota(jnp.int32, values.shape, 1)
+    return jnp.where(lane % 64 < 32, pltpu.roll(values, 96, 1), pltpu.roll(values, 32, 1))
+
+
+def turn_kernel(mixed, cosine, sine, flags, q_out, kv_out):
+    cos, sin = cosine[...], sine[...]
+    for g in range(2 * D // 128):
+        u = mixed[:, 128 * g : 128 * g + 128]
+        turned = (u * cos + swap_halves(u) * sin).astype(jnp.bfloat16)
+        if g < D // 128:
+            q_out[:, 128 * g : 128 * g + 128] = turned
+        else:
+            at = 128 * g - D
+            kv_out[:, at : at + 128] = turned
+    kv_out[:, D : 2 * D] = mixed[:, 2 * D :].astype(jnp.bfloat16)
+    kv_out[:, 2 * D :] = jnp.broadcast_to(flags[...], (flags.shape[0], 128)).astype(jnp.bfloat16)
+
+
+def widen(above, own, below, start, size):
+    return jnp.concatenate([ref[:, start : start + size] for ref in (above, own, below)], axis=0)
+
+
+def visible(above, own, below, pos):
+    flag = widen(above, own, below, 2 * D, 128).astype(jnp.float32).T
+    shape = flag.shape
+    offset = (
+        lax.broadcasted_iota(jnp.int32, shape, 1)
+        - HALF_WINDOW
+        - lax.broadcasted_iota(jnp.int32, shape, 0)
+    ).astype(jnp.float32)
+    place_of = jnp.broadcast_to(pos[...], shape)
+    earlier = (offset >= 0.0) | (place_of >= -offset)
+    later = (offset < 0.0) | (flag - 1.0 >= offset)
+    return (jnp.abs(offset) <= HALF_WINDOW) & (flag > 0.5) & earlier & later
+
+
+def dot_rows(left, right):
+    return lax.dot_general(
+        left, right, (((1,), (1,)), ((), ())), preferred_element_type=jnp.float32
+    )
+
+
+def attend_kernel(q, above, own, below, pos, o_out, lse_out):
+    allowed = visible(above, own, below, pos)
+    scale = HEAD_DIM ** (-0.5)
+    lane = lax.broadcasted_iota(jnp.int32, lse_out.shape, 1)
+    kept = jnp.zeros(lse_out.shape, jnp.float32)
+    for g in range(HEADS // 2):
+        keys = widen(above, own, below, 128 * g, 128)
+        values = widen(above, own, below, D + 128 * g, 128)
+        queries = q[:, 128 * g : 128 * g + 128]
+        outs = []
+        for j in range(2):
+            part = slice(64 * j, 64 * j + 64)
+            scores = dot_rows(queries[:, part], keys[:, part]) * scale
+            scores = jnp.where(allowed, scores, masked_score)
+            top = jnp.max(scores, axis=-1, keepdims=True)
+            expo = jnp.exp(scores - top)
+            total = jnp.sum(expo, axis=-1, keepdims=True)
+            kept = jnp.where(lane == 2 * g + j, top + jnp.log(total), kept)
+            probs = (expo / total).astype(jnp.bfloat16)
+            outs.append(jnp.dot(probs, values[:, part], preferred_element_type=jnp.float32))
+        o_out[:, 128 * g : 128 * g + 128] = jnp.concatenate(outs, axis=1).astype(jnp.bfloat16)
+    lse_out[...] = kept
+
+
+def attend_back_kernel(
+    q, above, own, below, pos, grad, lse, cosine, sine, dq_out, up_out, mid_out, down_out
+):
+    allowed = visible(above, own, below, pos)
+    scale = HEAD_DIM ** (-0.5)
+    cos, sin = cosine[...], sine[...]
+    low = jnp.bfloat16
+    count = q.shape[0]
+    edge = count + HALF_WINDOW
+    for g in range(HEADS // 2):
+        at = slice(128 * g, 128 * g + 128)
+        keys = widen(above, own, below, 128 * g, 128)
+        values = widen(above, own, below, D + 128 * g, 128)
+        queries, grads = q[:, at], grad[:, at]
+        dqs, dks, dvs = [], [], []
+        for j in range(2):
+            part = slice(64 * j, 64 * j + 64)
+            head = 2 * g + j
+            scores = dot_rows(queries[:, part], keys[:, part]) * scale
+            scores = jnp.where(allowed, scores, masked_score)
+            probs = jnp.exp(scores - lse[:, head : head + 1])
+            probs_low = probs.astype(low)
+            dp = dot_rows(grads[:, part], values[:, part])
+            row = jnp.sum(probs * dp, axis=-1, keepdims=True)
+            ds = (probs * (dp - row)).astype(low)
+            dqs.append(jnp.dot(ds, keys[:, part], preferred_element_type=jnp.float32) * scale)
+            dks.append(matmul_left(ds, queries[:, part]) * scale)
+            dvs.append(matmul_left(probs_low, grads[:, part]))
+        dq = jnp.concatenate(dqs, axis=1)
+        dq_out[:, at] = (dq * cos - swap_halves(dq) * sin).astype(low)
+        for start, pieces in ((0, dks), (D, dvs)):
+            wide = jnp.concatenate(pieces, axis=1)
+            to = slice(start + 128 * g, start + 128 * g + 128)
+            up_out[:, to] = wide[:HALF_WINDOW].astype(low)
+            mid_out[:, to] = wide[HALF_WINDOW:edge]
+            down_out[:, to] = wide[edge:].astype(low)
+
+
+def join_kernel(dq, mid, above, below, cosine, sine, out):
+    cos, sin = cosine[...], sine[...]
+    out[:, :D] = dq[...]
+    for g in range(2 * D // 128):
+        at = slice(128 * g, 128 * g + 128)
+        back = jnp.concatenate([above[:, at], below[:, at]], axis=0).astype(jnp.float32)
+        total = mid[:, at] + back
+        if g < D // 128:
+            total = total * cos - swap_halves(total) * sin
+        out[:, D + 128 * g : D + 128 * g + 128] = total.astype(jnp.bfloat16)
+
+
+def local_call(kernel, shapes, *operands):
+    vmem = pl.BlockSpec(memory_space=pltpu.VMEM)
+    return pl.pallas_call(
+        kernel,
+        out_shape=[jax.ShapeDtypeStruct(shape, kind) for shape, kind in shapes],
+        in_specs=[vmem] * len(operands),
+        out_specs=[vmem] * len(shapes),
+        compiler_params=pltpu.CompilerParams(vmem_limit_bytes=32 * 1024 * 1024),
+    )(*operands)
+
+
+def neighbours(up, down):
+    lanes = lax.axis_size("seq")
+    above = lax.ppermute(down, "seq", [(i, i + 1) for i in range(lanes - 1)])
+    below = lax.ppermute(up, "seq", [(i + 1, i) for i in range(lanes - 1)])
+    return above, below
+
+
 def on_device(inputs, positions, cotangent, w_qkv, w_out, w_in, w_down, gain_attn, gain_mlp):
     gains = jnp.concatenate([gain_attn, gain_mlp])
     gains = jnp.pad(gains[None], ((0, PAD - 1), (0, D - gains.shape[0])))
@@ -466,47 +571,30 @@
     held = gain_attn.shape[0]
     gain_first = full_packed[:, owned_rows, :held].reshape(D).astype(jnp.float32)
     gain_second = full_packed[:, owned_rows, held : 2 * held].reshape(D).astype(jnp.float32)
-    scale = HEAD_DIM ** (-0.5)
     tokens = inputs[0].astype(jnp.float32)
     token_pos = positions[0]
     count = tokens.shape[0]
-    extent = count + 2 * HALF_WINDOW
     normed, norm_back = jax.vjp(layer_norm, tokens, gain_first)
     normed_low = normed.astype(jnp.bfloat16)
     mixed = jnp.dot(normed_low, full_qkv, preferred_element_type=jnp.float32)
-    query_raw = mixed[:, :D].reshape(count, HEADS, HEAD_DIM)
-    key_raw = mixed[:, D : 2 * D].reshape(count, HEADS, HEAD_DIM)
-    value_low = mixed[:, 2 * D :].astype(jnp.bfloat16)
-    query_rot, query_back = jax.vjp(lambda piece: rotary(piece, token_pos), query_raw)
-    key_rot, key_back = jax.vjp(lambda piece: rotary(piece, token_pos), key_raw)
-    query_low = query_rot.astype(jnp.bfloat16)
-    flags = (jnp.minimum(token_pos, 127) + 1).astype(jnp.bfloat16)
-    key_value = jnp.concatenate(
-        [key_rot.reshape(count, D).astype(jnp.bfloat16), value_low, flags[:, None]], axis=1
-    )
-    wide_kv = with_halo(key_value, (("seq", 0),), HALF_WINDOW)
-    wide_flags = wide_kv[:, 2 * D]
-    keys_wide = wide_kv[:, :D].reshape(extent, HEADS, HEAD_DIM)
-    values_wide = wide_kv[:, D : 2 * D].reshape(extent, HEADS, HEAD_DIM)
-    allowed = window_mask(token_pos, wide_flags, count)
-
-    def score_table():
-        raw = (
-            jnp.einsum("qhd,khd->hqk", query_low, keys_wide, preferred_element_type=jnp.float32)
-            * scale
-        )
-        return jnp.where(allowed[None], raw, masked_score)
-
-    scores = score_table()
-    top = jnp.max(scores, axis=-1, keepdims=True)
-    expo = jnp.exp(scores - top)
-    totals = jnp.sum(expo, axis=-1, keepdims=True)
-    logsum = top + jnp.log(totals)
-    probs_low = (expo / totals).astype(jnp.bfloat16)
-    attended = jnp.einsum(
-        "hqk,khd->qhd", probs_low, values_wide, preferred_element_type=jnp.float32
-    )
-    attended_low = attended.reshape(count, D).astype(jnp.bfloat16)
+    half = HEAD_DIM // 2
+    ladder = jnp.arange(half).astype(jnp.float32) * (2.0 / HEAD_DIM)
+    angles = token_pos.astype(jnp.float32)[:, None] * (rope_base ** (-ladder))[None, :]
+    cosine, sine = jnp.cos(angles), jnp.sin(angles)
+    cosine = jnp.concatenate([cosine] * 4, axis=1)
+    sine = jnp.concatenate([-sine, sine] * 2, axis=1)
+    flags = (jnp.minimum(token_pos, 127) + 1).astype(jnp.float32)[:, None]
+    pos = token_pos.astype(jnp.float32)[:, None]
+    low = jnp.bfloat16
+    query_low, key_value = local_call(
+        turn_kernel, [((count, D), low), ((count, 2 * D + 128), low)], mixed, cosine, sine, flags
+    )
+    above, below = neighbours(key_value[:HALF_WINDOW], key_value[count - HALF_WINDOW :])
+    attended_low, logsum = local_call(
+        attend_kernel,
+        [((count, D), low), ((count, 128), jnp.float32)],
+        query_low, above, key_value, below, pos,
+    )
     middle = tokens + jnp.dot(attended_low, full_out, preferred_element_type=jnp.float32)
     normed_mlp, mlp_norm_back = jax.vjp(layer_norm, middle, gain_second)
     normed_mlp_low = normed_mlp.astype(jnp.bfloat16)
@@ -528,52 +616,26 @@
     grad_middle = grad_result.astype(jnp.float32) + grad_middle_norm
     grad_branch = grad_middle.astype(jnp.bfloat16)
     grad_out_local = matmul_left(attended_low, grad_branch)
-    grad_attended = (
-        matmul_right(grad_branch, full_out).reshape(count, HEADS, HEAD_DIM).astype(jnp.bfloat16)
-    )
-    probs = jnp.exp(score_table() - logsum)
-    probs_low = probs.astype(jnp.bfloat16)
-    grad_probs = jnp.einsum(
-        "qhd,khd->hqk", grad_attended, values_wide, preferred_element_type=jnp.float32
-    )
-    row_dot = jnp.sum(probs * grad_probs, axis=-1, keepdims=True)
-    grad_scores = (probs * (grad_probs - row_dot)).astype(jnp.bfloat16)
-    grad_query = (
-        jnp.einsum("hqk,khd->qhd", grad_scores, keys_wide, preferred_element_type=jnp.float32)
-        * scale
-    )
-    grad_keys_wide = (
-        jnp.einsum("hqk,qhd->khd", grad_scores, query_low, preferred_element_type=jnp.float32)
-        * scale
-    )
-    grad_values_wide = jnp.einsum(
-        "hqk,qhd->khd", probs_low, grad_attended, preferred_element_type=jnp.float32
-    )
-    grad_wide = jnp.concatenate(
-        [grad_keys_wide.reshape(extent, D), grad_values_wide.reshape(extent, D)], axis=1
-    )
-    lanes = lax.axis_size("seq")
-    above = lax.ppermute(
-        grad_wide[extent - HALF_WINDOW :].astype(jnp.bfloat16),
-        "seq",
-        [(i, i + 1) for i in range(lanes - 1)],
-    )
-    below = lax.ppermute(
-        grad_wide[:HALF_WINDOW].astype(jnp.bfloat16),
-        "seq",
-        [(i + 1, i) for i in range(lanes - 1)],
-    )
-    returned = jnp.concatenate([above, below], axis=0).astype(jnp.float32)
-    grad_own = grad_wide[HALF_WINDOW : HALF_WINDOW + count] + returned
-    grad_key = key_back(grad_own[:, :D].reshape(count, HEADS, HEAD_DIM))[0]
-    grad_q = query_back(grad_query)[0]
-    grad_mixed = jnp.concatenate(
-        [grad_q.reshape(count, D), grad_key.reshape(count, D), grad_own[:, D:]], axis=1
-    ).astype(jnp.bfloat16)
+    grad_attended = matmul_right(grad_branch, full_out).astype(low)
+    grad_query, up, own, down = local_call(
+        attend_back_kernel,
+        [
+            ((count, D), low),
+            ((HALF_WINDOW, 2 * D), low),
+            ((count, 2 * D), jnp.float32),
+            ((HALF_WINDOW, 2 * D), low),
+        ],
+        query_low, above, key_value, below, pos, grad_attended, logsum, cosine, sine,
+    )
+    back_above, back_below = neighbours(up, down)
+    (grad_mixed,) = local_call(
+        join_kernel, [((count, 3 * D), low)], grad_query, own, back_above, back_below, cosine, sine
+    )
     grad_qkv_local = matmul_left(normed_low, grad_mixed)
     grad_normed = matmul_right(grad_mixed, full_qkv)
     grad_tokens_norm, grad_gain_first = norm_back(grad_normed)
     grad_tokens = grad_middle + grad_tokens_norm
+    lanes = lax.axis_size("seq")
     if lanes == 8:
         gain_rows = jnp.concatenate(
             [grad_gain_first.reshape(4, 1, held), grad_gain_second.reshape(4, 1, held)], axis=2
@@ -582,7 +644,7 @@
         hidden_rows = jnp.pad(
             hidden_low.T.reshape(4, owned_rows, count), ((0, 0), (0, PAD), (0, 0))
         )
-        grad_qkv, grad_out, grad_in, packed = reduce_grads(
+        grad_qkv, grad_out, grad_in, grad_down, gain_sums = reduce_grads(
             [normed_low.T, attended_low.T, normed_mlp_low.T, hidden_rows.reshape(-1, count)],
             [grad_mixed, grad_branch, grad_gate_up, grad_result],
             gain_rows.astype(jnp.bfloat16),
@@ -593,9 +655,9 @@
             grad_qkv,
             grad_out,
             grad_in,
-            packed[:owned_rows],
-            packed[owned_rows, :held],
-            packed[owned_rows, held : 2 * held],
+            grad_down,
+            gain_sums[0, :held],
+            gain_sums[0, held : 2 * held],
         )
     owned = (
         lax.psum_scatter(

time: 244 us -> 217 us (0.89)
  other arithmetic: 31 us -> 11.8 us
  local copies, waits for them, and re-layouts: 47.9 us -> 32.1 us
  Pallas kernels: 132 us -> 143 us
  matrix products: 16.9 us -> 13.4 us
    slice x14 -> x2, local copies, waits for them, and re-layouts: 17.9 us -> 2.2 us  [the longest x1 1.41 us: on_device(): gain_sums[0, held:2 * held]]
    pallas_call x1 -> x5, Pallas kernels: 83.2 us -> 94.3 us  [the longest x1 84.3 us: reduce_grads(): pl.pallas_call(reduce_kernel, out_shape=[jax.ShapeDtypeStruct(shape, jnp....]
    dot_general x6 -> x0, matrix products: 5.27 us -> none  [the longest x1 1.83 us: on_device(): jnp.einsum('qhd,khd->hqk', grad_attended, values_wide, preferred_element_...]
    mul x3 -> x0, local copies, waits for them, and re-layouts: 4.6 us -> none  [rotary(): return values * cosine + turned * sine]
    slice x2 -> x0, other arithmetic: 4.12 us -> none  [the longest x1 2.32 us: on_device(): query_raw = mixed[:, :D].reshape(count, HEADS, HEAD_DIM)]
    mul x3 -> x0, other arithmetic: 3.21 us -> none  [rotary(): return values * cosine + turned * sine]
    reshape x4 -> x0, local copies, waits for them, and re-layouts: 3.11 us -> none  [the longest x1 1.74 us: on_device(): grad_key.reshape(count, D)]
    convert_element_type x3 -> x1, other arithmetic: 4.2 us -> 1.26 us  [on_device(): token_pos.astype(jnp.float32)[:, None] * (rope_base ** (-ladder))[None, :]]
  transfers between devices with their start and end apart: 4 -> 4, of which waited for: 1 -> 2; matrix products, arithmetic and copies ran while one was open for 4% -> 3% of each run, Pallas kernels for 0% -> 0%
where the time goes in v3:
time: 217 us; the launch traced here: 216 us
  Pallas kernels  143 us (66%)
  local copies, waits for them, and re-layouts  32.1 us (15%)
  matrix products  13.4 us (6%)
  starting transfers between devices  12.3 us (6%)
  other arithmetic  11.8 us (5%)
  waiting for transfers between devices  2.22 us (1%)
    pallas_call x1, Pallas kernels, reduce_grads(): pl.pallas_call(reduce_kernel, out_shape=[jax.ShapeDtypeStruct(shape, jnp....  84.3 us
    pallas_call x1, Pallas kernels, gather_weights(): pl.pallas_call(gather_kernel, out_shape=[jax.ShapeDtypeStruct((4, 4 * r,...  48.5 us
    unnamed x96, local copies, waits for them, and re-layouts  18.8 us
    pallas_call x4, Pallas kernels, local_call(): pl.pallas_call(kernel, out_shape=[jax.ShapeDtypeStruct(shape, kind) for s...  10.1 us
    ppermute x2, starting transfers between devices, neighbours(): above = lax.ppermute(down, 'seq', [(i, i + 1) for i in range(lanes - 1)])  8.17 us
    dot_general x4, matrix products, matmul_right(): lax.dot_general(left, right, (((1,), (1,)), ((), ())), preferred_element_...  5.37 us
  transfers between devices with their start and end apart: 4, of which 2 were waited for; matrix products, arithmetic and copies ran while one was open for 3% of the time, Pallas kernels for 0%

profile of v3, /device:TPU:1, one launch (start us, length us, event | category | flops | bytes accessed | tf_op | source)
XLA Modules:
  0.0 215.9 jit_solution(9745570900676201818)
XLA Ops:
  1.2 1.0 convert_reduce_fusion
  2.2 1.1 fusion.20
  3.9 0.7 pad_maximum_fusion.2
  4.6 1.3 convert_bitcast_fusion.2
  6.6 1.0 fusion.15.refs_3_
  7.7 1.2 copy-done.14
  8.8 1.2 copy-done.15
  10.0 1.0 copy-done.22
  11.0 48.5 %shard_map.152 = (bf16[4,192,2304]{2,1,0:T(8,128)(2,1)S(1)}, bf16[4,192,768]{2,1,0:T(8,128)(2,1)S(1)}, bf16[4,192,2304]{2,1,0:T(8,128)(2,1)S(1)}, bf16[4,320,768]{2,1,0:T(8,128)(2,1)S(1)}) custom-call(bf16[192,2304]{1,0:T(8,128)(2,1)S(1)} %copy-done.14, bf16[192,768]{1,0:T(8,128)(2,1)S(1)} %copy-done.22, bf16[192,2304]{1,0:T(8,128)(2,1)S(1)} %copy-done.15, ...), custom_call_target="tpu_custom_call" | custom-call | tf_op jit(solution)/shard_map/pallas_call | solution.py:202
  59.5 1.7 copy-done
  61.2 1.0 copy-done.3
  62.3 1.3 copy-done.8
  63.7 1.0 fusion.40
  64.9 2.9 %fusion.33.mixed = f32[128,2304]{1,0:T(8,128)S(1)} fusion(bf16[768,2304]{1,0:T(8,128)(2,1)} %bitcast.85, bf16[1,128,768]{2,1,0:T(8,128)(2,1)} %param.9, f32[768]{0:T(1024)S(1)} %reshape.184, f32[128]{0:T(128)} %fusion.41, f32[128]{0:T(128)S(1)} %broadcast_multiply_fusion.1), kind=kOutput, calls=%fused_computation.64 | convolution fusion | flops 453476352 | bytes 4919296 | tf_op jit(solution)/shard_map/dot_general | solution.py:579
  68.3 0.8 fusion.49
  69.1 2.0 collective-permute-start.1
  71.1 3.8 %collective-permute-start = (bf16[64,1664]{1,0:T(8,128)(2,1)}, bf16[64,1664]{1,0:T(8,128)(2,1)}, u32[]{:S(2)}, u32[]{:S(2)}) collective-permute-start(bf16[64,1664]{1,0:T(8,128)(2,1)} %get-tuple-element.55), channel_id=1, source_target_pairs={{0,4},{4,8},{8,12},{12,16},{16,20},{20,24},{24,28},{1,5},{5,9},{9,... | collective-permute-start | bytes 638984 | tf_op jit(solution)/shard_map/ppermute | solution.py:556
  74.9 1.3 slice.33
  77.1 0.7 collective-permute-done.above
  77.8 1.0 copy-done.6
  78.8 0.9 copy-done.18
  79.7 0.8 copy-done.20
  80.6 3.5 %shard_map.154 = (bf16[128,768]{1,0:T(8,128)(2,1)S(1)}, f32[128,128]{1,0:T(8,128)S(1)}) custom-call(bf16[128,768]{1,0:T(8,128)(2,1)S(1)} %copy-done.18, bf16[64,1664]{1,0:T(8,128)(2,1)} %collective-permute-done.above, bf16[128,1664]{1,0:T(8,128)(2,1)S(1)} %copy-done.6, bf16[64,1664]{1,0:T(8,128)(2,1)} %collective-permute-done.1.below, f32[128,1]{1,0:T(8,128)S(1)} %copy-done.20), custom_call_target="tpu_custom_call" | custom-call | tf_op jit(solution)/shard_map/pallas_call | solution.py:545
  85.3 1.8 copy.40
  87.1 1.8 fusion.51
  89.8 0.8 copy-done.29
  90.6 1.6 fusion.39
  92.2 1.0 multiply_add_fusion
  93.3 1.9 multiply_reduce_fusion
  95.2 0.9 fusion.47
  96.2 1.9 copy.41
  98.9 1.8 copy.45.refs_2_
  100.7 5.8 %shard_map.155 = (bf16[128,768]{1,0:T(8,128)(2,1)S(1)}, bf16[64,1536]{1,0:T(8,128)(2,1)S(1)}, f32[128,1536]{1,0:T(8,128)S(1)}, bf16[64,1536]{1,0:T(8,128)(2,1)S(1)}) custom-call(bf16[128,768]{1,0:T(8,128)(2,1)S(1)} %copy-done.19, bf16[64,1664]{1,0:T(8,128)(2,1)} %collective-permute-done.above, bf16[128,1664]{1,0:T(8,128)(2,1)S(1)} %copy-done.7, ...), custom_call_target="tpu_custom_call" | custom-call | tf_op jit(solution)/shard_map/pallas_call | solution.py:545
  106.5 4.4 %collective-permute-start.2 = (bf16[64,1536]{1,0:T(8,128)(2,1)S(1)}, bf16[64,1536]{1,0:T(8,128)(2,1)S(1)}, u32[]{:S(2)}, u32[]{:S(2)}) collective-permute-start(bf16[64,1536]{1,0:T(8,128)(2,1)S(1)} %get-tuple-element.35), channel_id=1, source_target_pairs={{0,4},{4,8},{8,12},{12,16},{16,20},{20,24},{24,28},{1,5},{5,9},{9,... | collective-permute-start | bytes 589832 | tf_op jit(solution)/shard_map/ppermute | solution.py:556
  110.9 2.1 collective-permute-start.3
  113.1 1.7 pad.22
  114.8 2.7 %fusion.1 = bf16[1,128,768]{2,1,0:T(8,128)(2,1)} fusion(f32[128,768]{1,0:T(8,128)S(1)} %copy-done.27, bf16[128,1152]{1,0:T(8,128)(2,1)S(1)} %copy-done.31, bf16[1152,768]{1,0:T(8,128)(2,1)} %bitcast.89), kind=kOutput, calls=%fused_computation.6 | convolution fusion | flops 226689024 | bytes 2654208 | tf_op jit(solution)/shard_map/dot_general | solution.py:608
  117.5 1.5 collective-permute-done.3.below
  119.4 1.4 fusion.21
  121.1 1.0 add_bitcast_fusion
  122.2 0.8 copy.44.refs_0_
  123.0 0.8 fusion.31.refs_8_
  123.8 84.3 %shard_map.157 = (f32[192,2304]{1,0:T(8,128)}, f32[192,768]{1,0:T(8,128)}, f32[192,2304]{1,0:T(8,128)}, f32[288,768]{1,0:T(8,128)}, f32[32,768]{1,0:T(8,128)}) custom-call(bf16[768,128]{1,0:T(8,128)(2,1)} %copy.44.refs_0_, bf16[768,128]{1,0:T(8,128)(2,1)} %bitcast.95, bf16[768,128]{1,0:T(8,128)(2,1)} %copy.45.refs_2_, bf16[1280,128]{1,0:T(8,128)(2,1)} %bitcast.93, ...), custom_call_target="tpu_custom_call" | custom-call | tf_op jit(solution)/shard_map/pallas_call | solution.py:403
  208.0 1.4 fusion.50
  209.4 2.9 %copy.51 = f32[192,2304]{1,0:T(8,128)} copy(f32[192,2304]{1,0:T(8,128)} %get-tuple-element.84) | data formatting | bytes 3538944
  212.4 0.8 copy.52
  213.2 1.2 copy.53
  215.0 0.9 copy.54
  (110 shorter events, 7.9 us)
Async XLA Ops:
  3.3 1.3 copy-start.44
  7.7 1.2 copy-start.14
  8.8 1.2 copy-start.15
  10.0 1.0 copy-start.22
  59.5 1.7 copy-start
  61.2 1.0 copy-start.3
  62.3 1.3 copy-start.8
  64.9 2.9 %copy-start.10 = (f32[128,128]{1,0:T(8,128)}, f32[128,128]{1,0:T(8,128)S(1)}, u32[]{:S(2)}) copy-start(f32[128,128]{1,0:T(8,128)S(1)} %get-tuple-element.72.cosine) | copy-start | bytes 196612
  64.9 2.9 %copy-start.12 = (f32[128,128]{1,0:T(8,128)}, f32[128,128]{1,0:T(8,128)S(1)}, u32[]{:S(2)}) copy-start(f32[128,128]{1,0:T(8,128)S(1)} %get-tuple-element.73.sine) | copy-start | bytes 196612
  64.9 2.9 %copy-start.23 = (f32[128,1]{1,0:T(8,128)S(1)}, f32[128,1]{1,0:T(8,128)}, u32[]{:S(2)}) copy-start(f32[128,1]{1,0:T(8,128)} %copy.36.flags) | copy-start | bytes 1540
  67.8 7.1 %copy-start.9 = (bf16[4,320,768]{2,1,0:T(8,128)(2,1)S(1)}, bf16[4,320,768]{2,1,0:T(8,128)(2,1)}, u32[]{:S(2)}) copy-start(bf16[4,320,768]{2,1,0:T(8,128)(2,1)} %copy-done.8) | copy-start | bytes 5898244
  68.3 7.9 %copy-start.5 = (bf16[128,1664]{1,0:T(8,128)(2,1)}, bf16[128,1664]{1,0:T(8,128)(2,1)S(1)}, u32[]{:S(2)}) copy-start(bf16[128,1664]{1,0:T(8,128)(2,1)S(1)} %get-tuple-element.28.own) | copy-start | bytes 1277956
  68.3 7.9 %copy-start.17 = (bf16[128,768]{1,0:T(8,128)(2,1)}, bf16[128,768]{1,0:T(8,128)(2,1)S(1)}, u32[]{:S(2)}) copy-start(bf16[128,768]{1,0:T(8,128)(2,1)S(1)} %get-tuple-element.27.q) | copy-start | bytes 589828
  69.1 7.9 %collective-permute-start.1 = (bf16[64,1664]{1,0:T(8,128)(2,1)}, bf16[64,1664]{1,0:T(8,128)(2,1)}, u32[]{:S(2)}, u32[]{:S(2)}) collective-permute-start(bf16[64,1664]{1,0:T(8,128)(2,1)} %get-tuple-element.54), channel_id=1, source_target_pairs={{4,0},{8,4},{12,8},{16,12},{20,16},{24,20},{28,24},{5,1},{9,5},{13... | collective-permute-start | bytes 638984 | tf_op jit(solution)/shard_map/ppermute | solution.py:557
  71.1 5.1 %copy-start.41 = (f32[128,1]{0,1:T(1,128)S(1)}, f32[128,1]{0,1:T(1,128)}, u32[]{:S(2)}) copy-start(f32[128,1]{0,1:T(1,128)} %get-tuple-element.63) | copy-start | bytes 1540
  71.1 6.7 %collective-permute-start = (bf16[64,1664]{1,0:T(8,128)(2,1)}, bf16[64,1664]{1,0:T(8,128)(2,1)}, u32[]{:S(2)}, u32[]{:S(2)}) collective-permute-start(bf16[64,1664]{1,0:T(8,128)(2,1)} %get-tuple-element.55), channel_id=1, source_target_pairs={{0,4},{4,8},{8,12},{12,16},{16,20},{20,24},{24,28},{1,5},{5,9},{9,... | collective-permute-start | bytes 638984 | tf_op jit(solution)/shard_map/ppermute | solution.py:556
  77.8 1.0 copy-start.6
  78.8 0.9 copy-start.18
  79.7 0.8 copy-start.20
  88.9 6.3 %copy-start.26 = (f32[128,768]{1,0:T(8,128)}, f32[128,768]{1,0:T(8,128)S(1)}, u32[]{:S(2)}) copy-start(f32[128,768]{1,0:T(8,128)S(1)} %get-tuple-element.67) | copy-start | bytes 1179652
  89.1 1.5 copy-start.29
  89.1 1.5 copy-start.34
  93.2 1.9 copy-start.30
  95.2 2.9 %copy-start.39 = (bf16[768]{0:T(1024)(128)(2,1)S(1)}, bf16[768]{0:T(1024)(128)(2,1)}, u32[]{:S(2)}) copy-start(bf16[768]{0:T(1024)(128)(2,1)} %get-tuple-element.44) | copy-start | bytes 4612
  95.2 3.0 %copy-start.35 = (bf16[1,128,768]{2,1,0:T(8,128)(2,1)S(1)}, bf16[1,128,768]{2,1,0:T(8,128)(2,1)}, u32[]{:S(2)}) copy-start(bf16[1,128,768]{2,1,0:T(8,128)(2,1)} %param.11) | copy-start | bytes 589828
  95.2 3.1 %copy-start.4 = (bf16[4,192,768]{2,1,0:T(8,128)(2,1)S(1)}, bf16[4,192,768]{2,1,0:T(8,128)(2,1)}, u32[]{:S(2)}) copy-start(bf16[4,192,768]{2,1,0:T(8,128)(2,1)} %copy-done.3) | copy-start | bytes 3538948
  96.1 4.5 %copy-start.7 = (bf16[128,1664]{1,0:T(8,128)(2,1)S(1)}, bf16[128,1664]{1,0:T(8,128)(2,1)}, u32[]{:S(2)}) copy-start(bf16[128,1664]{1,0:T(8,128)(2,1)} %copy-done.5) | copy-start | bytes 1277956
  96.1 4.5 %copy-start.11 = (f32[128,128]{1,0:T(8,128)S(1)}, f32[128,128]{1,0:T(8,128)}, u32[]{:S(2)}) copy-start(f32[128,128]{1,0:T(8,128)} %copy-done.10) | copy-start | bytes 196612
  96.1 4.5 %copy-start.13 = (f32[128,128]{1,0:T(8,128)S(1)}, f32[128,128]{1,0:T(8,128)}, u32[]{:S(2)}) copy-start(f32[128,128]{1,0:T(8,128)} %copy-done.12) | copy-start | bytes 196612
  96.1 4.5 %copy-start.19 = (bf16[128,768]{1,0:T(8,128)(2,1)S(1)}, bf16[128,768]{1,0:T(8,128)(2,1)}, u32[]{:S(2)}) copy-start(bf16[128,768]{1,0:T(8,128)(2,1)} %copy-done.17) | copy-start | bytes 589828
  96.1 4.5 %copy-start.21 = (f32[128,1]{1,0:T(8,128)S(1)}, f32[128,1]{1,0:T(8,128)}, u32[]{:S(2)}) copy-start(f32[128,1]{1,0:T(8,128)} %copy.37.pos) | copy-start | bytes 1540
  96.1 4.5 %copy-start.25 = (f32[128,128]{1,0:T(8,128)S(1)}, f32[128,128]{1,0:T(8,128)}, u32[]{:S(2)}) copy-start(f32[128,128]{1,0:T(8,128)} %copy-done.24) | copy-start | bytes 196612
  96.1 10.4 %copy-start.42 = (f32[128]{0:T(128)}, f32[128]{0:T(128)S(1)}, u32[]{:S(2)}) copy-start(f32[128]{0:T(128)S(1)} %negate_multiply_fusion.2) | copy-start | bytes 1540
  98.3 16.5 %copy-start.33 = (bf16[128,768]{1,0:T(8,128)(2,1)}, bf16[128,768]{1,0:T(8,128)(2,1)S(1)}, u32[]{:S(2)}) copy-start(bf16[128,768]{1,0:T(8,128)(2,1)S(1)} %fusion.30.refs_5_) | copy-start | bytes 589828
  98.3 16.5 %copy-start.27 = (f32[128,768]{1,0:T(8,128)S(1)}, f32[128,768]{1,0:T(8,128)}, u32[]{:S(2)}) copy-start(f32[128,768]{1,0:T(8,128)} %copy-done.26) | copy-start | bytes 1179652
  98.3 16.5 %copy-start.31 = (bf16[128,1152]{1,0:T(8,128)(2,1)S(1)}, bf16[128,1152]{1,0:T(8,128)(2,1)}, u32[]{:S(2)}) copy-start(bf16[128,1152]{1,0:T(8,128)(2,1)} %get-tuple-element.53) | copy-start | bytes 884740
  106.5 11.0 %collective-permute-start.2 = (bf16[64,1536]{1,0:T(8,128)(2,1)S(1)}, bf16[64,1536]{1,0:T(8,128)(2,1)S(1)}, u32[]{:S(2)}, u32[]{:S(2)}) collective-permute-start(bf16[64,1536]{1,0:T(8,128)(2,1)S(1)} %get-tuple-element.35), channel_id=1, source_target_pairs={{0,4},{4,8},{8,12},{12,16},{16,20},{20,24},{24,28},{1,5},{5,9},{9,... | collective-permute-start | bytes 589832 | tf_op jit(solution)/shard_map/ppermute | solution.py:556
  110.9 8.1 %collective-permute-start.3 = (bf16[64,1536]{1,0:T(8,128)(2,1)S(1)}, bf16[64,1536]{1,0:T(8,128)(2,1)S(1)}, u32[]{:S(2)}, u32[]{:S(2)}) collective-permute-start(bf16[64,1536]{1,0:T(8,128)(2,1)S(1)} %get-tuple-element.36), channel_id=1, source_target_pairs={{4,0},{8,4},{12,8},{16,12},{20,16},{24,20},{28,24},{5,1},{9,5},{13... | collective-permute-start | bytes 589832 | tf_op jit(solution)/shard_map/ppermute | solution.py:557
  114.8 4.5 %copy-start.1 = (bf16[4,192,2304]{2,1,0:T(8,128)(2,1)S(1)}, bf16[4,192,2304]{2,1,0:T(8,128)(2,1)}, u32[]{:S(2)}) copy-start(bf16[4,192,2304]{2,1,0:T(8,128)(2,1)} %copy-done) | copy-start | bytes 10616836
  114.8 4.5 %copy-start.28 = (bf16[1,128,768]{2,1,0:T(8,128)(2,1)S(1)}, bf16[1,128,768]{2,1,0:T(8,128)(2,1)}, u32[]{:S(2)}) copy-start(bf16[1,128,768]{2,1,0:T(8,128)(2,1)} %param.9) | copy-start | bytes 589828
  119.3 1.4 copy-start.2
  119.3 1.4 copy-start.45
  119.3 1.5 copy-start.40
  119.4 1.8 copy-start.36
  119.4 1.8 copy-start.43
  209.4 3.0 %copy-start.38 = (f32[192,768]{1,0:T(8,128)S(1)}, f32[192,768]{1,0:T(8,128)}, u32[]{:S(2)}) copy-start(f32[192,768]{1,0:T(8,128)} %get-tuple-element.85) | copy-start | bytes 1769476
  209.4 3.8 %copy-start.32 = (f32[192,2304]{1,0:T(8,128)S(1)}, f32[192,2304]{1,0:T(8,128)}, u32[]{:S(2)}) copy-start(f32[192,2304]{1,0:T(8,128)} %get-tuple-element.86) | copy-start | bytes 5308420
  213.2 1.8 copy-start.37
  (2 other events, 1.3 us)

commit v4 on v3

--- a/solution.py
+++ b/solution.py
@@ -70,8 +70,10 @@
     return me, z, core, b1, b2
 
 
-def greet(me, z):
+def greet(me, z, others=()):
     barrier = pltpu.get_barrier_semaphore()
+    for other in others:
+        pl.semaphore_signal(barrier, inc=1, device_id={"seq": other}, device_id_type=MESH)
     for step in (1, 2, 4):
         pl.semaphore_signal(
             barrier, inc=1, device_id={"seq": partner(me, step)}, device_id_type=MESH
@@ -80,7 +82,7 @@
         pl.semaphore_signal(
             barrier, inc=1, device_id={"fsdp": (z + step) % 4}, device_id_type=MESH
         )
-    pl.semaphore_wait(barrier, 6)
+    pl.semaphore_wait(barrier, 6 + len(others))
 
 
 def rows(block, size, count=1):
@@ -215,31 +217,32 @@
 
 
 WIDE = 384
-CHUNKS = ((2, 0), (0, 0), (2, 384), (0, 384), (2, 768), (0, 768), (3, 0), (1, 0))
+CHUNKS = ((2, 0), (2, 384), (2, 768), (1, 0), (0, 0), (0, 384), (0, 768), (3, 0))
 
 
 def reduce_order():
-    ahead = 4
-    order = [("first", p) for p in range(ahead)]
+    order = []
     for t in range(4 + 6):
         for act, lag in (
             ("finish", 6), ("across", 5), ("spread", 4), ("owner", 3), ("share", 2), ("pair", 0)
         ):
             if 0 <= t - lag < 4:
                 order.append((act, t - lag))
-        if t + ahead < 4:
-            order.append(("first", t + ahead))
     return order
 
 
 def reduce_kernel(*refs):
-    xin, yin, gin, outs = refs[:4], refs[4:8], refs[8], refs[9:14]
-    xb, yb, gb = refs[14:18], refs[18:22], refs[22]
-    cs, b1s, s1s, b2s, s2s, bz, ag = (refs[23 + 8 * i : 31 + 8 * i] for i in range(7))
-    csem, sem1, sem2, zsem, asem = refs[79:]
+    xin, yin, gin = refs[:4], (None,) + refs[4:7], refs[7]
+    q, above, own, below, pos, grad, lse, cosine, sine, w_qkv, unit = refs[8:19]
+    outs, dh_out = refs[19:24], refs[24]
+    xb, yb, gb = refs[25:29], refs[29:33], refs[33]
+    cs, b1s, s1s, b2s, s2s, bz, ag = (refs[34 + 8 * i : 42 + 8 * i] for i in range(7))
+    csem, sem1, sem2, zsem, asem, hsem = refs[90:96]
+    dq, up, mid, down, back_above, back_below, mixed, gsum, gmine = refs[96:]
     me, z, core, b1, b2 = place()
     quarter = b1 + 2 * b2
-    greet(me, z)
+    after, before = (me + 1) % 8, (me + 7) % 8
+    greet(me, z, (after, before))
     f32, low = jnp.float32, jnp.bfloat16
     sent = []
     table = {}
@@ -256,14 +259,16 @@
 
     twin = {"seq": partner(me, 1)}
     lanes = cols(core, 128)
-    for w in (2, 0, 3, 1):
+    for w in (2, 1, 3, 0):
         c = SHARES[w][1]
         go(("x", w), xin[w], xb[w].at[:, lanes], csem.at[0, w], twin)
-        go(("x", w), yin[w].at[:, cols(1 - core, c)], yb[w].at[rows(core, 128)], csem.at[1, w], twin)
-    go("g", gin.at[:, :, cols(1 - core, WIDE)], gb, csem.at[2, 0], twin)
-    for w in (2, 0, 3, 1):
+        if w > 0:
+            src = yin[w].at[:, cols(1 - core, c)]
+            go(("x", w), src, yb[w].at[rows(core, 128)], csem.at[1, w], twin)
+    for w in (2, 1, 3, 0):
         xb[w][:, lanes] = xin[w][...]
-        yb[w][rows(core, 128), :] = yin[w][:, cols(core, SHARES[w][1])]
+        if w > 0:
+            yb[w][rows(core, 128), :] = yin[w][:, cols(core, SHARES[w][1])]
 
     def product(i):
         w, start = CHUNKS[i]
@@ -278,13 +283,8 @@
             return carry
 
         lax.fori_loop(0, 4, body, 0)
-        if w == 3:
-            take("g")
-            mine = gin[:, :, cols(core, WIDE)].astype(f32)
-            cs[i][:, height - PAD :, :] = (mine + gb[...].astype(f32)).astype(low)
 
     def first(i):
-        product(i)
         w = CHUNKS[i][0]
         r = SHARES[w][0]
         if BIT1_FIRST[w]:
@@ -386,25 +386,72 @@
         "first": first, "pair": pair, "share": share, "owner": owner,
         "spread": spread, "across": across, "finish": finish,
     }
+    for i in range(4):
+        product(i)
+        first(i)
+    product(7)
+    attend_back_kernel(
+        q, above, own, below, pos, grad, lse, cosine, sine, dq, up, mid, down
+    )
+    to_before = push(up, back_below, hsem.at[0, 0], hsem.at[0, 1], {"seq": before})
+    to_after = push(down, back_above, hsem.at[1, 0], hsem.at[1, 1], {"seq": after})
+    pl.when(me > 0)(to_before.start)
+    pl.when(me < 7)(to_after.start)
+
+    @pl.when(me == 0)
+    def _():
+        back_above[...] = jnp.zeros_like(back_above)
+
+    @pl.when(me == 7)
+    def _():
+        back_below[...] = jnp.zeros_like(back_below)
+
+    pl.when(me > 0)(to_after.wait_recv)
+    pl.when(me < 7)(to_before.wait_recv)
+    join_kernel(dq, mid, back_above, back_below, cosine, sine, mixed)
+    c = SHARES[0][1]
+    go(("x", 0), mixed.at[:, cols(1 - core, c)], yb[0].at[rows(core, 128)], csem.at[1, 0], twin)
+    yb[0][rows(core, 128), :] = mixed[:, cols(core, c)]
+    for i in (4, 5, 6):
+        product(i)
+        first(i)
+    for g in range(D // 128):
+        at = slice(128 * g, 128 * g + 128)
+        dh = dot_rows(mixed[...], w_qkv[at, :])
+        dh_out[:, at] = dh
+        gsum[0:1, at] = jnp.sum(dh * unit[:, at], axis=0, keepdims=True)
+    held = D // 4
+    for o in range(4):
+        piece = gsum[0:1, held * o : held * o + held]
+        piece = jnp.concatenate([piece, jnp.zeros((1, D - held), f32)], axis=1)
+        gmine[o] = (gin[o].astype(f32) + jnp.broadcast_to(piece, (PAD, D))).astype(low)
+    go("g", gmine.at[:, :, cols(1 - core, WIDE)], gb, csem.at[2, 0], twin)
+    take("g")
+    kept = gmine[:, :, cols(core, WIDE)].astype(f32)
+    cs[7][:, 4 * SHARES[3][0] - PAD :, :] = (kept + gb[...].astype(f32)).astype(low)
+    first(7)
     for act, p in reduce_order():
         for i in (2 * p, 2 * p + 1):
             acts[act](i)
     for copy in sent:
         copy.wait_send()
-
-
-def reduce_grads(lefts, rights, gain_rows):
+    pl.when(me > 0)(to_before.wait_send)
+    pl.when(me < 7)(to_after.wait_send)
+
+
+def reduce_grads(lefts, rights, gain_rows, attention):
     sem = pltpu.SemaphoreType.DMA
     vmem = lambda *shape: pltpu.VMEM(shape, jnp.bfloat16)
     heights = [SHARES[w][0] for w, start in CHUNKS]
     count = len(CHUNKS)
     shapes = [(4 * r, 2 * c) for r, c in SHARES]
-    shapes = shapes[:3] + [(shapes[3][0] - PAD, shapes[3][1]), (PAD, shapes[3][1])]
+    shapes = shapes[:3] + [(shapes[3][0] - PAD, shapes[3][1]), (PAD, shapes[3][1]), (128, D)]
+    rim = (HALF_WINDOW, 2 * D)
     return pl.pallas_call(
         reduce_kernel,
         out_shape=[jax.ShapeDtypeStruct(shape, jnp.float32) for shape in shapes],
-        in_specs=[pl.BlockSpec(memory_space=pltpu.VMEM)] * 9,
-        out_specs=[pl.BlockSpec(memory_space=pltpu.VMEM)] * 5,
+        in_specs=[pl.BlockSpec(memory_space=pltpu.VMEM)] * 19,
+        out_specs=[pl.BlockSpec(memory_space=pltpu.VMEM)] * 6,
         scratch_shapes=[vmem(16 * r, 256) for r, c in SHARES]
         + [vmem(256, c) for r, c in SHARES]
         + [vmem(4, PAD, WIDE)]
@@ -415,12 +462,15 @@
         + [vmem(2, 4 * r, WIDE) for r in heights]
         + [
             sem((3, 4, 2)), sem((count, 2, 2)), sem((count, 2)), sem((count, 3, 2)),
-            sem((count, 4, 2)),
-        ],
+            sem((count, 4, 2)), sem((2, 2)),
+        ]
+        + [vmem(128, D), vmem(*rim), pltpu.VMEM((128, 2 * D), jnp.float32)]
+        + [vmem(*rim), vmem(*rim), vmem(*rim), vmem(128, 3 * D)]
+        + [pltpu.VMEM((8, D), jnp.float32), vmem(4, PAD, D)],
         compiler_params=pltpu.CompilerParams(
             collective_id=1, has_side_effects=True, vmem_limit_bytes=56 * 1024 * 1024
         ),
-    )(*lefts, *rights, gain_rows)
+    )(*lefts, *rights, gain_rows, *attention)
 
 
 def swap_halves(values):
@@ -617,38 +667,25 @@
     grad_branch = grad_middle.astype(jnp.bfloat16)
     grad_out_local = matmul_left(attended_low, grad_branch)
     grad_attended = matmul_right(grad_branch, full_out).astype(low)
-    grad_query, up, own, down = local_call(
-        attend_back_kernel,
-        [
-            ((count, D), low),
-            ((HALF_WINDOW, 2 * D), low),
-            ((count, 2 * D), jnp.float32),
-            ((HALF_WINDOW, 2 * D), low),
-        ],
-        query_low, above, key_value, below, pos, grad_attended, logsum, cosine, sine,
-    )
-    back_above, back_below = neighbours(up, down)
-    (grad_mixed,) = local_call(
-        join_kernel, [((count, 3 * D), low)], grad_query, own, back_above, back_below, cosine, sine
-    )
-    grad_qkv_local = matmul_left(normed_low, grad_mixed)
-    grad_normed = matmul_right(grad_mixed, full_qkv)
-    grad_tokens_norm, grad_gain_first = norm_back(grad_normed)
-    grad_tokens = grad_middle + grad_tokens_norm
     lanes = lax.axis_size("seq")
     if lanes == 8:
-        gain_rows = jnp.concatenate(
-            [grad_gain_first.reshape(4, 1, held), grad_gain_second.reshape(4, 1, held)], axis=2
+        gain_rows = jnp.pad(
+            grad_gain_second.reshape(4, 1, held),
+            ((0, 0), (0, PAD - 1), (held, D - 2 * held)),
         )
-        gain_rows = jnp.pad(gain_rows, ((0, 0), (0, PAD - 1), (0, D - 2 * held)))
         hidden_rows = jnp.pad(
             hidden_low.T.reshape(4, owned_rows, count), ((0, 0), (0, PAD), (0, 0))
         )
-        grad_qkv, grad_out, grad_in, grad_down, gain_sums = reduce_grads(
+        grad_qkv, grad_out, grad_in, grad_down, gain_sums, grad_normed = reduce_grads(
             [normed_low.T, attended_low.T, normed_mlp_low.T, hidden_rows.reshape(-1, count)],
-            [grad_mixed, grad_branch, grad_gate_up, grad_result],
+            [grad_branch, grad_gate_up, grad_result],
             gain_rows.astype(jnp.bfloat16),
+            [
+                query_low, above, key_value, below, pos, grad_attended, logsum, cosine, sine,
+                full_qkv, layer_norm(tokens, jnp.ones_like(gain_first)),
+            ],
         )
+        grad_tokens = grad_middle + norm_back(grad_normed)[0]
         return (
             result[None].astype(jnp.bfloat16),
             grad_tokens[None],
@@ -659,6 +696,24 @@
             gain_sums[0, :held],
             gain_sums[0, held : 2 * held],
         )
+    grad_query, up, own, down = local_call(
+        attend_back_kernel,
+        [
+            ((count, D), low),
+            ((HALF_WINDOW, 2 * D), low),
+            ((count, 2 * D), jnp.float32),
+            ((HALF_WINDOW, 2 * D), low),
+        ],
+        query_low, above, key_value, below, pos, grad_attended, logsum, cosine, sine,
+    )
+    back_above, back_below = neighbours(up, down)
+    (grad_mixed,) = local_call(
+        join_kernel, [((count, 3 * D), low)], grad_query, own, back_above, back_below, cosine, sine
+    )
+    grad_qkv_local = matmul_left(normed_low, grad_mixed)
+    grad_normed = matmul_right(grad_mixed, full_qkv)
+    grad_tokens_norm, grad_gain_first = norm_back(grad_normed)
+    grad_tokens = grad_middle + grad_tokens_norm
     owned = (
         lax.psum_scatter(
             grad_qkv_local.astype(jnp.bfloat16), "fsdp", scatter_dimension=0, tiled=True

time: 217 us -> 220 us (1.014)
  Pallas kernels: 143 us -> 156 us
  starting transfers between devices: 12.3 us -> 5.27 us
  matrix products: 13.4 us -> 9.38 us
  other arithmetic: 11.8 us -> 14.4 us
    pallas_call x1, Pallas kernels: 84.3 us -> 105 us  [reduce_grads(): pl.pallas_call(reduce_kernel, out_shape=[jax.ShapeDtypeStruct(shape, jnp....]
    pallas_call x4 -> x2, Pallas kernels: 10.1 us -> 2.88 us  [local_call(): pl.pallas_call(kernel, out_shape=[jax.ShapeDtypeStruct(shape, kind) for s...]
    ppermute x2 -> x1, starting transfers between devices: 8.17 us -> 3.04 us  [neighbours(): above = lax.ppermute(down, 'seq', [(i, i + 1) for i in range(lanes - 1)])]
    unnamed x96 -> x94, local copies, waits for them, and re-layouts: 18.8 us -> 21.9 us
    dot_general x4 -> x3, matrix products: 5.37 us -> 4.18 us  [matmul_right(): lax.dot_general(left, right, (((1,), (1,)), ((), ())), preferred_element_...]
  transfers between devices with their start and end apart: 4 -> 2, of which waited for: 2 -> 1; matrix products, arithmetic and copies ran while one was open for 3% -> 2% of each run, Pallas kernels for 0% -> 0%
where the time goes in v4:
time: 220 us; the launch traced here: 219 us
  Pallas kernels  156 us (71%)
  local copies, waits for them, and re-layouts  32.2 us (15%)
  other arithmetic  14.4 us (7%)
  matrix products  9.38 us (4%)
  starting transfers between devices  5.27 us (2%)
    pallas_call x1, Pallas kernels, reduce_grads(): pl.pallas_call(reduce_kernel, out_shape=[jax.ShapeDtypeStruct(shape, jnp....  105 us
    pallas_call x1, Pallas kernels, gather_weights(): pl.pallas_call(gather_kernel, out_shape=[jax.ShapeDtypeStruct((4, 4 * r,...  48.5 us
    unnamed x94, local copies, waits for them, and re-layouts  21.9 us
  transfers between devices with their start and end apart: 2, of which 1 were waited for; matrix products, arithmetic and copies ran while one was open for 2% of the time, Pallas kernels for 0%

profile of v4, /device:TPU:1, one launch (start us, length us, event | category | flops | bytes accessed | tf_op | source)
XLA Modules:
  0.0 219.1 jit_solution(3893767137181748971)
XLA Ops:
  1.2 0.7 pad_maximum_fusion.2
  1.9 1.0 fusion.15.refs_3_
  3.0 1.2 copy-done.9
  4.1 1.2 copy-done.10
  5.3 1.0 copy-done.21
  6.3 48.5 %shard_map.152 = (bf16[4,192,2304]{2,1,0:T(8,128)(2,1)S(1)}, bf16[4,192,768]{2,1,0:T(8,128)(2,1)S(1)}, bf16[4,192,2304]{2,1,0:T(8,128)(2,1)S(1)}, bf16[4,320,768]{2,1,0:T(8,128)(2,1)S(1)}) custom-call(bf16[192,2304]{1,0:T(8,128)(2,1)S(1)} %copy-done.9, bf16[192,768]{1,0:T(8,128)(2,1)S(1)} %copy-done.21, bf16[192,2304]{1,0:T(8,128)(2,1)S(1)} %copy-done.10, ...), custom_call_target="tpu_custom_call" | custom-call | tf_op jit(solution)/shard_map/pallas_call | solution.py:204
  54.8 1.8 copy-done.1
  56.6 1.0 copy-done.3
  57.6 1.3 copy-done.7
  59.1 1.3 convert_reduce_fusion
  60.4 1.1 fusion.16
  62.0 1.3 convert_bitcast_fusion.2
  63.3 1.4 copy.35.flags
  64.7 1.0 fusion.30
  65.7 1.6 fusion.24.mixed
  68.1 3.0 %collective-permute-start = (bf16[64,1664]{1,0:T(8,128)(2,1)S(1)}, bf16[64,1664]{1,0:T(8,128)(2,1)S(1)}, u32[]{:S(2)}, u32[]{:S(2)}) collective-permute-start(bf16[64,1664]{1,0:T(8,128)(2,1)S(1)} %get-tuple-element.47), channel_id=1, source_target_pairs={{0,4},{4,8},{8,12},{12,16},{16,20},{20,24},{24,28},{1,5},{5,9},{9,... | collective-permute-start | bytes 638984 | tf_op jit(solution)/shard_map/ppermute | solution.py:606
  71.2 2.2 %collective-permute-start.1 = (bf16[64,1664]{1,0:T(8,128)(2,1)S(1)}, bf16[64,1664]{1,0:T(8,128)(2,1)S(1)}, u32[]{:S(2)}, u32[]{:S(2)}) collective-permute-start(bf16[64,1664]{1,0:T(8,128)(2,1)S(1)} %get-tuple-element.46), channel_id=1, source_target_pairs={{4,0},{8,4},{12,8},{16,12},{20,16},{24,20},{28,24},{5,1},{9,5},{13... | collective-permute-start | bytes 638984 | tf_op jit(solution)/shard_map/ppermute | solution.py:607
  73.4 1.3 slice.33
  74.8 0.7 copy.36.pos.refs_12_
  75.6 1.0 fusion.13
  76.6 0.8 copy.41.refs_0_
  79.2 1.0 copy-done.6
  80.2 0.9 copy-done.12
  81.1 0.9 copy-done.14
  82.1 0.9 copy-done.17
  83.0 0.8 copy-done.18
  83.8 2.4 %shard_map.154 = (bf16[128,768]{1,0:T(8,128)(2,1)S(1)}, f32[128,128]{1,0:T(8,128)S(1)}) custom-call(bf16[128,768]{1,0:T(8,128)(2,1)S(1)} %copy-done.17, bf16[64,1664]{1,0:T(8,128)(2,1)S(1)} %copy-done.12, bf16[128,1664]{1,0:T(8,128)(2,1)S(1)} %copy-done.6, bf16[64,1664]{1,0:T(8,128)(2,1)S(1)} %copy-done.14, f32[128,1]{1,0:T(8,128)S(1)} %copy-done.18), custom_call_target="tpu_custom_call" | custom-call | tf_op jit(solution)/shard_map/pallas_call | solution.py:595
  87.5 1.7 copy.38
  89.3 1.8 fusion.41
  92.0 0.8 copy-done.28
  92.8 1.5 fusion.29
  94.3 1.0 multiply_add_fusion
  95.4 1.4 multiply_reduce_fusion
  97.3 0.8 copy-done.4
  98.1 1.2 convolution_convert_fusion.refs_13_
  99.3 0.8 copy.42.refs_2_
  100.2 1.1 fusion.1
  101.6 0.8 pad.23.refs_7_
  102.3 0.7 pad.22
  103.1 105.0 %shard_map.155 = (f32[192,2304]{1,0:T(8,128)}, f32[192,768]{1,0:T(8,128)}, f32[192,2304]{1,0:T(8,128)}, f32[288,768]{1,0:T(8,128)}, f32[32,768]{1,0:T(8,128)}, /*index=5*/f32[128,768]{1,0:T(8,128)}) custom-call(bf16[768,128]{1,0:T(8,128)(2,1)} %copy.41.refs_0_, bf16[768,128]{1,0:T(8,128)(2,1)} %bitcast.85, bf16[768,128]{1,0:T(8,128)(2,1)} %copy.42.refs_2_, ...), custom_call_target="tpu_custom_call" | custom-call | tf_op jit(solution)/shard_map/pallas_call | solution.py:450
  208.1 1.3 fusion.17
  209.5 1.2 fusion.34
  210.7 2.0 add_bitcast_fusion
  212.7 1.4 fusion.40
  214.1 1.2 copy.49
  215.6 0.8 copy.50
  216.4 1.2 copy.51
  218.2 0.9 copy.52
  (102 shorter events, 7.7 us)
Async XLA Ops:
  3.0 1.2 copy-start.9
  4.1 1.2 copy-start.10
  5.3 1.0 copy-start.21
  54.8 1.8 copy-start.1
  56.6 1.0 copy-start.3
  57.6 1.3 copy-start.7
  57.6 9.7 %copy-start = (bf16[4,192,2304]{2,1,0:T(8,128)(2,1)}, bf16[4,192,2304]{2,1,0:T(8,128)(2,1)S(1)}, u32[]{:S(2)}) copy-start(bf16[4,192,2304]{2,1,0:T(8,128)(2,1)S(1)} %get-tuple-element.23) | copy-start | bytes 10616836
  61.5 0.5 copy-start.43
  62.0 5.3 %copy-start.39 = (f32[128]{0:T(128)}, f32[128]{0:T(128)S(1)}, u32[]{:S(2)}) copy-start(f32[128]{0:T(128)S(1)} %fusion.31) | copy-start | bytes 1540
  65.7 1.9 copy-start.22
  67.3 6.1 %copy-start.8 = (bf16[4,320,768]{2,1,0:T(8,128)(2,1)S(1)}, bf16[4,320,768]{2,1,0:T(8,128)(2,1)}, u32[]{:S(2)}) copy-start(bf16[4,320,768]{2,1,0:T(8,128)(2,1)} %copy-done.7) | copy-start | bytes 5898244
  67.5 7.2 %copy-start.19 = (f32[128,128]{1,0:T(8,128)}, f32[128,128]{1,0:T(8,128)S(1)}, u32[]{:S(2)}) copy-start(f32[128,128]{1,0:T(8,128)S(1)} %get-tuple-element.63.cosine.refs_15_) | copy-start | bytes 196612
  67.5 7.2 %copy-start.20 = (f32[128,128]{1,0:T(8,128)}, f32[128,128]{1,0:T(8,128)S(1)}, u32[]{:S(2)}) copy-start(f32[128,128]{1,0:T(8,128)S(1)} %get-tuple-element.64.sine.refs_16_) | copy-start | bytes 196612
  68.1 6.7 %copy-start.5 = (bf16[128,1664]{1,0:T(8,128)(2,1)}, bf16[128,1664]{1,0:T(8,128)(2,1)S(1)}, u32[]{:S(2)}) copy-start(bf16[128,1664]{1,0:T(8,128)(2,1)S(1)} %get-tuple-element.25.own.refs_10_) | copy-start | bytes 1277956
  68.1 6.7 %copy-start.16 = (bf16[128,768]{1,0:T(8,128)(2,1)}, bf16[128,768]{1,0:T(8,128)(2,1)S(1)}, u32[]{:S(2)}) copy-start(bf16[128,768]{1,0:T(8,128)(2,1)S(1)} %get-tuple-element.24.q.refs_8_) | copy-start | bytes 589828
  68.1 9.3 %collective-permute-start = (bf16[64,1664]{1,0:T(8,128)(2,1)S(1)}, bf16[64,1664]{1,0:T(8,128)(2,1)S(1)}, u32[]{:S(2)}, u32[]{:S(2)}) collective-permute-start(bf16[64,1664]{1,0:T(8,128)(2,1)S(1)} %get-tuple-element.47), channel_id=1, source_target_pairs={{0,4},{4,8},{8,12},{12,16},{16,20},{20,24},{24,28},{1,5},{5,9},{9,... | collective-permute-start | bytes 638984 | tf_op jit(solution)/shard_map/ppermute | solution.py:606
  71.2 3.6 %copy-start.42 = (f32[128,1]{0,1:T(1,128)S(1)}, f32[128,1]{0,1:T(1,128)}, u32[]{:S(2)}) copy-start(f32[128,1]{0,1:T(1,128)} %get-tuple-element.56) | copy-start | bytes 1540
  71.2 4.4 %copy-start.26 = (bf16[1,128,768]{2,1,0:T(8,128)(2,1)S(1)}, bf16[1,128,768]{2,1,0:T(8,128)(2,1)}, u32[]{:S(2)}) copy-start(bf16[1,128,768]{2,1,0:T(8,128)(2,1)} %param.9) | copy-start | bytes 589828
  71.2 4.4 %copy-start.40 = (f32[128]{0:T(128)S(1)}, f32[128]{0:T(128)}, u32[]{:S(2)}) copy-start(f32[128]{0:T(128)} %copy-done.39) | copy-start | bytes 1540
  71.2 7.3 %collective-permute-start.1 = (bf16[64,1664]{1,0:T(8,128)(2,1)S(1)}, bf16[64,1664]{1,0:T(8,128)(2,1)S(1)}, u32[]{:S(2)}, u32[]{:S(2)}) collective-permute-start(bf16[64,1664]{1,0:T(8,128)(2,1)S(1)} %get-tuple-element.46), channel_id=1, source_target_pairs={{4,0},{8,4},{12,8},{16,12},{20,16},{24,20},{28,24},{5,1},{9,5},{13... | collective-permute-start | bytes 638984 | tf_op jit(solution)/shard_map/ppermute | solution.py:607
  77.4 0.7 copy-start.11
  78.5 0.7 copy-start.13
  79.2 1.0 copy-start.6
  80.2 0.9 copy-start.12
  81.1 0.9 copy-start.14
  82.1 0.9 copy-start.17
  83.0 0.8 copy-start.18
  83.8 7.4 %copy-start.2 = (bf16[4,192,2304]{2,1,0:T(8,128)(2,1)S(1)}, bf16[4,192,2304]{2,1,0:T(8,128)(2,1)}, u32[]{:S(2)}) copy-start(bf16[4,192,2304]{2,1,0:T(8,128)(2,1)} %copy-done.1) | copy-start | bytes 10616836
  86.2 0.7 copy-start.15
  86.9 0.6 copy-start.23
  91.0 5.8 %copy-start.24 = (f32[128,768]{1,0:T(8,128)}, f32[128,768]{1,0:T(8,128)S(1)}, u32[]{:S(2)}) copy-start(f32[128,768]{1,0:T(8,128)S(1)} %get-tuple-element.60) | copy-start | bytes 1179652
  91.3 1.5 copy-start.28
  91.3 1.5 copy-start.35
  95.4 1.4 copy-start.30
  96.8 1.3 copy-start.4
  96.8 3.4 %copy-start.29 = (bf16[4,288,768]{2,1,0:T(8,128)(2,1)S(1)}, bf16[4,288,768]{2,1,0:T(8,128)(2,1)}, u32[]{:S(2)}) copy-start(bf16[4,288,768]{2,1,0:T(8,128)(2,1)} %slice.33) | copy-start | bytes 5308420
  96.8 3.4 %copy-start.31 = (bf16[128,1152]{1,0:T(8,128)(2,1)S(1)}, bf16[128,1152]{1,0:T(8,128)(2,1)}, u32[]{:S(2)}) copy-start(bf16[128,1152]{1,0:T(8,128)(2,1)} %get-tuple-element.45) | copy-start | bytes 884740
  97.1 3.1 %copy-start.25 = (f32[128,768]{1,0:T(8,128)S(1)}, f32[128,768]{1,0:T(8,128)}, u32[]{:S(2)}) copy-start(f32[128,768]{1,0:T(8,128)} %copy-done.24) | copy-start | bytes 1179652
  98.1 3.3 %copy-start.34 = (bf16[128,768]{1,0:T(8,128)(2,1)}, bf16[128,768]{1,0:T(8,128)(2,1)S(1)}, u32[]{:S(2)}) copy-start(bf16[128,768]{1,0:T(8,128)(2,1)S(1)} %fusion.21.refs_4_) | copy-start | bytes 589828
  103.1 105.1 %copy-start.27 = (bf16[1,128,768]{2,1,0:T(8,128)(2,1)S(1)}, bf16[1,128,768]{2,1,0:T(8,128)(2,1)}, u32[]{:S(2)}) copy-start(bf16[1,128,768]{2,1,0:T(8,128)(2,1)} %param.9) | copy-start | bytes 589828
  103.1 106.4 %copy-start.44 = (f32[128]{0:T(128)S(1)}, f32[128]{0:T(128)}, u32[]{:S(2)}) copy-start(f32[128]{0:T(128)} %copy-done.43) | copy-start | bytes 1540
  103.1 106.4 %copy-start.41 = (f32[128]{0:T(128)S(1)}, f32[128]{0:T(128)}, u32[]{:S(2)}) copy-start(f32[128]{0:T(128)} %copy-done.39) | copy-start | bytes 1540
  103.1 107.7 %copy-start.36 = (bf16[1,128,768]{2,1,0:T(8,128)(2,1)S(1)}, bf16[1,128,768]{2,1,0:T(8,128)(2,1)}, u32[]{:S(2)}) copy-start(bf16[1,128,768]{2,1,0:T(8,128)(2,1)} %param.11) | copy-start | bytes 589828
  208.1 6.0 %copy-start.33 = (f32[192,2304]{1,0:T(8,128)S(1)}, f32[192,2304]{1,0:T(8,128)}, u32[]{:S(2)}) copy-start(f32[192,2304]{1,0:T(8,128)} %get-tuple-element.75) | copy-start | bytes 5308420
  214.1 1.4 copy-start.38
  214.1 2.3 %copy-start.32 = (f32[192,2304]{1,0:T(8,128)S(1)}, f32[192,2304]{1,0:T(8,128)}, u32[]{:S(2)}) copy-start(f32[192,2304]{1,0:T(8,128)} %get-tuple-element.77) | copy-start | bytes 5308420
  216.4 1.8 copy-start.37

commit v5 on v4

--- a/solution.py
+++ b/solution.py
@@ -220,14 +220,22 @@
 CHUNKS = ((2, 0), (2, 384), (2, 768), (1, 0), (0, 0), (0, 384), (0, 768), (3, 0))
 
 
+CHUNK_BIT1 = (False, False, True, True, False, True, True, False)
+
+
 def reduce_order():
+    early, late = range(4), range(4, 8)
     order = []
-    for t in range(4 + 6):
-        for act, lag in (
-            ("finish", 6), ("across", 5), ("spread", 4), ("owner", 3), ("share", 2), ("pair", 0)
-        ):
-            if 0 <= t - lag < 4:
-                order.append((act, t - lag))
+    for i in early:
+        order += [("owner", i), ("pair", 4 + i)]
+    for i in early:
+        order += [("spread", i), ("share", 4 + i)]
+    for i in early:
+        order += [("across", i), ("owner", 4 + i)]
+    order += [("spread", i) for i in late]
+    order += [("finish", i) for i in early]
+    for act in ("across", "finish"):
+        order += [(act, i) for i in late]
     return order
 
 
@@ -287,7 +295,7 @@
     def first(i):
         w = CHUNKS[i][0]
         r = SHARES[w][0]
-        if BIT1_FIRST[w]:
+        if CHUNK_BIT1[i]:
             src = cs[i].at[:, rows(2 * (1 - b2), r, 2), :]
             go((1, i), src, b1s[i], sem1.at[i, 0], {"seq": partner(me, 4)})
         else:
@@ -303,14 +311,14 @@
 
         def body(t, carry):
             o, j = t // 2, t % 2
-            block = 2 * b2 + j if BIT1_FIRST[w] else b1 + 2 * j
+            block = 2 * b2 + j if CHUNK_BIT1[i] else b1 + 2 * j
             there = pl.ds(pl.multiple_of(j * r, 16), r)
             mine = cs[i][o, rows(block, r), :].astype(f32)
             s1s[i][o, there, :] = (mine + b1s[i][o, there, :].astype(f32)).astype(low)
             return carry
 
         lax.fori_loop(0, 8, body, 0)
-        bit, step = (b1, 2) if BIT1_FIRST[w] else (b2, 4)
+        bit, step = (b1, 2) if CHUNK_BIT1[i] else (b2, 4)
         src = s1s[i].at[:, rows(1 - bit, r), :]
         go((2, i), src, b2s[i], sem2.at[i], {"seq": partner(me, step)})
 
@@ -318,7 +326,7 @@
         w = CHUNKS[i][0]
         r = SHARES[w][0]
         take((2, i))
-        bit = b1 if BIT1_FIRST[w] else b2
+        bit = b1 if CHUNK_BIT1[i] else b2
 
         def body(o, carry):
             mine = s1s[i][o, rows(bit, r), :].astype(f32)
@@ -339,14 +347,14 @@
             total = total + bz[i][d].astype(f32)
         ag[i][core, rows(quarter, r), :] = total.astype(low)
         block = ag[i].at[core, rows(quarter, r), :]
-        step = 2 if BIT1_FIRST[w] else 4
+        step = 2 if CHUNK_BIT1[i] else 4
         go((4, i), block, block, asem.at[i, 0], {"seq": partner(me, step)})
 
     def spread(i):
         w = CHUNKS[i][0]
         r = SHARES[w][0]
         take((4, i))
-        if BIT1_FIRST[w]:
+        if CHUNK_BIT1[i]:
             block = ag[i].at[core, rows(2 * b2, r, 2), :]
             go((5, i), block, block, asem.at[i, 1], {"seq": partner(me, 4)})
         else:
@@ -398,6 +406,9 @@
     pl.when(me > 0)(to_before.start)
     pl.when(me < 7)(to_after.start)
 
+    for i in range(4):
+        pair(i)
+
     @pl.when(me == 0)
     def _():
         back_above[...] = jnp.zeros_like(back_above)
@@ -415,6 +426,8 @@
     for i in (4, 5, 6):
         product(i)
         first(i)
+    for i in range(4):
+        share(i)
     for g in range(D // 128):
         at = slice(128 * g, 128 * g + 128)
         dh = dot_rows(mixed[...], w_qkv[at, :])
@@ -430,9 +443,8 @@
     kept = gmine[:, :, cols(core, WIDE)].astype(f32)
     cs[7][:, 4 * SHARES[3][0] - PAD :, :] = (kept + gb[...].astype(f32)).astype(low)
     first(7)
-    for act, p in reduce_order():
-        for i in (2 * p, 2 * p + 1):
-            acts[act](i)
+    for act, i in reduce_order():
+        acts[act](i)
     for copy in sent:
         copy.wait_send()
     pl.when(me > 0)(to_before.wait_send)

time: 220 us -> 194 us (0.88)
  Pallas kernels: 156 us -> 131 us
    pallas_call x1, Pallas kernels: 105 us -> 79.4 us  [reduce_grads(): pl.pallas_call(reduce_kernel, out_shape=[jax.ShapeDtypeStruct(shape, jnp....]
where the time goes in v5:
time: 194 us
  Pallas kernels  131 us (68%)
  local copies, waits for them, and re-layouts  32.2 us (17%)
  other arithmetic  14.4 us (7%)
  matrix products  9.38 us (5%)
  starting transfers between devices  5.09 us (3%)
    pallas_call x1, Pallas kernels, reduce_grads(): pl.pallas_call(reduce_kernel, out_shape=[jax.ShapeDtypeStruct(shape, jnp....  79.4 us
    pallas_call x1, Pallas kernels, gather_weights(): pl.pallas_call(gather_kernel, out_shape=[jax.ShapeDtypeStruct((4, 4 * r,...  48.5 us
    unnamed x94, local copies, waits for them, and re-layouts  21.9 us
    dot_general x3, matrix products, matmul_right(): lax.dot_general(left, right, (((1,), (1,)), ((), ())), preferred_element_...  4.18 us
  transfers between devices with their start and end apart: 2, of which 1 were waited for; matrix products, arithmetic and copies ran while one was open for 2% of the time, Pallas kernels for 0%

profile of v5, /device:TPU:1, one launch (start us, length us, event | category | flops | bytes accessed | tf_op | source)
XLA Modules:
  0.0 193.5 jit_solution(953111766195328399)
XLA Ops:
  1.2 0.7 pad_maximum_fusion.2
  1.9 1.0 fusion.15.refs_3_
  3.0 1.2 copy-done.9
  4.1 1.2 copy-done.10
  5.3 1.0 copy-done.21
  6.3 48.5 %shard_map.152 = (bf16[4,192,2304]{2,1,0:T(8,128)(2,1)S(1)}, bf16[4,192,768]{2,1,0:T(8,128)(2,1)S(1)}, bf16[4,192,2304]{2,1,0:T(8,128)(2,1)S(1)}, bf16[4,320,768]{2,1,0:T(8,128)(2,1)S(1)}) custom-call(bf16[192,2304]{1,0:T(8,128)(2,1)S(1)} %copy-done.9, bf16[192,768]{1,0:T(8,128)(2,1)S(1)} %copy-done.21, bf16[192,2304]{1,0:T(8,128)(2,1)S(1)} %copy-done.10, ...), custom_call_target="tpu_custom_call" | custom-call | tf_op jit(solution)/shard_map/pallas_call | solution.py:204
  54.8 1.8 copy-done.1
  56.6 1.0 copy-done.3
  57.6 1.3 copy-done.7
  59.1 1.3 convert_reduce_fusion
  60.4 1.1 fusion.16
  62.0 1.3 convert_bitcast_fusion.2
  63.3 1.4 copy.35.flags
  64.7 1.0 fusion.30
  65.7 1.6 fusion.24.mixed
  68.1 3.0 %collective-permute-start = (bf16[64,1664]{1,0:T(8,128)(2,1)S(1)}, bf16[64,1664]{1,0:T(8,128)(2,1)S(1)}, u32[]{:S(2)}, u32[]{:S(2)}) collective-permute-start(bf16[64,1664]{1,0:T(8,128)(2,1)S(1)} %get-tuple-element.47), channel_id=1, source_target_pairs={{0,4},{4,8},{8,12},{12,16},{16,20},{20,24},{24,28},{1,5},{5,9},{9,... | collective-permute-start | bytes 638984 | tf_op jit(solution)/shard_map/ppermute | solution.py:618
  71.2 2.1 %collective-permute-start.1 = (bf16[64,1664]{1,0:T(8,128)(2,1)S(1)}, bf16[64,1664]{1,0:T(8,128)(2,1)S(1)}, u32[]{:S(2)}, u32[]{:S(2)}) collective-permute-start(bf16[64,1664]{1,0:T(8,128)(2,1)S(1)} %get-tuple-element.46), channel_id=1, source_target_pairs={{4,0},{8,4},{12,8},{16,12},{20,16},{24,20},{28,24},{5,1},{9,5},{13... | collective-permute-start | bytes 638984 | tf_op jit(solution)/shard_map/ppermute | solution.py:619
  73.3 1.3 slice.33
  74.6 0.7 copy.36.pos.refs_12_
  75.4 1.0 fusion.13
  76.4 0.8 copy.41.refs_0_
  79.2 1.0 copy-done.6
  80.2 0.9 copy-done.12
  81.1 0.9 copy-done.14
  82.1 0.9 copy-done.17
  83.0 0.8 copy-done.18
  83.8 2.4 %shard_map.154 = (bf16[128,768]{1,0:T(8,128)(2,1)S(1)}, f32[128,128]{1,0:T(8,128)S(1)}) custom-call(bf16[128,768]{1,0:T(8,128)(2,1)S(1)} %copy-done.17, bf16[64,1664]{1,0:T(8,128)(2,1)S(1)} %copy-done.12, bf16[128,1664]{1,0:T(8,128)(2,1)S(1)} %copy-done.6, bf16[64,1664]{1,0:T(8,128)(2,1)S(1)} %copy-done.14, f32[128,1]{1,0:T(8,128)S(1)} %copy-done.18), custom_call_target="tpu_custom_call" | custom-call | tf_op jit(solution)/shard_map/pallas_call | solution.py:607
  87.5 1.7 copy.38
  89.3 1.8 fusion.41
  92.0 0.8 copy-done.28
  92.8 1.5 fusion.29
  94.3 1.0 multiply_add_fusion
  95.4 1.4 multiply_reduce_fusion
  97.3 0.8 copy-done.4
  98.1 1.2 convolution_convert_fusion.refs_13_
  99.3 0.8 copy.42.refs_2_
  100.2 1.1 fusion.1
  101.6 0.8 pad.23.refs_7_
  102.3 0.7 pad.22
  103.1 79.4 %shard_map.155 = (f32[192,2304]{1,0:T(8,128)}, f32[192,768]{1,0:T(8,128)}, f32[192,2304]{1,0:T(8,128)}, f32[288,768]{1,0:T(8,128)}, f32[32,768]{1,0:T(8,128)}, /*index=5*/f32[128,768]{1,0:T(8,128)}) custom-call(bf16[768,128]{1,0:T(8,128)(2,1)} %copy.41.refs_0_, bf16[768,128]{1,0:T(8,128)(2,1)} %bitcast.85, bf16[768,128]{1,0:T(8,128)(2,1)} %copy.42.refs_2_, ...), custom_call_target="tpu_custom_call" | custom-call | tf_op jit(solution)/shard_map/pallas_call | solution.py:462
  182.5 1.3 fusion.17
  183.9 1.2 fusion.34
  185.2 2.0 %add_bitcast_fusion = f32[1,128,768]{2,1,0:T(8,128)} fusion(f32[128,768]{1,0:T(8,128)S(1)} %get-tuple-element.41, f32[128]{0:T(128)S(1)} %negate_multiply_fusion.1, f32[128]{0:T(128)S(1)} %negate_multiply_fusion.2, bf16[1,128,768]{2,1,0:T(8,128)(2,1)S(1)} %copy-done.36, f32[128]{0:T(128)S(1)} %multiply_multiply_fusion.5, ...), kind=kLoop, calls=%fused_computation.44 | loop fusion | flops 1179648 | bytes 1578496 | tf_op jit(solution)/shard_map/broadcast_in_dim | solution.py:703
  187.1 1.4 fusion.40
  188.6 1.2 copy.49
  190.0 0.8 copy.50
  190.9 1.2 copy.51
  192.6 0.9 copy.52
  (102 shorter events, 7.9 us)
Async XLA Ops:
  3.0 1.2 copy-start.9
  4.1 1.2 copy-start.10
  5.3 1.0 copy-start.21
  54.8 1.8 copy-start.1
  56.6 1.0 copy-start.3
  57.6 1.3 copy-start.7
  57.6 9.7 %copy-start = (bf16[4,192,2304]{2,1,0:T(8,128)(2,1)}, bf16[4,192,2304]{2,1,0:T(8,128)(2,1)S(1)}, u32[]{:S(2)}) copy-start(bf16[4,192,2304]{2,1,0:T(8,128)(2,1)S(1)} %get-tuple-element.23) | copy-start | bytes 10616836
  61.5 0.5 copy-start.43
  62.0 5.3 %copy-start.39 = (f32[128]{0:T(128)}, f32[128]{0:T(128)S(1)}, u32[]{:S(2)}) copy-start(f32[128]{0:T(128)S(1)} %fusion.31) | copy-start | bytes 1540
  65.7 1.9 copy-start.22
  67.3 5.9 %copy-start.8 = (bf16[4,320,768]{2,1,0:T(8,128)(2,1)S(1)}, bf16[4,320,768]{2,1,0:T(8,128)(2,1)}, u32[]{:S(2)}) copy-start(bf16[4,320,768]{2,1,0:T(8,128)(2,1)} %copy-done.7) | copy-start | bytes 5898244
  67.5 7.1 %copy-start.19 = (f32[128,128]{1,0:T(8,128)}, f32[128,128]{1,0:T(8,128)S(1)}, u32[]{:S(2)}) copy-start(f32[128,128]{1,0:T(8,128)S(1)} %get-tuple-element.63.cosine.refs_15_) | copy-start | bytes 196612
  67.5 7.1 %copy-start.20 = (f32[128,128]{1,0:T(8,128)}, f32[128,128]{1,0:T(8,128)S(1)}, u32[]{:S(2)}) copy-start(f32[128,128]{1,0:T(8,128)S(1)} %get-tuple-element.64.sine.refs_16_) | copy-start | bytes 196612
  68.1 6.5 %copy-start.5 = (bf16[128,1664]{1,0:T(8,128)(2,1)}, bf16[128,1664]{1,0:T(8,128)(2,1)S(1)}, u32[]{:S(2)}) copy-start(bf16[128,1664]{1,0:T(8,128)(2,1)S(1)} %get-tuple-element.25.own.refs_10_) | copy-start | bytes 1277956
  68.1 6.5 %copy-start.16 = (bf16[128,768]{1,0:T(8,128)(2,1)}, bf16[128,768]{1,0:T(8,128)(2,1)S(1)}, u32[]{:S(2)}) copy-start(bf16[128,768]{1,0:T(8,128)(2,1)S(1)} %get-tuple-element.24.q.refs_8_) | copy-start | bytes 589828
  68.1 9.1 %collective-permute-start = (bf16[64,1664]{1,0:T(8,128)(2,1)S(1)}, bf16[64,1664]{1,0:T(8,128)(2,1)S(1)}, u32[]{:S(2)}, u32[]{:S(2)}) collective-permute-start(bf16[64,1664]{1,0:T(8,128)(2,1)S(1)} %get-tuple-element.47), channel_id=1, source_target_pairs={{0,4},{4,8},{8,12},{12,16},{16,20},{20,24},{24,28},{1,5},{5,9},{9,... | collective-permute-start | bytes 638984 | tf_op jit(solution)/shard_map/ppermute | solution.py:618
  71.2 3.4 %copy-start.42 = (f32[128,1]{0,1:T(1,128)S(1)}, f32[128,1]{0,1:T(1,128)}, u32[]{:S(2)}) copy-start(f32[128,1]{0,1:T(1,128)} %get-tuple-element.56) | copy-start | bytes 1540
  71.2 4.3 %copy-start.26 = (bf16[1,128,768]{2,1,0:T(8,128)(2,1)S(1)}, bf16[1,128,768]{2,1,0:T(8,128)(2,1)}, u32[]{:S(2)}) copy-start(bf16[1,128,768]{2,1,0:T(8,128)(2,1)} %param.9) | copy-start | bytes 589828
  71.2 4.2 %copy-start.40 = (f32[128]{0:T(128)S(1)}, f32[128]{0:T(128)}, u32[]{:S(2)}) copy-start(f32[128]{0:T(128)} %copy-done.39) | copy-start | bytes 1540
  71.2 7.3 %collective-permute-start.1 = (bf16[64,1664]{1,0:T(8,128)(2,1)S(1)}, bf16[64,1664]{1,0:T(8,128)(2,1)S(1)}, u32[]{:S(2)}, u32[]{:S(2)}) collective-permute-start(bf16[64,1664]{1,0:T(8,128)(2,1)S(1)} %get-tuple-element.46), channel_id=1, source_target_pairs={{4,0},{8,4},{12,8},{16,12},{20,16},{24,20},{28,24},{5,1},{9,5},{13... | collective-permute-start | bytes 638984 | tf_op jit(solution)/shard_map/ppermute | solution.py:619
  77.2 0.7 copy-start.11
  78.5 0.7 copy-start.13
  79.2 1.0 copy-start.6
  80.2 0.9 copy-start.12
  81.1 0.9 copy-start.14
  82.1 0.9 copy-start.17
  83.0 0.8 copy-start.18
  83.8 7.4 %copy-start.2 = (bf16[4,192,2304]{2,1,0:T(8,128)(2,1)S(1)}, bf16[4,192,2304]{2,1,0:T(8,128)(2,1)}, u32[]{:S(2)}) copy-start(bf16[4,192,2304]{2,1,0:T(8,128)(2,1)} %copy-done.1) | copy-start | bytes 10616836
  86.2 0.7 copy-start.15
  86.9 0.6 copy-start.23
  91.0 5.8 %copy-start.24 = (f32[128,768]{1,0:T(8,128)}, f32[128,768]{1,0:T(8,128)S(1)}, u32[]{:S(2)}) copy-start(f32[128,768]{1,0:T(8,128)S(1)} %get-tuple-element.60) | copy-start | bytes 1179652
  91.3 1.5 copy-start.28
  91.3 1.5 copy-start.35
  95.4 1.4 copy-start.30
  96.8 1.3 copy-start.4
  96.8 3.4 %copy-start.29 = (bf16[4,288,768]{2,1,0:T(8,128)(2,1)S(1)}, bf16[4,288,768]{2,1,0:T(8,128)(2,1)}, u32[]{:S(2)}) copy-start(bf16[4,288,768]{2,1,0:T(8,128)(2,1)} %slice.33) | copy-start | bytes 5308420
  96.8 3.4 %copy-start.31 = (bf16[128,1152]{1,0:T(8,128)(2,1)S(1)}, bf16[128,1152]{1,0:T(8,128)(2,1)}, u32[]{:S(2)}) copy-start(bf16[128,1152]{1,0:T(8,128)(2,1)} %get-tuple-element.45) | copy-start | bytes 884740
  97.1 3.1 %copy-start.25 = (f32[128,768]{1,0:T(8,128)S(1)}, f32[128,768]{1,0:T(8,128)}, u32[]{:S(2)}) copy-start(f32[128,768]{1,0:T(8,128)} %copy-done.24) | copy-start | bytes 1179652
  98.1 3.3 %copy-start.34 = (bf16[128,768]{1,0:T(8,128)(2,1)}, bf16[128,768]{1,0:T(8,128)(2,1)S(1)}, u32[]{:S(2)}) copy-start(bf16[128,768]{1,0:T(8,128)(2,1)S(1)} %fusion.21.refs_4_) | copy-start | bytes 589828
  103.1 79.5 %copy-start.27 = (bf16[1,128,768]{2,1,0:T(8,128)(2,1)S(1)}, bf16[1,128,768]{2,1,0:T(8,128)(2,1)}, u32[]{:S(2)}) copy-start(bf16[1,128,768]{2,1,0:T(8,128)(2,1)} %param.9) | copy-start | bytes 589828
  103.1 80.8 %copy-start.44 = (f32[128]{0:T(128)S(1)}, f32[128]{0:T(128)}, u32[]{:S(2)}) copy-start(f32[128]{0:T(128)} %copy-done.43) | copy-start | bytes 1540
  103.1 80.8 %copy-start.41 = (f32[128]{0:T(128)S(1)}, f32[128]{0:T(128)}, u32[]{:S(2)}) copy-start(f32[128]{0:T(128)} %copy-done.39) | copy-start | bytes 1540
  103.1 82.1 %copy-start.36 = (bf16[1,128,768]{2,1,0:T(8,128)(2,1)S(1)}, bf16[1,128,768]{2,1,0:T(8,128)(2,1)}, u32[]{:S(2)}) copy-start(bf16[1,128,768]{2,1,0:T(8,128)(2,1)} %param.11) | copy-start | bytes 589828
  182.5 6.0 %copy-start.33 = (f32[192,2304]{1,0:T(8,128)S(1)}, f32[192,2304]{1,0:T(8,128)}, u32[]{:S(2)}) copy-start(f32[192,2304]{1,0:T(8,128)} %get-tuple-element.75) | copy-start | bytes 5308420
  188.5 1.4 copy-start.38
  188.5 2.3 %copy-start.32 = (f32[192,2304]{1,0:T(8,128)S(1)}, f32[192,2304]{1,0:T(8,128)}, u32[]{:S(2)}) copy-start(f32[192,2304]{1,0:T(8,128)} %get-tuple-element.77) | copy-start | bytes 5308420
  190.9 1.8 copy-start.37
